TPU v7x, 512 devices: a whole 4x8x8 slice. The times are simulated.
512 devices in a mesh: row: 32 (over x, y), col: 16 (over z, core).
Axes of the slice: x: 4, y: 8, z: 8, core: 2. Of those that a mesh axis runs over, the one named last changes fastest.
Arguments:
- eigvecs: float32 [131072, 2048], P('row', 'col'), may hold values from -6 to 6
- householder: float32 [2, 131072, 256], P(None, 'row', 'col'), may hold values from -4 to 4, as said below
Outputs:
- backvecs: float32 [131072, 2048], P('row', 'col')
Inputs may be any that keep to these rules, and one draw needn't show every extreme that they name: Every entry of householder has magnitude at least 0.5.
All inputs are finite; a program needn't handle non-finite values.
Results may differ from a plain program's by a relative error of at most 0.0001.
Values sent between devices are 32-bit elements; how exact they have to be, the bound alone decides.
No kernel may reach another device: no remote copies, remote signals or barrier semaphores. Data moves between devices by JAX's collectives and lax.ppermute only.
A program may use at most 64 MiB of HBM per device.

v0:
```python
import jax
import jax.numpy as jnp
from jax import lax
from jax.sharding import PartitionSpec as P

BLOCKS = 2


def hidot(left, right):
    return jnp.dot(left, right, precision=lax.Precision.HIGHEST, preferred_element_type=jnp.float32)


def upper_apply(diag_block, rhs):
    width = diag_block.shape[0]
    scale = 2.0 / jnp.diag(diag_block)
    nilpot = jnp.triu(diag_block, 1) * scale[:, None]
    identity = jnp.eye(width, dtype=jnp.float32)
    inverse = identity - nilpot
    power = nilpot
    for level in range(1, (width - 1).bit_length()):
        power = hidot(power, power)
        inverse = hidot(inverse, identity + power)
    return hidot(inverse, scale[:, None] * rhs)


def solve_group(gram, project, count):
    coefs = [None] * count
    coefs[0] = upper_apply(gram, project)
    return coefs[0]


def apply_group(current, local_panels):
    count = local_panels.shape[0]
    gathered = lax.all_gather(local_panels, "col", axis=2, tiled=True)
    panels = gathered[0]
    gram = hidot(panels.T, panels)
    project = hidot(panels.T, current)
    gram, project = lax.psum((gram, project), "row")
    coef = solve_group(gram, project, count)
    return current - hidot(panels, coef)


def shards(eigvecs, householder):
    current = eigvecs
    for block in range(BLOCKS - 1, -1, -1):
        current = apply_group(current, householder[block : block + 1])
    return current


def solution(mesh):
    in_specs = (P("row", "col"), P(None, "row", "col"))
    out_specs = P("row", "col")
    return jax.shard_map(shards, mesh=mesh, in_specs=in_specs, out_specs=out_specs, check_vma=False)
```

profile of v0, /device:TPU:1, one launch (start us, length us, event | category | flops | bytes accessed | tf_op | source)
XLA Modules:
  0.0 455.8 jit_solution(9816943755910376330)
XLA Ops:
  6.5 0.0 all-gather.3.cloned.1.call-start
  6.5 1.9 fusion.47
  8.4 0.0 all-gather.3.cloned.1.call-update
  8.5 0.0 all-gather.5.cloned.1.call-start
  8.5 0.7 all-gather.5.cloned.1.call-update
  9.2 0.0 copy-start.4
  9.2 0.0 all-reduce.7.cloned.1.call-start
  9.3 3.0 copy.5
  12.3 48.8 %all-gather.3.cloned.1.call-done = f32[1,4096,256]{1,2,0:T(8,128)} async-done(((f32[1,4096,16]{1,2,0:T(8,128)}), f32[1,4096,256]{1,2,0:T(8,128)}) %all-gather.3.cloned.1.call-update) | async-done | bytes 4194320 | tf_op jit(solution)/shard_map/all_gather | solution.py:34
  61.1 7.8 %fusion.10 = f32[256,256]{1,0:T(8,128)} fusion(f32[1,4096,256]{1,2,0:T(8,128)} %all-gather.3.cloned.1.call-done), kind=kOutput, calls=%fused_computation.14 | convolution fusion | flops 3221225472 | bytes 4456448 | tf_op jit(solution)/shard_map/dot_general | solution.py:10
  68.9 0.0 copy-done.4
  68.9 0.0 copy-done.2
  69.0 4.1 fusion.8
  73.1 0.0 all-reduce.7.cloned.1.call-update
  73.1 0.2 all-reduce.5.cloned.1.call-start
  73.3 33.7 %all-gather.5.cloned.1.call-done = f32[1,4096,256]{1,2,0:T(8,128)} async-done(((f32[1,4096,16]{1,2,0:T(8,128)}), f32[1,4096,256]{1,2,0:T(8,128)}) %all-gather.5.cloned.1.call-update) | async-done | bytes 4194320 | tf_op jit(solution)/shard_map/all_gather | solution.py:34
  107.0 7.7 %fusion.5 = f32[256,256]{1,0:T(8,128)} fusion(f32[1,4096,256]{1,2,0:T(8,128)} %all-gather.5.cloned.1.call-done), kind=kOutput, calls=%fused_computation.9 | convolution fusion | flops 3221225472 | bytes 4456448 | tf_op jit(solution)/shard_map/dot_general | solution.py:10
  114.7 145.4 %all-reduce.7.cloned.1.call-done = (f32[256,256]{1,0:T(8,128)}, f32[256,128]{1,0:T(8,128)}) async-done(((f32[256,256]{1,0:T(8,128)}, f32[256,128]{1,0:T(8,128)}), (f32[256,256]{1,0:T(8,128)}, f32[256,128]{1,0:T(8,128)})) %all-reduce.7.cloned.1.call-update) | async-done | bytes 393232 | tf_op jit(solution)/shard_map/psum | solution.py:38
  260.1 2.6 gather_fusion
  262.7 1.5 fusion.27
  264.2 1.4 fusion.15
  265.6 0.4 fusion.48
  266.0 0.0 copy-start.6
  266.0 0.4 fusion.49
  266.4 0.0 copy-start.3
  266.4 0.0 copy-start.5
  266.4 0.4 fusion.16
  266.8 0.4 fusion.50
  267.2 0.4 fusion.17
  267.6 0.4 fusion.51
  268.0 0.4 fusion.18
  268.4 0.4 fusion.52
  268.8 0.4 fusion.19
  269.2 0.4 convert_add_fusion.7
  269.6 0.4 fusion.20
  270.0 0.4 fusion.53
  270.4 0.0 copy-done.6
  270.4 0.5 fusion.33
  270.8 0.0 copy-done.3
  270.9 2.6 fusion.1
  273.5 0.0 copy-done
  273.5 4.1 fusion.12
  277.5 0.0 all-reduce.5.cloned.1.call-update
  277.6 154.4 %all-reduce.5.cloned.1.call-done = (f32[256,256]{1,0:T(8,128)}, f32[256,128]{1,0:T(8,128)}) async-done(((f32[256,256]{1,0:T(8,128)}, f32[256,128]{1,0:T(8,128)}), (f32[256,256]{1,0:T(8,128)}, f32[256,128]{1,0:T(8,128)})) %all-reduce.5.cloned.1.call-update) | async-done | bytes 393232 | tf_op jit(solution)/shard_map/psum | solution.py:38
  431.9 2.6 gather_fusion.1
  434.5 1.5 fusion.28
  436.0 1.4 fusion.21
  437.4 0.4 fusion.54
  437.8 0.0 copy-start.7
  437.8 0.4 fusion.55
  438.2 0.0 copy-start.1
  438.2 0.4 fusion.22
  438.6 0.4 fusion.56
  439.0 0.4 fusion.23
  439.4 0.4 fusion.57
  439.8 0.4 fusion.24
  440.2 0.4 fusion.58
  440.6 0.4 fusion.25
  441.0 0.4 convert_add_fusion
  441.4 0.4 fusion.26
  441.8 0.4 fusion.59
  442.2 0.5 fusion.29
  442.6 3.7 fusion
  446.4 2.9 copy.6
  (8 shorter events, 0.0 us)
Async XLA Ops:
  6.5 54.6 %all-gather.3.cloned.1.call-start = ((), (), s32[]{:S(2)}) async-start(), calls=%async_computation | async-start | bytes 4456448 | tf_op jit(solution)/shard_map/all_gather | solution.py:34
  8.5 98.5 %all-gather.5.cloned.1.call-start = ((), (), s32[]{:S(2)}) async-start(), calls=%async_computation.1 | async-start | bytes 4456448 | tf_op jit(solution)/shard_map/all_gather | solution.py:34
  9.2 59.7 %copy-start.4 = (f32[4096,128]{1,0:T(8,128)S(1)}, f32[4096,128]{1,0:T(8,128)}, u32[]{:S(2)}) copy-start(f32[4096,128]{1,0:T(8,128)} %param.2) | copy-start | bytes 6291460
  9.2 250.9 %all-reduce.7.cloned.1.call-start = ((), (), s32[]{:S(2)}) async-start(), calls=%async_computation.3 | async-start | bytes 786432 | tf_op jit(solution)/shard_map/psum | solution.py:38
  61.1 7.9 %copy-start.2 = (f32[1,4096,256]{1,2,0:T(8,128)S(1)}, f32[1,4096,256]{1,2,0:T(8,128)}, u32[]{:S(2)}) copy-start(f32[1,4096,256]{1,2,0:T(8,128)} %all-gather.3.cloned.1.call-done) | copy-start | bytes 12582916
  73.1 358.8 %all-reduce.5.cloned.1.call-start = ((), (), s32[]{:S(2)}) async-start(), calls=%async_computation.2 | async-start | bytes 786432 | tf_op jit(solution)/shard_map/psum | solution.py:38
  266.0 4.4 copy-start.6
  266.4 4.5 copy-start.3
  266.4 4.5 copy-start.5
  270.9 2.6 copy-start
  437.8 4.4 copy-start.7
  438.2 4.4 copy-start.1
Sparse Core Ops, SparseCore 0:
  9.5 51.5 all-gather.2
  63.2 43.7 all-gather.4
  110.4 149.6 all-reduce.6
  277.7 154.1 all-reduce.4
where the time goes:
time: 459 us; the launch traced here: 456 us
  waiting for transfers between devices  383 us (83%)
  matrix products  46 us (10%)
  between operations  13.5 us (3%)
  local copies, waits for them, and re-layouts  13 us (3%)
    psum x2, waiting for transfers between devices, apply_group(): gram, project = lax.psum((gram, project), 'row')  300 us
    all_gather x2, waiting for transfers between devices, apply_group(): gathered = lax.all_gather(local_panels, 'col', axis=2, tiled=True)  82.5 us
    dot_general x36, matrix products, hidot(): jnp.dot(left, right, precision=lax.Precision.HIGHEST, preferred_element_t...  46 us
  transfers between devices with their start and end apart: 4, of which 4 were waited for; matrix products, arithmetic and copies ran while one was open for 5% of the time, Pallas kernels for 0%

commit v1 on v0

v1 whole, which is shorter than its diff:
```python
import jax
import jax.numpy as jnp
from jax import lax
from jax.experimental import pallas as pl
from jax.experimental.pallas import tpu as pltpu
from jax.sharding import PartitionSpec as P

F32 = jnp.float32
BF16 = jnp.bfloat16
CHIPS = 8
ROWS = 4096
COLS = 128
NV = 512
STEP = 512
VMEM = 56 * 1024 * 1024
ARRIVAL = (0, 1, -1, -2, 2, 3, -3, -4)
GRAM_BLOCKS = (
    ((0, 0), (0, 1), (0, 2), (0, 3), (1, 1)),
    ((1, 2), (1, 3), (2, 2), (2, 3), (3, 3)),
)


def split(value):
    high = value.astype(BF16)
    low = (value - high.astype(F32)).astype(BF16)
    return high, low


def nt(left, right):
    return lax.dot_general(left, right, (((1,), (1,)), ((), ())), preferred_element_type=F32)


def nn(left, right):
    return lax.dot_general(left, right, (((1,), (0,)), ((), ())), preferred_element_type=F32)


def hidot(left, right):
    return jnp.dot(left, right, precision=lax.Precision.HIGHEST, preferred_element_type=F32)


def products_kernel(place, *refs):
    pieces = refs[:8]
    c_ref, vhi, vlo, out, proj, gram = refs[8:]
    step = pl.program_id(0)

    @pl.when(step == 0)
    def _():
        proj[...] = jnp.zeros_like(proj)
        gram[...] = jnp.zeros_like(gram)

    for piece in range(8):
        for half in range(2):
            for block in range(2):
                first = half * 32 + block * 16
                high, low = split(pieces[piece][first : first + 16, :])
                at = pl.ds(pl.multiple_of(place[piece * 2 + half] + block * 256, 16), 16)
                vhi[at, :] = high
                vlo[at, :] = low
    chi, clo = split(c_ref[...])
    both = nn(vhi[...], jnp.concatenate([chi, clo], axis=1))
    proj[...] += both[:, :COLS] + both[:, COLS:] + nn(vlo[...], chi)
    for index in range(5):
        left = pl.ds(pl.multiple_of(place[16 + 2 * index], 128), 128)
        right = pl.ds(pl.multiple_of(place[17 + 2 * index], 128), 128)
        lhi, llo = vhi[left, :], vlo[left, :]
        rhi, rlo = vhi[right, :], vlo[right, :]
        gram[index * 128 : index * 128 + 128, :] += nt(lhi, rhi) + nt(lhi, rlo) + nt(llo, rhi)

    @pl.when(step == pl.num_programs(0) - 1)
    def _():
        out[:, :16, :] = proj[...].reshape(32, 16, COLS)
        out[:, 16:, :] = gram[...].reshape(32, 24, COLS)


def products(place, pieces, current):
    steps = ROWS // STEP
    return pl.pallas_call(
        products_kernel,
        grid=(steps,),
        in_specs=[pl.BlockSpec(memory_space=pltpu.SMEM)]
        + [pl.BlockSpec((64, STEP), lambda k: (0, k))] * 8
        + [pl.BlockSpec((STEP, COLS), lambda k: (k, 0))],
        out_specs=[
            pl.BlockSpec((NV, STEP), lambda k: (0, k)),
            pl.BlockSpec((NV, STEP), lambda k: (0, k)),
            pl.BlockSpec((32, 40, COLS), lambda k: (0, 0, 0)),
        ],
        out_shape=[
            jax.ShapeDtypeStruct((NV, ROWS), BF16),
            jax.ShapeDtypeStruct((NV, ROWS), BF16),
            jax.ShapeDtypeStruct((32, 40, COLS), F32),
        ],
        scratch_shapes=[pltpu.VMEM((NV, COLS), F32), pltpu.VMEM((768, 128), F32)],
        compiler_params=pltpu.CompilerParams(vmem_limit_bytes=VMEM),
        name="products",
    )(place, *pieces, current)


def invert_unit(nilpot):
    row = lax.broadcasted_iota(jnp.int32, (128, 128), 0)
    col = lax.broadcasted_iota(jnp.int32, (128, 128), 1)
    eye = (row == col).astype(F32)
    near = [jnp.where(row // 4 == col // 4, n, 0.0) for n in nilpot]
    square = [hidot(n, n) for n in near]
    inverse = [hidot(eye - n, eye + s) for n, s in zip(near, square)]
    size = 4
    while size < 128:
        pair = (row // (2 * size) == col // (2 * size)) & (row // size != col // size)
        right = [hidot(jnp.where(pair, n, 0.0), r) for n, r in zip(nilpot, inverse)]
        inverse = [r - hidot(r, t) for r, t in zip(inverse, right)]
        size *= 2
    return inverse


def solve_kernel(core, mine, other, xhi, xlo):
    zero = core[0] == 0
    gram = {}
    for which in range(2):
        flat = jnp.where(zero == (which == 0), mine[:, 16:, :], other[...]).reshape(768, 128)
        for index, at in enumerate(GRAM_BLOCKS[which]):
            gram[at] = flat[index * 128 : index * 128 + 128]
    project = mine[:, :16, :].reshape(NV, COLS)
    row = lax.broadcasted_iota(jnp.int32, (128, 128), 0)
    col = lax.broadcasted_iota(jnp.int32, (128, 128), 1)
    scale = [2.0 / jnp.sum(jnp.where(row == col, gram[i, i], 0.0), axis=1, keepdims=True) for i in range(4)]
    inverse = invert_unit([jnp.where(row < col, gram[i, i] * scale[i], 0.0) for i in range(4)])
    coef = [None] * 4
    for i in range(3, -1, -1):
        rhs = project[i * 128 : i * 128 + 128]
        if i < 3:
            panel = jnp.concatenate([gram[i, j] for j in range(i + 1, 4)], axis=1)
            rhs = rhs - hidot(panel, jnp.concatenate(coef[i + 1 :], axis=0))
        coef[i] = hidot(inverse[i], rhs * scale[i])
    high, low = split(jnp.concatenate(coef, axis=0).T)
    xhi[...] = high
    xlo[...] = low


def solve(core, mine, other):
    return pl.pallas_call(
        solve_kernel,
        in_specs=[pl.BlockSpec(memory_space=pltpu.SMEM)] + [pl.BlockSpec(memory_space=pltpu.VMEM)] * 2,
        out_specs=[pl.BlockSpec(memory_space=pltpu.VMEM)] * 2,
        out_shape=[jax.ShapeDtypeStruct((COLS, NV), BF16)] * 2,
        compiler_params=pltpu.CompilerParams(vmem_limit_bytes=VMEM),
        name="solve",
    )(core, mine, other)


def update_kernel(c_ref, vhi, vlo, xhi, xlo, out):
    both = nn(jnp.concatenate([xhi[...], xlo[...]], axis=0), vhi[...])
    change = both[:COLS] + both[COLS:] + nn(xhi[...], vlo[...])
    out[...] = c_ref[...] - change.T


def update(current, vhi, vlo, xhi, xlo):
    steps = ROWS // STEP
    return pl.pallas_call(
        update_kernel,
        grid=(steps,),
        in_specs=[
            pl.BlockSpec((STEP, COLS), lambda k: (k, 0)),
            pl.BlockSpec((NV, STEP), lambda k: (0, k)),
            pl.BlockSpec((NV, STEP), lambda k: (0, k)),
            pl.BlockSpec((COLS, NV), lambda k: (0, 0)),
            pl.BlockSpec((COLS, NV), lambda k: (0, 0)),
        ],
        out_specs=pl.BlockSpec((STEP, COLS), lambda k: (k, 0)),
        out_shape=jax.ShapeDtypeStruct((ROWS, COLS), F32),
        compiler_params=pltpu.CompilerParams(vmem_limit_bytes=VMEM),
        name="update",
    )(current, vhi, vlo, xhi, xlo)


def turn(chip, core):
    return 1 if (chip + core) % 2 == 0 else -1


def exchange(value, side):
    perm = []
    for chip in range(CHIPS):
        for core in range(2):
            target = (chip + side * turn(chip, core)) % CHIPS
            perm.append((chip * 2 + core, target * 2 + core))
    return lax.ppermute(value, "col", perm)


def swap_cores(value):
    return lax.ppermute(value, "col", [(i, i ^ 1) for i in range(2 * CHIPS)])


def shards(eigvecs, householder):
    me = lax.axis_index("col")
    chip, core = me // 2, me % 2
    sign = 1 - 2 * ((chip + core) % 2)
    steps = jnp.array(ARRIVAL, jnp.int32)
    here = ((chip + sign * steps + 8) % CHIPS) * 32 + core * 16
    there = ((chip - sign * steps + 8) % CHIPS) * 32 + (1 - core) * 16
    blocks = jnp.where(core == 0, jnp.array(GRAM_BLOCKS[0], jnp.int32), jnp.array(GRAM_BLOCKS[1], jnp.int32))
    place = jnp.concatenate([here, there, blocks.reshape(-1) * 128])

    own = householder.transpose(0, 2, 1).reshape(32, ROWS)
    first = exchange(own, 1)
    pieces = [jnp.concatenate([own, first], axis=0)]
    for side in (-1, 1, -1):
        pieces.append(exchange(pieces[-1], side))
    pieces += [swap_cores(piece) for piece in pieces]

    vhi, vlo, partial = products(place, pieces, eigvecs)
    summed = lax.all_to_all(partial, "row", 0, 0, tiled=True).sum(axis=0)
    mine = lax.all_to_all(jnp.broadcast_to(summed[None], (32, 40, COLS)), "row", 0, 0, tiled=True)
    other = swap_cores(mine[:, 16:, :])
    xhi, xlo = solve(core.reshape(1), mine, other)
    return update(eigvecs, vhi, vlo, xhi, xlo)


def solution(mesh):
    in_specs = (P("row", "col"), P(None, "row", "col"))
    out_specs = P("row", "col")
    return jax.shard_map(shards, mesh=mesh, in_specs=in_specs, out_specs=out_specs, check_vma=False)
```

time: 459 us -> 167 us (0.36)
  waiting for transfers between devices: 383 us -> 36.8 us
  blocking collectives: 0 us -> 51.1 us
  matrix products: 46 us -> 0 us
  starting transfers between devices: 0.3 us -> 44.8 us
  Pallas kernels: 0 us -> 29.4 us
  between operations: 13.5 us -> 0.16 us
  local copies, waits for them, and re-layouts: 13 us -> 0.93 us
    psum x2 -> x0, waiting for transfers between devices: 300 us -> none  [apply_group(): gram, project = lax.psum((gram, project), 'row')]
    all_gather x2 -> x0, waiting for transfers between devices: 82.5 us -> none  [apply_group(): gathered = lax.all_gather(local_panels, 'col', axis=2, tiled=True)]
    all_to_all x0 -> x2, blocking collectives: none -> 51.1 us  [the longest x1 26.5 us: shards(): summed = lax.all_to_all(partial, 'row', 0, 0, tiled=True).sum(axis=0)]
    dot_general x36 -> x0, matrix products: 46 us -> none  [hidot(): jnp.dot(left, right, precision=lax.Precision.HIGHEST, preferred_element_t...]
    ppermute x0 -> x9, starting transfers between devices: none -> 44.8 us  [the longest x5 24.9 us: swap_cores(): return lax.ppermute(value, 'col', [(i, i ^ 1) for i in range(2 * CHIPS)])]
    ppermute x0 -> x9, waiting for transfers between devices: none -> 36.8 us  [the longest x4 35.1 us: exchange(): return lax.ppermute(value, 'col', perm)]
    pallas_call x0 -> x3, Pallas kernels: none -> 29.4 us  [the longest x1 13.5 us: products(): pl.pallas_call(products_kernel, grid=(steps,), in_specs=[pl.BlockSpec(mem...]
    gather x2 -> x0, local copies, waits for them, and re-layouts: 5.13 us -> none  [upper_apply(): scale = 2.0 / jnp.diag(diag_block)]
  transfers between devices with their start and end apart: 4 -> 9, of which waited for: 4 -> 6; matrix products, arithmetic and copies ran while one was open for 5% -> 1% of each run, Pallas kernels for 0% -> 0%
where the time goes in v1:
time: 167 us; the launch traced here: 166 us
  blocking collectives  51.1 us (31%)
  starting transfers between devices  44.8 us (27%)
  waiting for transfers between devices  36.8 us (22%)
  Pallas kernels  29.4 us (18%)
  other arithmetic  3.2 us (2%)
    ppermute x4, waiting for transfers between devices, exchange(): return lax.ppermute(value, 'col', perm)  35.1 us
    all_to_all x1, blocking collectives, shards(): summed = lax.all_to_all(partial, 'row', 0, 0, tiled=True).sum(axis=0)  26.5 us
    ppermute x5, starting transfers between devices, swap_cores(): return lax.ppermute(value, 'col', [(i, i ^ 1) for i in range(2 * CHIPS)])  24.9 us
    all_to_all x1, blocking collectives, shards(): lax.all_to_all(jnp.broadcast_to(summed[None], (32, 40, COLS)), 'row', 0,...  24.5 us
    ppermute x4, starting transfers between devices, exchange(): return lax.ppermute(value, 'col', perm)  19.9 us
    pallas_call x1, Pallas kernels, products(): pl.pallas_call(products_kernel, grid=(steps,), in_specs=[pl.BlockSpec(mem...  13.5 us
    pallas_call x1, Pallas kernels, update(): pl.pallas_call(update_kernel, grid=(steps,), in_specs=[pl.BlockSpec((STEP...  9.16 us
    pallas_call x1, Pallas kernels, solve(): pl.pallas_call(solve_kernel, in_specs=[pl.BlockSpec(memory_space=pltpu.SM...  6.73 us
  transfers between devices with their start and end apart: 9, of which 6 were waited for; matrix products, arithmetic and copies ran while one was open for 1% of the time, Pallas kernels for 0%

profile of v1, /device:TPU:1, one launch (start us, length us, event | category | flops | bytes accessed | tf_op | source)
XLA Modules:
  0.0 166.4 jit_solution(734929395593119442)
XLA Ops:
  0.0 11.5 %collective-permute-start = (f32[32,4096]{1,0:T(8,128)}, f32[32,4096]{1,0:T(8,128)S(1)}, u32[]{:S(2)}, u32[]{:S(2)}) collective-permute-start(f32[32,4096]{1,0:T(8,128)} %bitcast.4), channel_id=1, source_target_pairs={{0,2},{1,15},{2,0},{3,5},{4,6},{5,3},{6,4},{7,9},{8,10},{9,7},{10,... | collective-permute-start | bytes 1572872 | tf_op jit(solution)/shard_map/ppermute | solution.py:185
  11.5 6.8 %collective-permute-done = f32[32,4096]{1,0:T(8,128)S(1)} collective-permute-done((f32[32,4096]{1,0:T(8,128)}, f32[32,4096]{1,0:T(8,128)S(1)}, u32[]{:S(2)}, u32[]{:S(2)}) %collective-permute-start) | collective-permute-done | bytes 524320 | tf_op jit(solution)/shard_map/ppermute | solution.py:185
  18.3 1.1 pad_maximum_fusion.refs_0_
  19.4 0.0 copy-start.1
  19.4 1.9 %collective-permute-start.1 = (f32[64,4096]{1,0:T(8,128)S(1)}, f32[64,4096]{1,0:T(8,128)S(1)}, u32[]{:S(2)}, u32[]{:S(2)}) collective-permute-start(f32[64,4096]{1,0:T(8,128)S(1)} %pad_maximum_fusion.refs_0_), channel_id=1, source_target_pairs={{0,14},{1,3},{2,4},{3,1},{4,2},{5,7},{6,8},{7,5},{8,6},{9,11},{10,... | collective-permute-start | bytes 3145736 | tf_op jit(solution)/shard_map/ppermute | solution.py:185
  21.3 13.9 %collective-permute-done.1.refs_1_ = f32[64,4096]{1,0:T(8,128)S(1)} collective-permute-done((f32[64,4096]{1,0:T(8,128)S(1)}, f32[64,4096]{1,0:T(8,128)S(1)}, u32[]{:S(2)}, u32[]{:S(2)}) %collective-permute-start.1) | collective-permute-done | bytes 1048608 | tf_op jit(solution)/shard_map/ppermute | solution.py:185
  35.2 0.0 copy-start.2
  35.2 4.6 %collective-permute-start.2 = (f32[64,4096]{1,0:T(8,128)S(1)}, f32[64,4096]{1,0:T(8,128)S(1)}, u32[]{:S(2)}, u32[]{:S(2)}) collective-permute-start(f32[64,4096]{1,0:T(8,128)S(1)} %collective-permute-done.1.refs_1_), channel_id=1, source_target_pairs={{0,2},{1,15},{2,0},{3,5},{4,6},{5,3},{6,4},{7,9},{8,10},{9,7},{10,... | collective-permute-start | bytes 3145736 | tf_op jit(solution)/shard_map/ppermute | solution.py:185
  39.8 12.2 %collective-permute-done.2.refs_2_ = f32[64,4096]{1,0:T(8,128)S(1)} collective-permute-done((f32[64,4096]{1,0:T(8,128)S(1)}, f32[64,4096]{1,0:T(8,128)S(1)}, u32[]{:S(2)}, u32[]{:S(2)}) %collective-permute-start.2) | collective-permute-done | bytes 1048608 | tf_op jit(solution)/shard_map/ppermute | solution.py:185
  52.0 0.0 copy-start.3
  52.0 1.9 %collective-permute-start.3 = (f32[64,4096]{1,0:T(8,128)S(1)}, f32[64,4096]{1,0:T(8,128)}, u32[]{:S(2)}, u32[]{:S(2)}) collective-permute-start(f32[64,4096]{1,0:T(8,128)S(1)} %collective-permute-done.2.refs_2_), channel_id=1, source_target_pairs={{0,14},{1,3},{2,4},{3,1},{4,2},{5,7},{6,8},{7,5},{8,6},{9,11},{10,... | collective-permute-start | bytes 3145736 | tf_op jit(solution)/shard_map/ppermute | solution.py:185
  53.9 7.5 %collective-permute-start.4 = (f32[64,4096]{1,0:T(8,128)S(1)}, f32[64,4096]{1,0:T(8,128)}, u32[]{:S(2)}, u32[]{:S(2)}) collective-permute-start(f32[64,4096]{1,0:T(8,128)S(1)} %pad_maximum_fusion.refs_0_), channel_id=1, source_target_pairs={{0,1},{1,0},{2,3},{3,2},{4,5},{5,4},{6,7},{7,6},{8,9},{9,8},{10,11... | collective-permute-start | bytes 3145736 | tf_op jit(solution)/shard_map/ppermute | solution.py:189
  61.4 1.9 %collective-permute-start.5 = (f32[64,4096]{1,0:T(8,128)S(1)}, f32[64,4096]{1,0:T(8,128)}, u32[]{:S(2)}, u32[]{:S(2)}) collective-permute-start(f32[64,4096]{1,0:T(8,128)S(1)} %collective-permute-done.1.refs_1_), channel_id=1, source_target_pairs={{0,1},{1,0},{2,3},{3,2},{4,5},{5,4},{6,7},{7,6},{8,9},{9,8},{10,11... | collective-permute-start | bytes 3145736 | tf_op jit(solution)/shard_map/ppermute | solution.py:189
  63.3 2.4 %collective-permute-start.6 = (f32[64,4096]{1,0:T(8,128)S(1)}, f32[64,4096]{1,0:T(8,128)}, u32[]{:S(2)}, u32[]{:S(2)}) collective-permute-start(f32[64,4096]{1,0:T(8,128)S(1)} %collective-permute-done.2.refs_2_), channel_id=1, source_target_pairs={{0,1},{1,0},{2,3},{3,2},{4,5},{5,4},{6,7},{7,6},{8,9},{9,8},{10,11... | collective-permute-start | bytes 3145736 | tf_op jit(solution)/shard_map/ppermute | solution.py:189
  65.7 2.2 %collective-permute-done.3.refs_3_ = f32[64,4096]{1,0:T(8,128)} collective-permute-done((f32[64,4096]{1,0:T(8,128)S(1)}, f32[64,4096]{1,0:T(8,128)}, u32[]{:S(2)}, u32[]{:S(2)}) %collective-permute-start.3) | collective-permute-done | bytes 1048608 | tf_op jit(solution)/shard_map/ppermute | solution.py:185
  67.9 6.3 %collective-permute-start.7 = (f32[64,4096]{1,0:T(8,128)}, f32[64,4096]{1,0:T(8,128)}, u32[]{:S(2)}, u32[]{:S(2)}) collective-permute-start(f32[64,4096]{1,0:T(8,128)} %collective-permute-done.3.refs_3_), channel_id=1, source_target_pairs={{0,1},{1,0},{2,3},{3,2},{4,5},{5,4},{6,7},{7,6},{8,9},{9,8},{10,11... | collective-permute-start | bytes 3145736 | tf_op jit(solution)/shard_map/ppermute | solution.py:189
  74.3 0.7 select_multiply_fusion
  75.0 0.1 mul.37
  75.0 0.7 fusion.3
  75.7 0.7 pad_add_fusion.place
  76.4 0.0 collective-permute-done.4.refs_4_
  76.4 0.0 collective-permute-done.5.refs_5_
  76.4 0.0 collective-permute-done.6.refs_6_
  76.4 0.4 collective-permute-done.7.refs_7_
  76.8 0.0 copy-done.1
  76.8 0.0 copy-done.2
  76.8 0.0 copy-done.3
  76.8 13.5 %products.1 = (bf16[512,4096]{1,0:T(8,128)(2,1)}, bf16[512,4096]{1,0:T(8,128)(2,1)}, f32[32,40,128]{2,1,0:T(8,128)}) custom-call(s32[26]{0:T(128)} %pad_add_fusion.place, f32[64,4096]{1,0:T(8,128)} %copy-done.1, f32[64,4096]{1,0:T(8,128)} %copy-done.2, f32[64,4096]{1,0:T(8,128)} %copy-done.3, f32[64,4096]{1,0:T(8,128)} %collective-permute-done.3.refs_3_, ...), custom_call_target="tpu_custom_call" | custom-call | tf_op jit(solution)/shard_map/products/pallas_call | solution.py:77
  90.3 26.5 %all_to_all.10 = f32[32,40,128]{2,1,0:T(8,128)S(1)} all-to-all(f32[32,40,128]{2,1,0:T(8,128)} %get-tuple-element.12), channel_id=1, replica_groups=mesh['row'=32,'col'=16] {'row'}, dimensions={0} | all-to-all | bytes 1310720 | tf_op jit(solution)/shard_map/all_to_all | solution.py:210
  116.9 0.1 reduce_sum.9
  117.0 24.5 %all_to_all.11.mine = f32[32,40,128]{2,1,0:T(8,128)S(1)} all-to-all(f32[32,40,128]{2,1,0:T(8,128)S(1)} %broadcast_in_dim.2), channel_id=1, replica_groups=mesh['row'=32,'col'=16] {'row'}, dimensions={0} | all-to-all | bytes 1310720 | tf_op jit(solution)/shard_map/all_to_all | solution.py:211
  141.5 0.0 copy-start
  141.5 6.8 %collective-permute-start.8 = (f32[32,24,128]{2,1,0:T(8,128)S(1)}, f32[32,24,128]{2,1,0:T(8,128)S(1)}, u32[]{:S(2)}, u32[]{:S(2)}) collective-permute-start(f32[32,24,128]{2,1,0:T(8,128)S(1)} %slice.4), channel_id=1, source_target_pairs={{0,1},{1,0},{2,3},{3,2},{4,5},{5,4},{6,7},{7,6},{8,9},{9,8},{10,11... | collective-permute-start | bytes 1179656 | tf_op jit(solution)/shard_map/ppermute | solution.py:189
  148.4 1.3 collective-permute-done.8.other
  149.7 0.0 copy-start.4
  149.7 0.0 copy-done
  149.7 0.8 copy-done.4
  150.5 6.7 %solve.1 = (bf16[128,512]{1,0:T(8,128)(2,1)}, bf16[128,512]{1,0:T(8,128)(2,1)}) custom-call(s32[1]{0:T(128)} %bitcast.3.core, f32[32,40,128]{2,1,0:T(8,128)} %copy-done, f32[32,24,128]{2,1,0:T(8,128)} %copy-done.4), custom_call_target="tpu_custom_call" | custom-call | tf_op jit(solution)/shard_map/solve/pallas_call | solution.py:140
  157.2 9.2 %update.1 = f32[4096,128]{1,0:T(8,128)} custom-call(f32[4096,128]{1,0:T(8,128)} %c_ref.1, bf16[512,4096]{1,0:T(8,128)(2,1)} %get-tuple-element.10.vhi, bf16[512,4096]{1,0:T(8,128)(2,1)} %get-tuple-element.11.vlo, bf16[128,512]{1,0:T(8,128)(2,1)} %get-tuple-element.13.xhi, bf16[128,512]{1,0:T(8,128)(2,1)} %get-tuple-element.14.xlo), custom_call_target="tpu_custom_call" | custom-call | tf_op jit(solution)/shard_map/update/pallas_call | solution.py:158
  (2 shorter events, 0.1 us)
Async XLA Ops:
  0.0 18.3 %collective-permute-start = (f32[32,4096]{1,0:T(8,128)}, f32[32,4096]{1,0:T(8,128)S(1)}, u32[]{:S(2)}, u32[]{:S(2)}) collective-permute-start(f32[32,4096]{1,0:T(8,128)} %bitcast.4), channel_id=1, source_target_pairs={{0,2},{1,15},{2,0},{3,5},{4,6},{5,3},{6,4},{7,9},{8,10},{9,7},{10,... | collective-permute-start | bytes 1572872 | tf_op jit(solution)/shard_map/ppermute | solution.py:185
  19.4 57.4 %copy-start.1 = (f32[64,4096]{1,0:T(8,128)}, f32[64,4096]{1,0:T(8,128)S(1)}, u32[]{:S(2)}) copy-start(f32[64,4096]{1,0:T(8,128)S(1)} %pad_maximum_fusion.refs_0_) | copy-start | bytes 3145732
  19.4 15.8 %collective-permute-start.1 = (f32[64,4096]{1,0:T(8,128)S(1)}, f32[64,4096]{1,0:T(8,128)S(1)}, u32[]{:S(2)}, u32[]{:S(2)}) collective-permute-start(f32[64,4096]{1,0:T(8,128)S(1)} %pad_maximum_fusion.refs_0_), channel_id=1, source_target_pairs={{0,14},{1,3},{2,4},{3,1},{4,2},{5,7},{6,8},{7,5},{8,6},{9,11},{10,... | collective-permute-start | bytes 3145736 | tf_op jit(solution)/shard_map/ppermute | solution.py:185
  35.2 41.6 %copy-start.2 = (f32[64,4096]{1,0:T(8,128)}, f32[64,4096]{1,0:T(8,128)S(1)}, u32[]{:S(2)}) copy-start(f32[64,4096]{1,0:T(8,128)S(1)} %collective-permute-done.1.refs_1_) | copy-start | bytes 3145732
  35.2 16.7 %collective-permute-start.2 = (f32[64,4096]{1,0:T(8,128)S(1)}, f32[64,4096]{1,0:T(8,128)S(1)}, u32[]{:S(2)}, u32[]{:S(2)}) collective-permute-start(f32[64,4096]{1,0:T(8,128)S(1)} %collective-permute-done.1.refs_1_), channel_id=1, source_target_pairs={{0,2},{1,15},{2,0},{3,5},{4,6},{5,3},{6,4},{7,9},{8,10},{9,7},{10,... | collective-permute-start | bytes 3145736 | tf_op jit(solution)/shard_map/ppermute | solution.py:185
  52.0 24.9 %copy-start.3 = (f32[64,4096]{1,0:T(8,128)}, f32[64,4096]{1,0:T(8,128)S(1)}, u32[]{:S(2)}) copy-start(f32[64,4096]{1,0:T(8,128)S(1)} %collective-permute-done.2.refs_2_) | copy-start | bytes 3145732
  52.0 15.9 %collective-permute-start.3 = (f32[64,4096]{1,0:T(8,128)S(1)}, f32[64,4096]{1,0:T(8,128)}, u32[]{:S(2)}, u32[]{:S(2)}) collective-permute-start(f32[64,4096]{1,0:T(8,128)S(1)} %collective-permute-done.2.refs_2_), channel_id=1, source_target_pairs={{0,14},{1,3},{2,4},{3,1},{4,2},{5,7},{6,8},{7,5},{8,6},{9,11},{10,... | collective-permute-start | bytes 3145736 | tf_op jit(solution)/shard_map/ppermute | solution.py:185
  53.9 22.5 %collective-permute-start.4 = (f32[64,4096]{1,0:T(8,128)S(1)}, f32[64,4096]{1,0:T(8,128)}, u32[]{:S(2)}, u32[]{:S(2)}) collective-permute-start(f32[64,4096]{1,0:T(8,128)S(1)} %pad_maximum_fusion.refs_0_), channel_id=1, source_target_pairs={{0,1},{1,0},{2,3},{3,2},{4,5},{5,4},{6,7},{7,6},{8,9},{9,8},{10,11... | collective-permute-start | bytes 3145736 | tf_op jit(solution)/shard_map/ppermute | solution.py:189
  61.4 15.0 %collective-permute-start.5 = (f32[64,4096]{1,0:T(8,128)S(1)}, f32[64,4096]{1,0:T(8,128)}, u32[]{:S(2)}, u32[]{:S(2)}) collective-permute-start(f32[64,4096]{1,0:T(8,128)S(1)} %collective-permute-done.1.refs_1_), channel_id=1, source_target_pairs={{0,1},{1,0},{2,3},{3,2},{4,5},{5,4},{6,7},{7,6},{8,9},{9,8},{10,11... | collective-permute-start | bytes 3145736 | tf_op jit(solution)/shard_map/ppermute | solution.py:189
  63.3 13.1 %collective-permute-start.6 = (f32[64,4096]{1,0:T(8,128)S(1)}, f32[64,4096]{1,0:T(8,128)}, u32[]{:S(2)}, u32[]{:S(2)}) collective-permute-start(f32[64,4096]{1,0:T(8,128)S(1)} %collective-permute-done.2.refs_2_), channel_id=1, source_target_pairs={{0,1},{1,0},{2,3},{3,2},{4,5},{5,4},{6,7},{7,6},{8,9},{9,8},{10,11... | collective-permute-start | bytes 3145736 | tf_op jit(solution)/shard_map/ppermute | solution.py:189
  67.9 8.9 %collective-permute-start.7 = (f32[64,4096]{1,0:T(8,128)}, f32[64,4096]{1,0:T(8,128)}, u32[]{:S(2)}, u32[]{:S(2)}) collective-permute-start(f32[64,4096]{1,0:T(8,128)} %collective-permute-done.3.refs_3_), channel_id=1, source_target_pairs={{0,1},{1,0},{2,3},{3,2},{4,5},{5,4},{6,7},{7,6},{8,9},{9,8},{10,11... | collective-permute-start | bytes 3145736 | tf_op jit(solution)/shard_map/ppermute | solution.py:189
  141.5 8.2 %copy-start = (f32[32,40,128]{2,1,0:T(8,128)}, f32[32,40,128]{2,1,0:T(8,128)S(1)}, u32[]{:S(2)}) copy-start(f32[32,40,128]{2,1,0:T(8,128)S(1)} %all_to_all.11.mine) | copy-start | bytes 1966084
  141.5 8.2 %collective-permute-start.8 = (f32[32,24,128]{2,1,0:T(8,128)S(1)}, f32[32,24,128]{2,1,0:T(8,128)S(1)}, u32[]{:S(2)}, u32[]{:S(2)}) collective-permute-start(f32[32,24,128]{2,1,0:T(8,128)S(1)} %slice.4), channel_id=1, source_target_pairs={{0,1},{1,0},{2,3},{3,2},{4,5},{5,4},{6,7},{7,6},{8,9},{9,8},{10,11... | collective-permute-start | bytes 1179656 | tf_op jit(solution)/shard_map/ppermute | solution.py:189
  149.7 0.8 copy-start.4

commit v2 on v1

v2 whole, which is shorter than its diff:
```python
import jax
import jax.numpy as jnp
from jax import lax
from jax.experimental import pallas as pl
from jax.experimental.pallas import tpu as pltpu
from jax.sharding import PartitionSpec as P

F32 = jnp.float32
BF16 = jnp.bfloat16
CHIPS = 8
ROWS = 4096
COLS = 128
NV = 512
STEP = 1024
VMEM = 24 * 1024 * 1024
GRAM_BLOCKS = (
    ((0, 2), (0, 3), (1, 2), (1, 3)),
    ((0, 0), (0, 1), (1, 1), (2, 2), (2, 3), (3, 3)),
)


def split(value):
    high = value.astype(BF16)
    low = (value - high.astype(F32)).astype(BF16)
    return high, low


def nt(left, right):
    return lax.dot_general(left, right, (((1,), (1,)), ((), ())), preferred_element_type=F32)


def nn(left, right):
    return lax.dot_general(left, right, (((1,), (0,)), ((), ())), preferred_element_type=F32)


def hidot(left, right):
    return jnp.dot(left, right, precision=lax.Precision.HIGHEST, preferred_element_type=F32)


def assemble(place, pieces, vhi, vlo):
    for index, piece in enumerate(pieces):
        for block in range(2):
            high, low = split(piece[block * 16 : block * 16 + 16, :])
            at = pl.ds(pl.multiple_of(place[index] + block * 256, 16), 16)
            vhi[at, :] = high
            vlo[at, :] = low


def products_kernel(place, *refs):
    pieces = refs[:16]
    c_ref, out, proj, gram, vhi, vlo = refs[16:]
    step = pl.program_id(0)
    first_core = place[16] == 0

    @pl.when(step == 0)
    def _():
        proj[...] = jnp.zeros_like(proj)
        gram[...] = jnp.zeros_like(gram)

    assemble(place, pieces, vhi, vlo)
    chi, clo = split(c_ref[...])
    both = nn(vhi[...], jnp.concatenate([chi, clo], axis=1))
    proj[...] += both[:, :COLS] + both[:, COLS:] + nn(vlo[...], chi)

    @pl.when(first_core)
    def _():
        lhi, llo = vhi[:256, :], vlo[:256, :]
        rhi, rlo = vhi[256:, :], vlo[256:, :]
        gram[:256, :256] += nt(lhi, rhi) + nt(lhi, rlo) + nt(llo, rhi)

    @pl.when(jnp.logical_not(first_core))
    def _():
        for at in (0, 256):
            high, low = vhi[at : at + 256, :], vlo[at : at + 256, :]
            gram[at : at + 256, :256] += nt(high, high)
            gram[at : at + 256, 256:] += nt(high, low)

    @pl.when(step == pl.num_programs(0) - 1)
    def _():
        out[:, :16, :] = proj[...].reshape(32, 16, COLS)

        @pl.when(first_core)
        def _():
            cross = gram[:256, :256]
            parts = [cross[:128, :128], cross[:128, 128:], cross[128:, :128], cross[128:, 128:]]
            parts.append(jnp.zeros((256, 128), F32))
            out[:, 16:, :] = jnp.concatenate(parts, axis=0).reshape(32, 24, COLS)

        @pl.when(jnp.logical_not(first_core))
        def _():
            parts = []
            for at in (0, 256):
                mixed = gram[at : at + 256, 256:]
                square = gram[at : at + 256, :256] + mixed + mixed.T
                parts += [square[:128, :128], square[:128, 128:], square[128:, 128:]]
            out[:, 16:, :] = jnp.concatenate(parts, axis=0).reshape(32, 24, COLS)


def products(place, pieces, current):
    return pl.pallas_call(
        products_kernel,
        grid=(ROWS // STEP,),
        in_specs=[pl.BlockSpec(memory_space=pltpu.SMEM)]
        + [pl.BlockSpec((32, STEP), lambda k: (0, k))] * 16
        + [pl.BlockSpec((STEP, COLS), lambda k: (k, 0))],
        out_specs=pl.BlockSpec((32, 40, COLS), lambda k: (0, 0, 0)),
        out_shape=jax.ShapeDtypeStruct((32, 40, COLS), F32),
        scratch_shapes=[
            pltpu.VMEM((NV, COLS), F32),
            pltpu.VMEM((512, 512), F32),
            pltpu.VMEM((NV, STEP), BF16),
            pltpu.VMEM((NV, STEP), BF16),
        ],
        compiler_params=pltpu.CompilerParams(vmem_limit_bytes=VMEM),
        name="products",
    )(place, *pieces, current)


def invert_unit(nilpot):
    row = lax.broadcasted_iota(jnp.int32, (128, 128), 0)
    col = lax.broadcasted_iota(jnp.int32, (128, 128), 1)
    eye = (row == col).astype(F32)
    near = [jnp.where(row // 4 == col // 4, n, 0.0) for n in nilpot]
    square = [hidot(n, n) for n in near]
    inverse = [hidot(eye - n, eye + s) for n, s in zip(near, square)]
    size = 4
    while size < 128:
        pair = (row // (2 * size) == col // (2 * size)) & (row // size != col // size)
        right = [hidot(jnp.where(pair, n, 0.0), r) for n, r in zip(nilpot, inverse)]
        inverse = [r - hidot(r, t) for r, t in zip(inverse, right)]
        size *= 2
    return inverse


def solve_kernel(place, mine, other, xt):
    zero = place[16] == 0
    gram = {}
    for which in range(2):
        flat = jnp.where(zero == (which == 0), mine[:, 16:, :], other[...]).reshape(768, 128)
        for index, at in enumerate(GRAM_BLOCKS[which]):
            gram[at] = flat[index * 128 : index * 128 + 128]
    project = mine[:, :16, :].reshape(NV, COLS)
    row = lax.broadcasted_iota(jnp.int32, (128, 128), 0)
    col = lax.broadcasted_iota(jnp.int32, (128, 128), 1)
    scale = [2.0 / jnp.sum(jnp.where(row == col, gram[i, i], 0.0), axis=1, keepdims=True) for i in range(4)]
    inverse = invert_unit([jnp.where(row < col, gram[i, i] * scale[i], 0.0) for i in range(4)])
    coef = [None] * 4
    for i in range(3, -1, -1):
        rhs = project[i * 128 : i * 128 + 128]
        if i < 3:
            panel = jnp.concatenate([gram[i, j] for j in range(i + 1, 4)], axis=1)
            rhs = rhs - hidot(panel, jnp.concatenate(coef[i + 1 :], axis=0))
        coef[i] = hidot(inverse[i], rhs * scale[i])
    high, low = split(jnp.concatenate(coef, axis=0).T)
    xt[:COLS, :] = high
    xt[COLS:, :] = low


def solve(place, mine, other):
    return pl.pallas_call(
        solve_kernel,
        in_specs=[pl.BlockSpec(memory_space=pltpu.SMEM)] + [pl.BlockSpec(memory_space=pltpu.VMEM)] * 2,
        out_specs=pl.BlockSpec(memory_space=pltpu.VMEM),
        out_shape=jax.ShapeDtypeStruct((2 * COLS, NV), BF16),
        compiler_params=pltpu.CompilerParams(vmem_limit_bytes=VMEM),
        name="solve",
    )(place, mine, other)


def update_kernel(place, *refs):
    pieces = refs[:16]
    c_ref, xt, out, vhi, vlo = refs[16:]
    assemble(place, pieces, vhi, vlo)
    both = nn(xt[...], vhi[...])
    change = both[:COLS] + both[COLS:] + nn(xt[:COLS, :], vlo[...])
    out[...] = c_ref[...] - change.T


def update(place, pieces, current, xt):
    return pl.pallas_call(
        update_kernel,
        grid=(ROWS // STEP,),
        in_specs=[pl.BlockSpec(memory_space=pltpu.SMEM)]
        + [pl.BlockSpec((32, STEP), lambda k: (0, k))] * 16
        + [pl.BlockSpec((STEP, COLS), lambda k: (k, 0)), pl.BlockSpec((2 * COLS, NV), lambda k: (0, 0))],
        out_specs=pl.BlockSpec((STEP, COLS), lambda k: (k, 0)),
        out_shape=jax.ShapeDtypeStruct((ROWS, COLS), F32),
        scratch_shapes=[pltpu.VMEM((NV, STEP), BF16), pltpu.VMEM((NV, STEP), BF16)],
        compiler_params=pltpu.CompilerParams(vmem_limit_bytes=VMEM),
        name="update",
    )(place, *pieces, current, xt)


def shift(value, way):
    perm = []
    for chip in range(CHIPS):
        for core in range(2):
            target = (chip + way * (1 - 2 * core)) % CHIPS
            perm.append((chip * 2 + core, target * 2 + core))
    return lax.ppermute(value, "col", perm)


def swap_cores(value):
    return lax.ppermute(value, "col", [(i, i ^ 1) for i in range(2 * CHIPS)])


def shards(eigvecs, householder):
    me = lax.axis_index("col")
    chip, core = me // 2, me % 2
    steps = jnp.array((0, -1, 1, -2, 2, -3, 3, -4), jnp.int32) * (1 - 2 * core)
    here = ((chip + steps + 8) % CHIPS) * 32 + core * 16
    there = ((chip - steps + 8) % CHIPS) * 32 + (1 - core) * 16
    place = jnp.concatenate([here, there, core.reshape(1)])

    own = householder.transpose(0, 2, 1).reshape(32, ROWS)
    pieces = [own]
    ahead = behind = own
    for _ in range(3):
        ahead, behind = shift(ahead, 1), shift(behind, -1)
        pieces += [ahead, behind]
    pieces.append(shift(ahead, 1))
    pieces += [swap_cores(piece) for piece in pieces]

    partial = products(place, pieces, eigvecs)
    summed = lax.all_to_all(partial, "row", 0, 0, tiled=True).sum(axis=0)
    mine = lax.all_to_all(jnp.broadcast_to(summed[None], (32, 40, COLS)), "row", 0, 0, tiled=True)
    other = swap_cores(mine[:, 16:, :])
    return update(place, pieces, eigvecs, solve(place, mine, other))


def solution(mesh):
    in_specs = (P("row", "col"), P(None, "row", "col"))
    out_specs = P("row", "col")
    return jax.shard_map(shards, mesh=mesh, in_specs=in_specs, out_specs=out_specs, check_vma=False)
```

time: 167 us -> 158 us (0.946)
  waiting for transfers between devices: 36.8 us -> 14.7 us
  starting transfers between devices: 44.8 us -> 60 us
  Pallas kernels: 29.4 us -> 21.2 us
  local copies, waits for them, and re-layouts: 0.93 us -> 6.4 us
    ppermute x4 -> x7, waiting for transfers between devices: 35.1 us -> 11.9 us  [shift(): return lax.ppermute(value, 'col', perm)]
    ppermute x4 -> x7, starting transfers between devices: 19.9 us -> 33.3 us  [shift(): return lax.ppermute(value, 'col', perm)]
    pallas_call x2, Pallas kernels: 22.6 us -> 15.8 us  [the longest x1 9.09 us: products(): pl.pallas_call(products_kernel, grid=(ROWS // STEP,), in_specs=[pl.BlockS...]
    unnamed x10 -> x20, local copies, waits for them, and re-layouts: 0.78 us -> 6.33 us
    all_to_all x1, blocking collectives: 26.5 us -> 28.7 us  [shards(): summed = lax.all_to_all(partial, 'row', 0, 0, tiled=True).sum(axis=0)]
    ppermute x5 -> x9, starting transfers between devices: 24.9 us -> 26.8 us  [swap_cores(): return lax.ppermute(value, 'col', [(i, i ^ 1) for i in range(2 * CHIPS)])]
    concatenate x2 -> x1, other arithmetic: 1.77 us -> 0.08 us  [shards(): place = jnp.concatenate([here, there, core.reshape(1)])]
  transfers between devices with their start and end apart: 9 -> 16, of which waited for: 6 -> 4; matrix products, arithmetic and copies ran while one was open for 1% -> 0% of each run, Pallas kernels for 0% -> 0%
where the time goes in v2:
time: 158 us; the launch traced here: 156 us
  starting transfers between devices  60 us (38%)
  blocking collectives  51.9 us (33%)
  Pallas kernels  21.2 us (13%)
  waiting for transfers between devices  14.7 us (9%)
  local copies, waits for them, and re-layouts  6.4 us (4%)
  other arithmetic  1.9 us (1%)
    ppermute x7, starting transfers between devices, shift(): return lax.ppermute(value, 'col', perm)  33.3 us
    all_to_all x1, blocking collectives, shards(): summed = lax.all_to_all(partial, 'row', 0, 0, tiled=True).sum(axis=0)  28.7 us
    ppermute x9, starting transfers between devices, swap_cores(): return lax.ppermute(value, 'col', [(i, i ^ 1) for i in range(2 * CHIPS)])  26.8 us
    all_to_all x1, blocking collectives, shards(): lax.all_to_all(jnp.broadcast_to(summed[None], (32, 40, COLS)), 'row', 0,...  23.2 us
    ppermute x7, waiting for transfers between devices, shift(): return lax.ppermute(value, 'col', perm)  11.9 us
    pallas_call x1, Pallas kernels, products(): pl.pallas_call(products_kernel, grid=(ROWS // STEP,), in_specs=[pl.BlockS...  9.09 us
    pallas_call x1, Pallas kernels, update(): pl.pallas_call(update_kernel, grid=(ROWS // STEP,), in_specs=[pl.BlockSpe...  6.74 us
    unnamed x20, local copies, waits for them, and re-layouts  6.33 us
  transfers between devices with their start and end apart: 16, of which 4 were waited for; matrix products, arithmetic and copies ran while one was open for 0% of the time, Pallas kernels for 0%

profile of v2, /device:TPU:1, one launch (start us, length us, event | category | flops | bytes accessed | tf_op | source)
XLA Modules:
  0.0 156.5 jit_solution(10775308147963396429)
XLA Ops:
  0.0 11.5 %collective-permute-start = (f32[32,4096]{1,0:T(8,128)}, f32[32,4096]{1,0:T(8,128)S(1)}, u32[]{:S(2)}, u32[]{:S(2)}) collective-permute-start(f32[32,4096]{1,0:T(8,128)} %bitcast.4), channel_id=1, source_target_pairs={{0,2},{1,15},{2,4},{3,1},{4,6},{5,3},{6,8},{7,5},{8,10},{9,7},{10,... | collective-permute-start | bytes 1572872 | tf_op jit(solution)/shard_map/ppermute | solution.py:200
  11.5 1.9 %collective-permute-start.1 = (f32[32,4096]{1,0:T(8,128)}, f32[32,4096]{1,0:T(8,128)S(1)}, u32[]{:S(2)}, u32[]{:S(2)}) collective-permute-start(f32[32,4096]{1,0:T(8,128)} %bitcast.5), channel_id=1, source_target_pairs={{0,14},{1,3},{2,0},{3,5},{4,2},{5,7},{6,4},{7,9},{8,6},{9,11},{10,... | collective-permute-start | bytes 1572872 | tf_op jit(solution)/shard_map/ppermute | solution.py:200
  13.4 7.0 %collective-permute-done.refs_1_ = f32[32,4096]{1,0:T(8,128)S(1)} collective-permute-done((f32[32,4096]{1,0:T(8,128)}, f32[32,4096]{1,0:T(8,128)S(1)}, u32[]{:S(2)}, u32[]{:S(2)}) %collective-permute-start) | collective-permute-done | bytes 524320 | tf_op jit(solution)/shard_map/ppermute | solution.py:200
  20.4 5.2 %collective-permute-start.2 = (f32[32,4096]{1,0:T(8,128)S(1)}, f32[32,4096]{1,0:T(8,128)S(1)}, u32[]{:S(2)}, u32[]{:S(2)}) collective-permute-start(f32[32,4096]{1,0:T(8,128)S(1)} %collective-permute-done.refs_1_), channel_id=1, source_target_pairs={{0,2},{1,15},{2,4},{3,1},{4,6},{5,3},{6,8},{7,5},{8,10},{9,7},{10,... | collective-permute-start | bytes 1572872 | tf_op jit(solution)/shard_map/ppermute | solution.py:200
  25.6 0.0 collective-permute-done.1.refs_2_
  25.6 1.9 %collective-permute-start.3 = (f32[32,4096]{1,0:T(8,128)S(1)}, f32[32,4096]{1,0:T(8,128)S(1)}, u32[]{:S(2)}, u32[]{:S(2)}) collective-permute-start(f32[32,4096]{1,0:T(8,128)S(1)} %collective-permute-done.1.refs_2_), channel_id=1, source_target_pairs={{0,14},{1,3},{2,0},{3,5},{4,2},{5,7},{6,4},{7,9},{8,6},{9,11},{10,... | collective-permute-start | bytes 1572872 | tf_op jit(solution)/shard_map/ppermute | solution.py:200
  27.6 4.9 %collective-permute-done.2.refs_3_ = f32[32,4096]{1,0:T(8,128)S(1)} collective-permute-done((f32[32,4096]{1,0:T(8,128)S(1)}, f32[32,4096]{1,0:T(8,128)S(1)}, u32[]{:S(2)}, u32[]{:S(2)}) %collective-permute-start.2) | collective-permute-done | bytes 524320 | tf_op jit(solution)/shard_map/ppermute | solution.py:200
  32.5 5.3 %collective-permute-start.4 = (f32[32,4096]{1,0:T(8,128)S(1)}, f32[32,4096]{1,0:T(8,128)S(1)}, u32[]{:S(2)}, u32[]{:S(2)}) collective-permute-start(f32[32,4096]{1,0:T(8,128)S(1)} %collective-permute-done.2.refs_3_), channel_id=1, source_target_pairs={{0,2},{1,15},{2,4},{3,1},{4,6},{5,3},{6,8},{7,5},{8,10},{9,7},{10,... | collective-permute-start | bytes 1572872 | tf_op jit(solution)/shard_map/ppermute | solution.py:200
  37.8 5.0 %collective-permute-start.7 = (f32[32,4096]{1,0:T(8,128)}, f32[32,4096]{1,0:T(8,128)S(1)}, u32[]{:S(2)}, u32[]{:S(2)}) collective-permute-start(f32[32,4096]{1,0:T(8,128)} %bitcast.6), channel_id=1, source_target_pairs={{0,1},{1,0},{2,3},{3,2},{4,5},{5,4},{6,7},{7,6},{8,9},{9,8},{10,11... | collective-permute-start | bytes 1572872 | tf_op jit(solution)/shard_map/ppermute | solution.py:204
  42.8 1.9 %collective-permute-start.9 = (f32[32,4096]{1,0:T(8,128)S(1)}, f32[32,4096]{1,0:T(8,128)S(1)}, u32[]{:S(2)}, u32[]{:S(2)}) collective-permute-start(f32[32,4096]{1,0:T(8,128)S(1)} %collective-permute-done.1.refs_2_), channel_id=1, source_target_pairs={{0,1},{1,0},{2,3},{3,2},{4,5},{5,4},{6,7},{7,6},{8,9},{9,8},{10,11... | collective-permute-start | bytes 1572872 | tf_op jit(solution)/shard_map/ppermute | solution.py:204
  44.7 2.4 %collective-permute-start.8 = (f32[32,4096]{1,0:T(8,128)S(1)}, f32[32,4096]{1,0:T(8,128)S(1)}, u32[]{:S(2)}, u32[]{:S(2)}) collective-permute-start(f32[32,4096]{1,0:T(8,128)S(1)} %collective-permute-done.refs_1_), channel_id=1, source_target_pairs={{0,1},{1,0},{2,3},{3,2},{4,5},{5,4},{6,7},{7,6},{8,9},{9,8},{10,11... | collective-permute-start | bytes 1572872 | tf_op jit(solution)/shard_map/ppermute | solution.py:204
  47.1 0.0 collective-permute-done.3.refs_4_
  47.1 2.7 %collective-permute-start.5 = (f32[32,4096]{1,0:T(8,128)S(1)}, f32[32,4096]{1,0:T(8,128)}, u32[]{:S(2)}, u32[]{:S(2)}) collective-permute-start(f32[32,4096]{1,0:T(8,128)S(1)} %collective-permute-done.3.refs_4_), channel_id=1, source_target_pairs={{0,14},{1,3},{2,0},{3,5},{4,2},{5,7},{6,4},{7,9},{8,6},{9,11},{10,... | collective-permute-start | bytes 1572872 | tf_op jit(solution)/shard_map/ppermute | solution.py:200
  49.9 0.0 collective-permute-done.4.refs_5_
  49.9 4.7 %collective-permute-start.6 = (f32[32,4096]{1,0:T(8,128)S(1)}, f32[32,4096]{1,0:T(8,128)}, u32[]{:S(2)}, u32[]{:S(2)}) collective-permute-start(f32[32,4096]{1,0:T(8,128)S(1)} %collective-permute-done.4.refs_5_), channel_id=1, source_target_pairs={{0,2},{1,15},{2,4},{3,1},{4,6},{5,3},{6,8},{7,5},{8,10},{9,7},{10,... | collective-permute-start | bytes 1572872 | tf_op jit(solution)/shard_map/ppermute | solution.py:200
  54.6 0.0 collective-permute-done.7.refs_8_
  54.6 2.2 %collective-permute-start.11 = (f32[32,4096]{1,0:T(8,128)S(1)}, f32[32,4096]{1,0:T(8,128)}, u32[]{:S(2)}, u32[]{:S(2)}) collective-permute-start(f32[32,4096]{1,0:T(8,128)S(1)} %collective-permute-done.3.refs_4_), channel_id=1, source_target_pairs={{0,1},{1,0},{2,3},{3,2},{4,5},{5,4},{6,7},{7,6},{8,9},{9,8},{10,11... | collective-permute-start | bytes 1572872 | tf_op jit(solution)/shard_map/ppermute | solution.py:204
  56.8 0.0 collective-permute-done.9.refs_10_
  56.8 0.0 copy-start.4
  56.8 0.8 copy-done.4
  57.7 2.1 %collective-permute-start.10 = (f32[32,4096]{1,0:T(8,128)S(1)}, f32[32,4096]{1,0:T(8,128)}, u32[]{:S(2)}, u32[]{:S(2)}) collective-permute-start(f32[32,4096]{1,0:T(8,128)S(1)} %collective-permute-done.2.refs_3_), channel_id=1, source_target_pairs={{0,1},{1,0},{2,3},{3,2},{4,5},{5,4},{6,7},{7,6},{8,9},{9,8},{10,11... | collective-permute-start | bytes 1572872 | tf_op jit(solution)/shard_map/ppermute | solution.py:204
  59.8 0.0 collective-permute-done.8.refs_9_
  59.8 0.0 copy-start.7
  59.8 0.8 copy-done.7
  60.6 2.2 %collective-permute-start.12 = (f32[32,4096]{1,0:T(8,128)S(1)}, f32[32,4096]{1,0:T(8,128)}, u32[]{:S(2)}, u32[]{:S(2)}) collective-permute-start(f32[32,4096]{1,0:T(8,128)S(1)} %collective-permute-done.4.refs_5_), channel_id=1, source_target_pairs={{0,1},{1,0},{2,3},{3,2},{4,5},{5,4},{6,7},{7,6},{8,9},{9,8},{10,11... | collective-permute-start | bytes 1572872 | tf_op jit(solution)/shard_map/ppermute | solution.py:204
  62.8 0.0 collective-permute-done.5.refs_6_
  62.8 2.8 %collective-permute-start.13 = (f32[32,4096]{1,0:T(8,128)}, f32[32,4096]{1,0:T(8,128)}, u32[]{:S(2)}, u32[]{:S(2)}) collective-permute-start(f32[32,4096]{1,0:T(8,128)} %collective-permute-done.5.refs_6_), channel_id=1, source_target_pairs={{0,1},{1,0},{2,3},{3,2},{4,5},{5,4},{6,7},{7,6},{8,9},{9,8},{10,11... | collective-permute-start | bytes 1572872 | tf_op jit(solution)/shard_map/ppermute | solution.py:204
  65.6 0.0 collective-permute-done.6.refs_7_
  65.6 1.9 %collective-permute-start.14 = (f32[32,4096]{1,0:T(8,128)}, f32[32,4096]{1,0:T(8,128)}, u32[]{:S(2)}, u32[]{:S(2)}) collective-permute-start(f32[32,4096]{1,0:T(8,128)} %collective-permute-done.6.refs_7_), channel_id=1, source_target_pairs={{0,1},{1,0},{2,3},{3,2},{4,5},{5,4},{6,7},{7,6},{8,9},{9,8},{10,11... | collective-permute-start | bytes 1572872 | tf_op jit(solution)/shard_map/ppermute | solution.py:204
  67.6 0.7 fusion.3
  68.3 0.1 pad_add_fusion.place
  68.3 0.0 collective-permute-done.11.refs_12_
  68.3 0.0 collective-permute-done.10.refs_11_
  68.3 0.0 collective-permute-done.13.refs_14_
  68.4 0.0 collective-permute-done.12.refs_13_
  68.4 1.4 collective-permute-done.14.refs_15_
  69.8 0.0 copy-start
  69.8 1.6 %copy-done = f32[4096,128]{1,0:T(8,128)S(1)} copy-done((f32[4096,128]{1,0:T(8,128)S(1)}, f32[4096,128]{1,0:T(8,128)}, u32[]{:S(2)}) %copy-start) | copy-done | bytes 2097176
  71.4 0.0 copy-start.2
  71.4 1.0 copy-done.2
  72.4 0.0 copy-start.5
  72.4 1.0 copy-done.5
  73.5 0.0 copy-start.8
  73.5 1.0 copy-done.8
  74.5 9.1 %products.1 = f32[32,40,128]{2,1,0:T(8,128)S(1)} custom-call(s32[17]{0:T(128)S(1)} %pad_add_fusion.place, f32[32,4096]{1,0:T(8,128)S(1)} %bitcast.7, f32[32,4096]{1,0:T(8,128)S(1)} %collective-permute-done.refs_1_, f32[32,4096]{1,0:T(8,128)S(1)} %collective-permute-done.1.refs_2_, f32[32,4096]{1,0:T(8,128)S(1)} %collective-permute-done.2.refs_3_, ...), custom_call_target="tpu_custom_call" | custom-call | tf_op jit(solution)/shard_map/products/pallas_call | solution.py:100
  83.6 28.7 %all_to_all.10 = f32[32,40,128]{2,1,0:T(8,128)} all-to-all(f32[32,40,128]{2,1,0:T(8,128)S(1)} %products.1), channel_id=1, replica_groups=mesh['row'=32,'col'=16] {'row'}, dimensions={0} | all-to-all | bytes 1310720 | tf_op jit(solution)/shard_map/all_to_all | solution.py:225
  112.3 1.1 reduce_sum.9
  113.4 0.0 copy-start.1
  113.4 0.0 copy-start.3
  113.5 0.0 copy-start.6
  113.5 0.0 copy-start.9
  113.5 23.2 %all_to_all.11.mine = f32[32,40,128]{2,1,0:T(8,128)S(1)} all-to-all(f32[32,40,128]{2,1,0:T(8,128)S(1)} %broadcast_in_dim.2), channel_id=1, replica_groups=mesh['row'=32,'col'=16] {'row'}, dimensions={0} | all-to-all | bytes 1310720 | tf_op jit(solution)/shard_map/all_to_all | solution.py:226
  136.8 6.2 %collective-permute-start.15 = (f32[32,24,128]{2,1,0:T(8,128)S(1)}, f32[32,24,128]{2,1,0:T(8,128)S(1)}, u32[]{:S(2)}, u32[]{:S(2)}) collective-permute-start(f32[32,24,128]{2,1,0:T(8,128)S(1)} %slice.4), channel_id=1, source_target_pairs={{0,1},{1,0},{2,3},{3,2},{4,5},{5,4},{6,7},{7,6},{8,9},{9,8},{10,11... | collective-permute-start | bytes 1179656 | tf_op jit(solution)/shard_map/ppermute | solution.py:204
  143.0 1.3 collective-permute-done.15.other
  144.3 5.4 %solve.1.refs_17_ = bf16[256,512]{1,0:T(8,128)(2,1)S(1)} custom-call(s32[17]{0:T(128)S(1)} %pad_add_fusion.place, f32[32,40,128]{2,1,0:T(8,128)S(1)} %all_to_all.11.mine, f32[32,24,128]{2,1,0:T(8,128)S(1)} %collective-permute-done.15.other), custom_call_target="tpu_custom_call" | custom-call | tf_op jit(solution)/shard_map/solve/pallas_call | solution.py:160
  149.7 0.0 copy-done.1
  149.7 0.0 copy-done.3
  149.7 0.0 copy-done.6
  149.7 0.0 copy-done.9
  149.7 6.7 %update.1 = f32[4096,128]{1,0:T(8,128)} custom-call(s32[17]{0:T(128)S(1)} %pad_add_fusion.place, f32[32,4096]{1,0:T(8,128)S(1)} %bitcast.8, f32[32,4096]{1,0:T(8,128)S(1)} %collective-permute-done.refs_1_, f32[32,4096]{1,0:T(8,128)S(1)} %collective-permute-done.1.refs_2_, f32[32,4096]{1,0:T(8,128)S(1)} %collective-permute-done.2.refs_3_, ...), custom_call_target="tpu_custom_call" | custom-call | tf_op jit(solution)/shard_map/update/pallas_call | solution.py:180
  (2 shorter events, 0.1 us)
Async XLA Ops:
  0.0 20.4 %collective-permute-start = (f32[32,4096]{1,0:T(8,128)}, f32[32,4096]{1,0:T(8,128)S(1)}, u32[]{:S(2)}, u32[]{:S(2)}) collective-permute-start(f32[32,4096]{1,0:T(8,128)} %bitcast.4), channel_id=1, source_target_pairs={{0,2},{1,15},{2,4},{3,1},{4,6},{5,3},{6,8},{7,5},{8,10},{9,7},{10,... | collective-permute-start | bytes 1572872 | tf_op jit(solution)/shard_map/ppermute | solution.py:200
  11.5 14.1 %collective-permute-start.1 = (f32[32,4096]{1,0:T(8,128)}, f32[32,4096]{1,0:T(8,128)S(1)}, u32[]{:S(2)}, u32[]{:S(2)}) collective-permute-start(f32[32,4096]{1,0:T(8,128)} %bitcast.5), channel_id=1, source_target_pairs={{0,14},{1,3},{2,0},{3,5},{4,2},{5,7},{6,4},{7,9},{8,6},{9,11},{10,... | collective-permute-start | bytes 1572872 | tf_op jit(solution)/shard_map/ppermute | solution.py:200
  20.4 12.1 %collective-permute-start.2 = (f32[32,4096]{1,0:T(8,128)S(1)}, f32[32,4096]{1,0:T(8,128)S(1)}, u32[]{:S(2)}, u32[]{:S(2)}) collective-permute-start(f32[32,4096]{1,0:T(8,128)S(1)} %collective-permute-done.refs_1_), channel_id=1, source_target_pairs={{0,2},{1,15},{2,4},{3,1},{4,6},{5,3},{6,8},{7,5},{8,10},{9,7},{10,... | collective-permute-start | bytes 1572872 | tf_op jit(solution)/shard_map/ppermute | solution.py:200
  25.6 21.5 %collective-permute-start.3 = (f32[32,4096]{1,0:T(8,128)S(1)}, f32[32,4096]{1,0:T(8,128)S(1)}, u32[]{:S(2)}, u32[]{:S(2)}) collective-permute-start(f32[32,4096]{1,0:T(8,128)S(1)} %collective-permute-done.1.refs_2_), channel_id=1, source_target_pairs={{0,14},{1,3},{2,0},{3,5},{4,2},{5,7},{6,4},{7,9},{8,6},{9,11},{10,... | collective-permute-start | bytes 1572872 | tf_op jit(solution)/shard_map/ppermute | solution.py:200
  32.5 17.4 %collective-permute-start.4 = (f32[32,4096]{1,0:T(8,128)S(1)}, f32[32,4096]{1,0:T(8,128)S(1)}, u32[]{:S(2)}, u32[]{:S(2)}) collective-permute-start(f32[32,4096]{1,0:T(8,128)S(1)} %collective-permute-done.2.refs_3_), channel_id=1, source_target_pairs={{0,2},{1,15},{2,4},{3,1},{4,6},{5,3},{6,8},{7,5},{8,10},{9,7},{10,... | collective-permute-start | bytes 1572872 | tf_op jit(solution)/shard_map/ppermute | solution.py:200
  37.8 16.8 %collective-permute-start.7 = (f32[32,4096]{1,0:T(8,128)}, f32[32,4096]{1,0:T(8,128)S(1)}, u32[]{:S(2)}, u32[]{:S(2)}) collective-permute-start(f32[32,4096]{1,0:T(8,128)} %bitcast.6), channel_id=1, source_target_pairs={{0,1},{1,0},{2,3},{3,2},{4,5},{5,4},{6,7},{7,6},{8,9},{9,8},{10,11... | collective-permute-start | bytes 1572872 | tf_op jit(solution)/shard_map/ppermute | solution.py:204
  42.8 14.0 %collective-permute-start.9 = (f32[32,4096]{1,0:T(8,128)S(1)}, f32[32,4096]{1,0:T(8,128)S(1)}, u32[]{:S(2)}, u32[]{:S(2)}) collective-permute-start(f32[32,4096]{1,0:T(8,128)S(1)} %collective-permute-done.1.refs_2_), channel_id=1, source_target_pairs={{0,1},{1,0},{2,3},{3,2},{4,5},{5,4},{6,7},{7,6},{8,9},{9,8},{10,11... | collective-permute-start | bytes 1572872 | tf_op jit(solution)/shard_map/ppermute | solution.py:204
  44.7 15.1 %collective-permute-start.8 = (f32[32,4096]{1,0:T(8,128)S(1)}, f32[32,4096]{1,0:T(8,128)S(1)}, u32[]{:S(2)}, u32[]{:S(2)}) collective-permute-start(f32[32,4096]{1,0:T(8,128)S(1)} %collective-permute-done.refs_1_), channel_id=1, source_target_pairs={{0,1},{1,0},{2,3},{3,2},{4,5},{5,4},{6,7},{7,6},{8,9},{9,8},{10,11... | collective-permute-start | bytes 1572872 | tf_op jit(solution)/shard_map/ppermute | solution.py:204
  47.1 15.6 %collective-permute-start.5 = (f32[32,4096]{1,0:T(8,128)S(1)}, f32[32,4096]{1,0:T(8,128)}, u32[]{:S(2)}, u32[]{:S(2)}) collective-permute-start(f32[32,4096]{1,0:T(8,128)S(1)} %collective-permute-done.3.refs_4_), channel_id=1, source_target_pairs={{0,14},{1,3},{2,0},{3,5},{4,2},{5,7},{6,4},{7,9},{8,6},{9,11},{10,... | collective-permute-start | bytes 1572872 | tf_op jit(solution)/shard_map/ppermute | solution.py:200
  49.9 15.7 %collective-permute-start.6 = (f32[32,4096]{1,0:T(8,128)S(1)}, f32[32,4096]{1,0:T(8,128)}, u32[]{:S(2)}, u32[]{:S(2)}) collective-permute-start(f32[32,4096]{1,0:T(8,128)S(1)} %collective-permute-done.4.refs_5_), channel_id=1, source_target_pairs={{0,2},{1,15},{2,4},{3,1},{4,6},{5,3},{6,8},{7,5},{8,10},{9,7},{10,... | collective-permute-start | bytes 1572872 | tf_op jit(solution)/shard_map/ppermute | solution.py:200
  54.6 13.7 %collective-permute-start.11 = (f32[32,4096]{1,0:T(8,128)S(1)}, f32[32,4096]{1,0:T(8,128)}, u32[]{:S(2)}, u32[]{:S(2)}) collective-permute-start(f32[32,4096]{1,0:T(8,128)S(1)} %collective-permute-done.3.refs_4_), channel_id=1, source_target_pairs={{0,1},{1,0},{2,3},{3,2},{4,5},{5,4},{6,7},{7,6},{8,9},{9,8},{10,11... | collective-permute-start | bytes 1572872 | tf_op jit(solution)/shard_map/ppermute | solution.py:204
  56.8 0.8 copy-start.4
  57.7 10.7 %collective-permute-start.10 = (f32[32,4096]{1,0:T(8,128)S(1)}, f32[32,4096]{1,0:T(8,128)}, u32[]{:S(2)}, u32[]{:S(2)}) collective-permute-start(f32[32,4096]{1,0:T(8,128)S(1)} %collective-permute-done.2.refs_3_), channel_id=1, source_target_pairs={{0,1},{1,0},{2,3},{3,2},{4,5},{5,4},{6,7},{7,6},{8,9},{9,8},{10,11... | collective-permute-start | bytes 1572872 | tf_op jit(solution)/shard_map/ppermute | solution.py:204
  59.8 0.8 copy-start.7
  60.6 7.8 %collective-permute-start.12 = (f32[32,4096]{1,0:T(8,128)S(1)}, f32[32,4096]{1,0:T(8,128)}, u32[]{:S(2)}, u32[]{:S(2)}) collective-permute-start(f32[32,4096]{1,0:T(8,128)S(1)} %collective-permute-done.4.refs_5_), channel_id=1, source_target_pairs={{0,1},{1,0},{2,3},{3,2},{4,5},{5,4},{6,7},{7,6},{8,9},{9,8},{10,11... | collective-permute-start | bytes 1572872 | tf_op jit(solution)/shard_map/ppermute | solution.py:204
  62.8 5.6 %collective-permute-start.13 = (f32[32,4096]{1,0:T(8,128)}, f32[32,4096]{1,0:T(8,128)}, u32[]{:S(2)}, u32[]{:S(2)}) collective-permute-start(f32[32,4096]{1,0:T(8,128)} %collective-permute-done.5.refs_6_), channel_id=1, source_target_pairs={{0,1},{1,0},{2,3},{3,2},{4,5},{5,4},{6,7},{7,6},{8,9},{9,8},{10,11... | collective-permute-start | bytes 1572872 | tf_op jit(solution)/shard_map/ppermute | solution.py:204
  65.6 4.1 %collective-permute-start.14 = (f32[32,4096]{1,0:T(8,128)}, f32[32,4096]{1,0:T(8,128)}, u32[]{:S(2)}, u32[]{:S(2)}) collective-permute-start(f32[32,4096]{1,0:T(8,128)} %collective-permute-done.6.refs_7_), channel_id=1, source_target_pairs={{0,1},{1,0},{2,3},{3,2},{4,5},{5,4},{6,7},{7,6},{8,9},{9,8},{10,11... | collective-permute-start | bytes 1572872 | tf_op jit(solution)/shard_map/ppermute | solution.py:204
  69.8 1.6 %copy-start = (f32[4096,128]{1,0:T(8,128)S(1)}, f32[4096,128]{1,0:T(8,128)}, u32[]{:S(2)}) copy-start(f32[4096,128]{1,0:T(8,128)} %refs_16_.3) | copy-start | bytes 6291460
  71.4 1.0 copy-start.2
  72.4 1.0 copy-start.5
  73.5 1.0 copy-start.8
  113.4 36.2 %copy-start.1 = (f32[4096,128]{1,0:T(8,128)S(1)}, f32[4096,128]{1,0:T(8,128)}, u32[]{:S(2)}) copy-start(f32[4096,128]{1,0:T(8,128)} %refs_16_.3) | copy-start | bytes 6291460
  113.4 36.2 %copy-start.3 = (f32[2,4096,16]{1,2,0:T(8,128)S(1)}, f32[2,4096,16]{1,2,0:T(8,128)}, u32[]{:S(2)}) copy-start(f32[2,4096,16]{1,2,0:T(8,128)} %param.4) | copy-start | bytes 1572868
  113.5 36.2 %copy-start.6 = (f32[32,4096]{1,0:T(8,128)S(1)}, f32[32,4096]{1,0:T(8,128)}, u32[]{:S(2)}) copy-start(f32[32,4096]{1,0:T(8,128)} %copy-done.4) | copy-start | bytes 1572868
  113.5 36.2 %copy-start.9 = (f32[32,4096]{1,0:T(8,128)S(1)}, f32[32,4096]{1,0:T(8,128)}, u32[]{:S(2)}) copy-start(f32[32,4096]{1,0:T(8,128)} %copy-done.7) | copy-start | bytes 1572868
  136.8 7.5 %collective-permute-start.15 = (f32[32,24,128]{2,1,0:T(8,128)S(1)}, f32[32,24,128]{2,1,0:T(8,128)S(1)}, u32[]{:S(2)}, u32[]{:S(2)}) collective-permute-start(f32[32,24,128]{2,1,0:T(8,128)S(1)} %slice.4), channel_id=1, source_target_pairs={{0,1},{1,0},{2,3},{3,2},{4,5},{5,4},{6,7},{7,6},{8,9},{9,8},{10,11... | collective-permute-start | bytes 1179656 | tf_op jit(solution)/shard_map/ppermute | solution.py:204

commit v3 on v2

--- a/solution.py
+++ b/solution.py
@@ -38,82 +38,147 @@
 
 
 def assemble(place, pieces, vhi, vlo):
-    for index, piece in enumerate(pieces):
-        for block in range(2):
-            high, low = split(piece[block * 16 : block * 16 + 16, :])
-            at = pl.ds(pl.multiple_of(place[index] + block * 256, 16), 16)
+    index = 0
+    for piece in pieces:
+        for first in range(0, piece.shape[0], 16):
+            high, low = split(piece[first : first + 16, :])
+            at = pl.ds(pl.multiple_of(place[index], 16), 16)
             vhi[at, :] = high
             vlo[at, :] = low
-
-
-def products_kernel(place, *refs):
-    pieces = refs[:16]
-    c_ref, out, proj, gram, vhi, vlo = refs[16:]
-    step = pl.program_id(0)
-    first_core = place[16] == 0
-
-    @pl.when(step == 0)
-    def _():
-        proj[...] = jnp.zeros_like(proj)
-        gram[...] = jnp.zeros_like(gram)
-
-    assemble(place, pieces, vhi, vlo)
+            index += 1
+
+
+def add_projection(proj, c_ref, vhi, vlo):
     chi, clo = split(c_ref[...])
     both = nn(vhi[...], jnp.concatenate([chi, clo], axis=1))
     proj[...] += both[:, :COLS] + both[:, COLS:] + nn(vlo[...], chi)
 
+
+def add_square(gram, vhi, vlo):
+    gram[:, :256] += nt(vhi[...], vhi[...])
+    gram[:, 256:] += nt(vhi[...], vlo[...])
+
+
+def upper_blocks(gram):
+    mixed = gram[:, 256:]
+    square = gram[:, :256] + mixed + mixed.T
+    return [square[:128, :128], square[:128, 128:], square[128:, 128:]]
+
+
+def later_kernel(place, *refs):
+    pieces = refs[:8]
+    c_ref, vhi, vlo, proj, out, gram = refs[8:]
+    step = pl.program_id(0)
+
+    @pl.when(step == 0)
+    def _():
+        proj[...] = jnp.zeros_like(proj)
+        gram[...] = jnp.zeros_like(gram)
+
+    assemble(place, pieces, vhi, vlo)
+    add_projection(proj, c_ref, vhi, vlo)
+
+    @pl.when(place[16] == 1)
+    def _():
+        add_square(gram, vhi, vlo)
+
+    @pl.when(step == pl.num_programs(0) - 1)
+    def _():
+        out[...] = jnp.concatenate(upper_blocks(gram), axis=0)
+
+
+def strip(rows):
+    return pl.BlockSpec((rows, STEP), lambda k: (0, k))
+
+
+def whole(*shape):
+    return pl.BlockSpec(shape, lambda k: (0,) * len(shape))
+
+
+def later_products(place, pieces, current):
+    return pl.pallas_call(
+        later_kernel,
+        grid=(ROWS // STEP,),
+        in_specs=[pl.BlockSpec(memory_space=pltpu.SMEM)]
+        + [strip(piece.shape[0]) for piece in pieces]
+        + [pl.BlockSpec((STEP, COLS), lambda k: (k, 0))],
+        out_specs=[strip(256), strip(256), whole(256, COLS), whole(384, 128)],
+        out_shape=[
+            jax.ShapeDtypeStruct((256, ROWS), BF16),
+            jax.ShapeDtypeStruct((256, ROWS), BF16),
+            jax.ShapeDtypeStruct((256, COLS), F32),
+            jax.ShapeDtypeStruct((384, 128), F32),
+        ],
+        scratch_shapes=[pltpu.VMEM((256, 512), F32)],
+        compiler_params=pltpu.CompilerParams(vmem_limit_bytes=VMEM),
+        cost_estimate=pl.CostEstimate(flops=4 * 10**9, bytes_accessed=10 * 2**20, transcendentals=0),
+        name="later_products",
+    )(place, *pieces, current)
+
+
+def earlier_kernel(place, mine, other, c_ref, whi, wlo, proj1, gram1, vhi, vlo, out, proj, gram):
+    step = pl.program_id(0)
+    first_core = place[16] == 0
+
+    @pl.when(step == 0)
+    def _():
+        proj[...] = jnp.zeros_like(proj)
+        gram[...] = jnp.zeros_like(gram)
+
+    assemble(place, [mine, other], vhi, vlo)
+    add_projection(proj, c_ref, vhi, vlo)
+
     @pl.when(first_core)
     def _():
-        lhi, llo = vhi[:256, :], vlo[:256, :]
-        rhi, rlo = vhi[256:, :], vlo[256:, :]
-        gram[:256, :256] += nt(lhi, rhi) + nt(lhi, rlo) + nt(llo, rhi)
+        gram[:, :256] += nt(vhi[...], whi[...]) + nt(vhi[...], wlo[...]) + nt(vlo[...], whi[...])
 
     @pl.when(jnp.logical_not(first_core))
     def _():
-        for at in (0, 256):
-            high, low = vhi[at : at + 256, :], vlo[at : at + 256, :]
-            gram[at : at + 256, :256] += nt(high, high)
-            gram[at : at + 256, 256:] += nt(high, low)
+        add_square(gram, vhi, vlo)
 
     @pl.when(step == pl.num_programs(0) - 1)
     def _():
-        out[:, :16, :] = proj[...].reshape(32, 16, COLS)
+        out[:, :16, :] = jnp.concatenate([proj[...], proj1[...]], axis=0).reshape(32, 16, COLS)
 
         @pl.when(first_core)
         def _():
-            cross = gram[:256, :256]
+            cross = gram[:, :256]
             parts = [cross[:128, :128], cross[:128, 128:], cross[128:, :128], cross[128:, 128:]]
             parts.append(jnp.zeros((256, 128), F32))
             out[:, 16:, :] = jnp.concatenate(parts, axis=0).reshape(32, 24, COLS)
 
         @pl.when(jnp.logical_not(first_core))
         def _():
-            parts = []
-            for at in (0, 256):
-                mixed = gram[at : at + 256, 256:]
-                square = gram[at : at + 256, :256] + mixed + mixed.T
-                parts += [square[:128, :128], square[:128, 128:], square[128:, 128:]]
+            parts = upper_blocks(gram) + [gram1[...]]
             out[:, 16:, :] = jnp.concatenate(parts, axis=0).reshape(32, 24, COLS)
 
 
-def products(place, pieces, current):
+def earlier_products(place, mine, other, current, later):
+    whi, wlo, proj1, gram1 = later
     return pl.pallas_call(
-        products_kernel,
+        earlier_kernel,
         grid=(ROWS // STEP,),
-        in_specs=[pl.BlockSpec(memory_space=pltpu.SMEM)]
-        + [pl.BlockSpec((32, STEP), lambda k: (0, k))] * 16
-        + [pl.BlockSpec((STEP, COLS), lambda k: (k, 0))],
-        out_specs=pl.BlockSpec((32, 40, COLS), lambda k: (0, 0, 0)),
-        out_shape=jax.ShapeDtypeStruct((32, 40, COLS), F32),
-        scratch_shapes=[
-            pltpu.VMEM((NV, COLS), F32),
-            pltpu.VMEM((512, 512), F32),
-            pltpu.VMEM((NV, STEP), BF16),
-            pltpu.VMEM((NV, STEP), BF16),
+        in_specs=[
+            pl.BlockSpec(memory_space=pltpu.SMEM),
+            strip(128),
+            strip(128),
+            pl.BlockSpec((STEP, COLS), lambda k: (k, 0)),
+            strip(256),
+            strip(256),
+            whole(256, COLS),
+            whole(384, 128),
         ],
+        out_specs=[strip(256), strip(256), whole(32, 40, COLS)],
+        out_shape=[
+            jax.ShapeDtypeStruct((256, ROWS), BF16),
+            jax.ShapeDtypeStruct((256, ROWS), BF16),
+            jax.ShapeDtypeStruct((32, 40, COLS), F32),
+        ],
+        scratch_shapes=[pltpu.VMEM((256, COLS), F32), pltpu.VMEM((256, 512), F32)],
         compiler_params=pltpu.CompilerParams(vmem_limit_bytes=VMEM),
-        name="products",
-    )(place, *pieces, current)
+        cost_estimate=pl.CostEstimate(flops=4 * 10**9, bytes_accessed=14 * 2**20, transcendentals=0),
+        name="earlier_products",
+    )(place, mine, other, current, whi, wlo, proj1, gram1)
 
 
 def invert_unit(nilpot):
@@ -167,28 +232,23 @@
     )(place, mine, other)
 
 
-def update_kernel(place, *refs):
-    pieces = refs[:16]
-    c_ref, xt, out, vhi, vlo = refs[16:]
-    assemble(place, pieces, vhi, vlo)
-    both = nn(xt[...], vhi[...])
-    change = both[:COLS] + both[COLS:] + nn(xt[:COLS, :], vlo[...])
-    out[...] = c_ref[...] - change.T
-
-
-def update(place, pieces, current, xt):
+def update_kernel(c_ref, vhi, vlo, whi, wlo, xt, out):
+    xhi = xt[:COLS, :]
+    change = nn(xhi[:, :256], vlo[...]) + nn(xhi[:, 256:], wlo[...])
+    both = nn(xt[:, :256], vhi[...]) + nn(xt[:, 256:], whi[...])
+    out[...] = c_ref[...] - (change + both[:COLS] + both[COLS:]).T
+
+
+def update(current, parts, xt):
     return pl.pallas_call(
         update_kernel,
         grid=(ROWS // STEP,),
-        in_specs=[pl.BlockSpec(memory_space=pltpu.SMEM)]
-        + [pl.BlockSpec((32, STEP), lambda k: (0, k))] * 16
-        + [pl.BlockSpec((STEP, COLS), lambda k: (k, 0)), pl.BlockSpec((2 * COLS, NV), lambda k: (0, 0))],
+        in_specs=[pl.BlockSpec((STEP, COLS), lambda k: (k, 0))] + [strip(256)] * 4 + [whole(2 * COLS, NV)],
         out_specs=pl.BlockSpec((STEP, COLS), lambda k: (k, 0)),
         out_shape=jax.ShapeDtypeStruct((ROWS, COLS), F32),
-        scratch_shapes=[pltpu.VMEM((NV, STEP), BF16), pltpu.VMEM((NV, STEP), BF16)],
         compiler_params=pltpu.CompilerParams(vmem_limit_bytes=VMEM),
         name="update",
-    )(place, *pieces, current, xt)
+    )(current, *parts, xt)
 
 
 def shift(value, way):
@@ -210,22 +270,31 @@
     steps = jnp.array((0, -1, 1, -2, 2, -3, 3, -4), jnp.int32) * (1 - 2 * core)
     here = ((chip + steps + 8) % CHIPS) * 32 + core * 16
     there = ((chip - steps + 8) % CHIPS) * 32 + (1 - core) * 16
-    place = jnp.concatenate([here, there, core.reshape(1)])
-
-    own = householder.transpose(0, 2, 1).reshape(32, ROWS)
-    pieces = [own]
-    ahead = behind = own
-    for _ in range(3):
+    later_place = jnp.concatenate([here, there, core.reshape(1)])
+    order = jnp.arange(CHIPS, dtype=jnp.int32) * 32
+    earlier_place = jnp.concatenate([order + core * 16, order + (1 - core) * 16, core.reshape(1)])
+
+    own = householder.transpose(0, 2, 1)
+    same_core = [[2 * chip + core for chip in range(CHIPS)] for core in range(2)]
+    mine = lax.all_gather(own[0], "col", axis=0, tiled=True, axis_index_groups=same_core)
+
+    ahead = behind = own[1]
+    groups = [[own[1]]]
+    for step in range(3):
         ahead, behind = shift(ahead, 1), shift(behind, -1)
-        pieces += [ahead, behind]
-    pieces.append(shift(ahead, 1))
+        if step:
+            groups.append([])
+        groups[-1] += [ahead, behind]
+    mine, last, groups[-1][1] = lax.optimization_barrier((mine, shift(ahead, 1), behind))
+    pieces = [jnp.concatenate(group, axis=0) for group in groups] + [last]
     pieces += [swap_cores(piece) for piece in pieces]
-
-    partial = products(place, pieces, eigvecs)
+    later = later_products(later_place, pieces, eigvecs)
+    vhi, vlo, partial = earlier_products(earlier_place, mine, swap_cores(mine), eigvecs, later)
+
     summed = lax.all_to_all(partial, "row", 0, 0, tiled=True).sum(axis=0)
-    mine = lax.all_to_all(jnp.broadcast_to(summed[None], (32, 40, COLS)), "row", 0, 0, tiled=True)
-    other = swap_cores(mine[:, 16:, :])
-    return update(place, pieces, eigvecs, solve(place, mine, other))
+    total = lax.all_to_all(jnp.broadcast_to(summed[None], (32, 40, COLS)), "row", 0, 0, tiled=True)
+    coef = solve(earlier_place, total, swap_cores(total[:, 16:, :]))
+    return update(eigvecs, (vhi, vlo, later[0], later[1]), coef)
 
 
 def solution(mesh):

time: 158 us -> 176 us (1.11)
  between operations: 0.34 us -> 13.7 us
  local copies, waits for them, and re-layouts: 6.4 us -> 13.9 us
  starting transfers between devices: 60 us -> 54.6 us
  waiting for transfers between devices: 14.7 us -> 19 us
    ppermute x9 -> x6, starting transfers between devices: 26.8 us -> 19.7 us  [swap_cores(): return lax.ppermute(value, 'col', [(i, i ^ 1) for i in range(2 * CHIPS)])]
    unnamed x20 -> x34, local copies, waits for them, and re-layouts: 6.33 us -> 10.1 us
    ppermute x7, waiting for transfers between devices: 11.9 us -> 15.2 us  [shift(): return lax.ppermute(value, 'col', perm)]
    pallas_call x1 -> x2, Pallas kernels: 9.09 us -> 11.8 us  [the longest x1 5.95 us: later_products(): pl.pallas_call(later_kernel, grid=(ROWS // STEP,), in_specs=[pl.BlockSpec...]
    pallas_call x1, Pallas kernels: 6.74 us -> 4.2 us  [update(): pl.pallas_call(update_kernel, grid=(ROWS // STEP,), in_specs=[pl.BlockSpe...]
    concatenate x0 -> x2, local copies, waits for them, and re-layouts: none -> 1.94 us  [shards(): pieces = [jnp.concatenate(group, axis=0) for group in groups] + [last]]
    squeeze x0 -> x1, local copies, waits for them, and re-layouts: none -> 1.77 us  [shards(): ahead = behind = own[1]]
  transfers between devices with their start and end apart: 16 -> 14, of which waited for: 4 -> 9; matrix products, arithmetic and copies ran while one was open for 0% -> 3% of each run, Pallas kernels for 0% -> 3%
where the time goes in v3:
time: 176 us; the launch traced here: 175 us
  starting transfers between devices  54.6 us (31%)
  blocking collectives  51.6 us (29%)
  Pallas kernels  21.4 us (12%)
  waiting for transfers between devices  19 us (11%)
  local copies, waits for them, and re-layouts  13.9 us (8%)
  between operations  13.7 us (8%)
    ppermute x7, starting transfers between devices, shift(): return lax.ppermute(value, 'col', perm)  34.9 us
    all_to_all x1, blocking collectives, shards(): summed = lax.all_to_all(partial, 'row', 0, 0, tiled=True).sum(axis=0)  29.1 us
    all_to_all x1, blocking collectives, shards(): lax.all_to_all(jnp.broadcast_to(summed[None], (32, 40, COLS)), 'row', 0,...  22.5 us
    ppermute x6, starting transfers between devices, swap_cores(): return lax.ppermute(value, 'col', [(i, i ^ 1) for i in range(2 * CHIPS)])  19.7 us
    ppermute x7, waiting for transfers between devices, shift(): return lax.ppermute(value, 'col', perm)  15.2 us
    unnamed x34, local copies, waits for them, and re-layouts  10.1 us
    pallas_call x1, Pallas kernels, later_products(): pl.pallas_call(later_kernel, grid=(ROWS // STEP,), in_specs=[pl.BlockSpec...  5.95 us
    pallas_call x1, Pallas kernels, earlier_products(): pl.pallas_call(earlier_kernel, grid=(ROWS // STEP,), in_specs=[pl.BlockSp...  5.86 us
  transfers between devices with their start and end apart: 14, of which 9 were waited for; matrix products, arithmetic and copies ran while one was open for 3% of the time, Pallas kernels for 3%

profile of v3, /device:TPU:1, one launch (start us, length us, event | category | flops | bytes accessed | tf_op | source)
XLA Modules:
  0.0 175.4 jit_solution(4856107268077008488)
XLA Ops:
  6.5 0.0 all-gather.3.cloned.1.call-start
  6.5 1.8 %slice_bitcast_fusion = (f32[16,4096]{1,0:T(8,128)S(1)}, f32[1,16,4096]{2,1,0:T(8,128)}) fusion(f32[2,16,4096]{2,1,0:T(8,128)} %bitcast.7), kind=kLoop, calls=%fused_computation.1 | loop fusion | bytes 1048576 | tf_op jit(solution)/shard_map/squeeze | solution.py:281
  8.3 0.0 all-gather.3.cloned.1.call-update
  8.3 11.6 %collective-permute-start = (f32[16,4096]{1,0:T(8,128)S(1)}, f32[16,4096]{1,0:T(8,128)S(1)}, u32[]{:S(2)}, u32[]{:S(2)}) collective-permute-start(f32[16,4096]{1,0:T(8,128)S(1)} %get-tuple-element.25), channel_id=1, source_target_pairs={{0,2},{1,15},{2,4},{3,1},{4,6},{5,3},{6,8},{7,5},{8,10},{9,7},{10,... | collective-permute-start | bytes 786440 | tf_op jit(solution)/shard_map/ppermute | solution.py:260
  20.0 1.9 %collective-permute-start.4 = (f32[16,4096]{1,0:T(8,128)S(1)}, f32[16,4096]{1,0:T(8,128)}, u32[]{:S(2)}, u32[]{:S(2)}) collective-permute-start(f32[16,4096]{1,0:T(8,128)S(1)} %get-tuple-element.25), channel_id=1, source_target_pairs={{0,14},{1,3},{2,0},{3,5},{4,2},{5,7},{6,4},{7,9},{8,6},{9,11},{10,... | collective-permute-start | bytes 786440 | tf_op jit(solution)/shard_map/ppermute | solution.py:260
  21.9 1.4 collective-permute-done
  23.3 5.0 %collective-permute-start.1 = (f32[16,4096]{1,0:T(8,128)S(1)}, f32[16,4096]{1,0:T(8,128)S(1)}, u32[]{:S(2)}, u32[]{:S(2)}) collective-permute-start(f32[16,4096]{1,0:T(8,128)S(1)} %collective-permute-done), channel_id=1, source_target_pairs={{0,2},{1,15},{2,4},{3,1},{4,6},{5,3},{6,8},{7,5},{8,10},{9,7},{10,... | collective-permute-start | bytes 786440 | tf_op jit(solution)/shard_map/ppermute | solution.py:260
  28.3 0.1 collective-permute-done.4
  28.4 1.9 %collective-permute-start.5 = (f32[16,4096]{1,0:T(8,128)}, f32[16,4096]{1,0:T(8,128)S(1)}, u32[]{:S(2)}, u32[]{:S(2)}) collective-permute-start(f32[16,4096]{1,0:T(8,128)} %collective-permute-done.4), channel_id=1, source_target_pairs={{0,14},{1,3},{2,0},{3,5},{4,2},{5,7},{6,4},{7,9},{8,6},{9,11},{10,... | collective-permute-start | bytes 786440 | tf_op jit(solution)/shard_map/ppermute | solution.py:260
  30.3 4.6 %collective-permute-done.1 = f32[16,4096]{1,0:T(8,128)S(1)} collective-permute-done((f32[16,4096]{1,0:T(8,128)S(1)}, f32[16,4096]{1,0:T(8,128)S(1)}, u32[]{:S(2)}, u32[]{:S(2)}) %collective-permute-start.1) | collective-permute-done | bytes 262176 | tf_op jit(solution)/shard_map/ppermute | solution.py:260
  35.0 0.0 copy-done.14
  35.0 5.3 %collective-permute-start.2 = (f32[16,4096]{1,0:T(8,128)S(1)}, f32[16,4096]{1,0:T(8,128)S(1)}, u32[]{:S(2)}, u32[]{:S(2)}) collective-permute-start(f32[16,4096]{1,0:T(8,128)S(1)} %collective-permute-done.1), channel_id=1, source_target_pairs={{0,2},{1,15},{2,4},{3,1},{4,6},{5,3},{6,8},{7,5},{8,10},{9,7},{10,... | collective-permute-start | bytes 786440 | tf_op jit(solution)/shard_map/ppermute | solution.py:260
  40.3 1.1 pad_maximum_fusion.refs_0_
  41.4 2.5 %collective-permute-start.8 = (f32[48,4096]{1,0:T(8,128)S(1)}, f32[48,4096]{1,0:T(8,128)}, u32[]{:S(2)}, u32[]{:S(2)}) collective-permute-start(f32[48,4096]{1,0:T(8,128)S(1)} %pad_maximum_fusion.refs_0_), channel_id=1, source_target_pairs={{0,1},{1,0},{2,3},{3,2},{4,5},{5,4},{6,7},{7,6},{8,9},{9,8},{10,11... | collective-permute-start | bytes 2359304 | tf_op jit(solution)/shard_map/ppermute | solution.py:264
  43.9 0.0 collective-permute-done.5
  43.9 0.0 copy-start.11
  43.9 3.7 %collective-permute-start.6 = (f32[16,4096]{1,0:T(8,128)S(1)}, f32[16,4096]{1,0:T(8,128)S(1)}, u32[]{:S(2)}, u32[]{:S(2)}) collective-permute-start(f32[16,4096]{1,0:T(8,128)S(1)} %collective-permute-done.5), channel_id=1, source_target_pairs={{0,14},{1,3},{2,0},{3,5},{4,2},{5,7},{6,4},{7,9},{8,6},{9,11},{10,... | collective-permute-start | bytes 786440 | tf_op jit(solution)/shard_map/ppermute | solution.py:260
  47.6 0.7 collective-permute-done.2
  48.4 0.0 copy-done.10
  48.4 5.4 %collective-permute-start.3 = (f32[16,4096]{1,0:T(8,128)S(1)}, f32[16,4096]{1,0:T(8,128)}, u32[]{:S(2)}, u32[]{:S(2)}) collective-permute-start(f32[16,4096]{1,0:T(8,128)S(1)} %collective-permute-done.2), channel_id=1, source_target_pairs={{0,2},{1,15},{2,4},{3,1},{4,6},{5,3},{6,8},{7,5},{8,10},{9,7},{10,... | collective-permute-start | bytes 786440 | tf_op jit(solution)/shard_map/ppermute | solution.py:260
  53.8 0.0 copy-done.11
  53.8 1.0 constant_dynamic-update-slice_fusion.1
  54.8 6.9 %collective-permute-done.6 = f32[16,4096]{1,0:T(8,128)S(1)} collective-permute-done((f32[16,4096]{1,0:T(8,128)S(1)}, f32[16,4096]{1,0:T(8,128)S(1)}, u32[]{:S(2)}, u32[]{:S(2)}) %collective-permute-start.6) | collective-permute-done | bytes 262176 | tf_op jit(solution)/shard_map/ppermute | solution.py:260
  61.7 0.0 copy-done.12
  61.7 0.7 copy-done.13
  62.4 1.5 collective-permute-done.3.refs_3_
  63.9 0.9 all-gather.3.cloned.1.call-done
  64.7 4.9 %collective-permute-start.7 = (f32[128,4096]{1,0:T(8,128)}, f32[128,4096]{1,0:T(8,128)S(1)}, u32[]{:S(2)}, u32[]{:S(2)}) collective-permute-start(f32[128,4096]{1,0:T(8,128)} %bitcast.5), channel_id=1, source_target_pairs={{0,1},{1,0},{2,3},{3,2},{4,5},{5,4},{6,7},{7,6},{8,9},{9,8},{10,11... | collective-permute-start | bytes 6291464 | tf_op jit(solution)/shard_map/ppermute | solution.py:264
  69.6 1.0 constant_dynamic-update-slice_fusion.refs_1_
  70.6 1.9 %collective-permute-start.9 = (f32[32,4096]{1,0:T(8,128)S(1)}, f32[32,4096]{1,0:T(8,128)S(1)}, u32[]{:S(2)}, u32[]{:S(2)}) collective-permute-start(f32[32,4096]{1,0:T(8,128)S(1)} %constant_dynamic-update-slice_fusion.refs_1_), channel_id=1, source_target_pairs={{0,1},{1,0},{2,3},{3,2},{4,5},{5,4},{6,7},{7,6},{8,9},{9,8},{10,11... | collective-permute-start | bytes 1572872 | tf_op jit(solution)/shard_map/ppermute | solution.py:264
  72.5 1.0 constant_dynamic-update-slice_fusion.3
  73.5 1.0 constant_dynamic-update-slice_fusion.2.refs_2_
  74.4 2.4 %collective-permute-start.10 = (f32[32,4096]{1,0:T(8,128)S(1)}, f32[32,4096]{1,0:T(8,128)S(1)}, u32[]{:S(2)}, u32[]{:S(2)}) collective-permute-start(f32[32,4096]{1,0:T(8,128)S(1)} %constant_dynamic-update-slice_fusion.2.refs_2_), channel_id=1, source_target_pairs={{0,1},{1,0},{2,3},{3,2},{4,5},{5,4},{6,7},{7,6},{8,9},{9,8},{10,11... | collective-permute-start | bytes 1572872 | tf_op jit(solution)/shard_map/ppermute | solution.py:264
  76.9 0.0 copy-done.15
  76.9 1.9 %collective-permute-start.11 = (f32[16,4096]{1,0:T(8,128)}, f32[16,4096]{1,0:T(8,128)S(1)}, u32[]{:S(2)}, u32[]{:S(2)}) collective-permute-start(f32[16,4096]{1,0:T(8,128)} %collective-permute-done.3.refs_3_), channel_id=1, source_target_pairs={{0,1},{1,0},{2,3},{3,2},{4,5},{5,4},{6,7},{7,6},{8,9},{9,8},{10,11... | collective-permute-start | bytes 786440 | tf_op jit(solution)/shard_map/ppermute | solution.py:264
  78.8 0.1 add_add_fusion.1.place
  78.9 0.1 add_add_fusion.place
  79.0 0.0 collective-permute-done.9.refs_5_
  79.0 0.0 collective-permute-done.8.refs_4_
  79.0 1.5 collective-permute-done.11.refs_7_
  80.5 0.0 collective-permute-done.10.refs_6_
  80.5 0.0 copy-done
  80.5 6.0 %later_products.1 = (bf16[256,4096]{1,0:T(8,128)(2,1)S(1)}, bf16[256,4096]{1,0:T(8,128)(2,1)S(1)}, f32[256,128]{1,0:T(8,128)S(1)}, f32[384,128]{1,0:T(8,128)S(1)}) custom-call(s32[17]{0:T(128)S(1)} %add_add_fusion.1.place, f32[48,4096]{1,0:T(8,128)S(1)} %pad_maximum_fusion.refs_0_, f32[32,4096]{1,0:T(8,128)S(1)} %constant_dynamic-update-slice_fusion.refs_1_, ...), custom_call_target="tpu_custom_call" | custom-call | flops 4000000000 | bytes 10485760 | tf_op jit(solution)/shard_map/later_products/pallas_call | solution.py:99
  86.5 0.0 copy-start.1
  86.5 0.0 collective-permute-done.7.other
  86.5 0.0 copy-done.9
  86.5 5.9 %earlier_products.1 = (bf16[256,4096]{1,0:T(8,128)(2,1)S(1)}, bf16[256,4096]{1,0:T(8,128)(2,1)S(1)}, f32[32,40,128]{2,1,0:T(8,128)S(1)}) custom-call(s32[17]{0:T(128)S(1)} %add_add_fusion.place, f32[128,4096]{1,0:T(8,128)S(1)} %bitcast.6, f32[128,4096]{1,0:T(8,128)S(1)} %collective-permute-done.7.other, f32[4096,128]{1,0:T(8,128)S(1)} %copy-done, ...), custom_call_target="tpu_custom_call" | custom-call | flops 4000000000 | bytes 14680064 | tf_op jit(solution)/shard_map/earlier_products/pallas_call | solution.py:158
  92.4 0.0 copy-done.1
  92.4 0.0 copy-done.3
  92.4 0.0 copy-start.5
  92.4 1.3 copy-done.5
  93.7 1.3 copy-done.7
  95.1 29.1 %all_to_all.10 = f32[32,40,128]{2,1,0:T(8,128)S(1)} all-to-all(f32[32,40,128]{2,1,0:T(8,128)S(1)} %get-tuple-element.24), channel_id=1, replica_groups=mesh['row'=32,'col'=16] {'row'}, dimensions={0} | all-to-all | bytes 1310720 | tf_op jit(solution)/shard_map/all_to_all | solution.py:294
  124.2 0.1 reduce_sum.9
  124.3 22.5 %all_to_all.11.mine = f32[32,40,128]{2,1,0:T(8,128)S(1)} all-to-all(f32[32,40,128]{2,1,0:T(8,128)S(1)} %broadcast_in_dim.2), channel_id=1, replica_groups=mesh['row'=32,'col'=16] {'row'}, dimensions={0} | all-to-all | bytes 1310720 | tf_op jit(solution)/shard_map/all_to_all | solution.py:295
  146.8 6.0 %collective-permute-start.12 = (f32[32,24,128]{2,1,0:T(8,128)S(1)}, f32[32,24,128]{2,1,0:T(8,128)S(1)}, u32[]{:S(2)}, u32[]{:S(2)}) collective-permute-start(f32[32,24,128]{2,1,0:T(8,128)S(1)} %slice.15), channel_id=1, source_target_pairs={{0,1},{1,0},{2,3},{3,2},{4,5},{5,4},{6,7},{7,6},{8,9},{9,8},{10,11... | collective-permute-start | bytes 1179656 | tf_op jit(solution)/shard_map/ppermute | solution.py:264
  152.9 1.3 collective-permute-done.12.other
  154.2 5.4 %solve.1.xt = bf16[256,512]{1,0:T(8,128)(2,1)S(1)} custom-call(s32[17]{0:T(128)S(1)} %add_add_fusion.place, f32[32,40,128]{2,1,0:T(8,128)S(1)} %all_to_all.11.mine, f32[32,24,128]{2,1,0:T(8,128)S(1)} %collective-permute-done.12.other), custom_call_target="tpu_custom_call" | custom-call | tf_op jit(solution)/shard_map/solve/pallas_call | solution.py:225
  159.6 0.0 copy-done.2
  159.6 0.0 copy-start.4
  159.6 1.6 copy-done.4
  161.2 1.6 copy-done.6
  162.8 1.6 copy-done.8
  164.3 4.2 %update.1 = f32[4096,128]{1,0:T(8,128)} custom-call(f32[4096,128]{1,0:T(8,128)S(1)} %copy-done, bf16[256,4096]{1,0:T(8,128)(2,1)S(1)} %copy-done.6, bf16[256,4096]{1,0:T(8,128)(2,1)S(1)} %copy-done.8, bf16[256,4096]{1,0:T(8,128)(2,1)S(1)} %copy-done.2, bf16[256,4096]{1,0:T(8,128)(2,1)S(1)} %copy-done.4, bf16[256,512]{1,0:T(8,128)(2,1)S(1)} %solve.1.xt), custom_call_target="tpu_custom_call" | custom-call | tf_op jit(solution)/shard_map/update/pallas_call | solution.py:243
  (16 shorter events, 0.1 us)
Async XLA Ops:
  6.5 58.2 %all-gather.3.cloned.1.call-start = ((), (), s32[]{:S(2)}) async-start(), calls=%async_computation.2 | async-start | bytes 2359296 | tf_op jit(solution)/shard_map/all_gather | solution.py:279
  8.3 68.5 %copy-start.15 = (s32[8]{0:T(128)S(1)}, s32[8]{0:T(128)}, u32[]{:S(2)}) copy-start(s32[8]{0:T(128)} %constant.57.clone) | copy-start | bytes 100
  8.3 72.2 %copy-start = (f32[4096,128]{1,0:T(8,128)S(1)}, f32[4096,128]{1,0:T(8,128)}, u32[]{:S(2)}) copy-start(f32[4096,128]{1,0:T(8,128)} %c_ref.3) | copy-start | bytes 6291460
  8.3 14.9 %collective-permute-start = (f32[16,4096]{1,0:T(8,128)S(1)}, f32[16,4096]{1,0:T(8,128)S(1)}, u32[]{:S(2)}, u32[]{:S(2)}) collective-permute-start(f32[16,4096]{1,0:T(8,128)S(1)} %get-tuple-element.25), channel_id=1, source_target_pairs={{0,2},{1,15},{2,4},{3,1},{4,6},{5,3},{6,8},{7,5},{8,10},{9,7},{10,... | collective-permute-start | bytes 786440 | tf_op jit(solution)/shard_map/ppermute | solution.py:260
  20.0 8.4 %collective-permute-start.4 = (f32[16,4096]{1,0:T(8,128)S(1)}, f32[16,4096]{1,0:T(8,128)}, u32[]{:S(2)}, u32[]{:S(2)}) collective-permute-start(f32[16,4096]{1,0:T(8,128)S(1)} %get-tuple-element.25), channel_id=1, source_target_pairs={{0,14},{1,3},{2,0},{3,5},{4,2},{5,7},{6,4},{7,9},{8,6},{9,11},{10,... | collective-permute-start | bytes 786440 | tf_op jit(solution)/shard_map/ppermute | solution.py:260
  23.3 11.7 %copy-start.14 = (f32[16,4096]{1,0:T(8,128)}, f32[16,4096]{1,0:T(8,128)S(1)}, u32[]{:S(2)}) copy-start(f32[16,4096]{1,0:T(8,128)S(1)} %collective-permute-done) | copy-start | bytes 786436
  23.3 11.7 %collective-permute-start.1 = (f32[16,4096]{1,0:T(8,128)S(1)}, f32[16,4096]{1,0:T(8,128)S(1)}, u32[]{:S(2)}, u32[]{:S(2)}) collective-permute-start(f32[16,4096]{1,0:T(8,128)S(1)} %collective-permute-done), channel_id=1, source_target_pairs={{0,2},{1,15},{2,4},{3,1},{4,6},{5,3},{6,8},{7,5},{8,10},{9,7},{10,... | collective-permute-start | bytes 786440 | tf_op jit(solution)/shard_map/ppermute | solution.py:260
  28.4 15.5 %collective-permute-start.5 = (f32[16,4096]{1,0:T(8,128)}, f32[16,4096]{1,0:T(8,128)S(1)}, u32[]{:S(2)}, u32[]{:S(2)}) collective-permute-start(f32[16,4096]{1,0:T(8,128)} %collective-permute-done.4), channel_id=1, source_target_pairs={{0,14},{1,3},{2,0},{3,5},{4,2},{5,7},{6,4},{7,9},{8,6},{9,11},{10,... | collective-permute-start | bytes 786440 | tf_op jit(solution)/shard_map/ppermute | solution.py:260
  35.0 13.4 %copy-start.10 = (f32[16,4096]{1,0:T(8,128)}, f32[16,4096]{1,0:T(8,128)S(1)}, u32[]{:S(2)}) copy-start(f32[16,4096]{1,0:T(8,128)S(1)} %collective-permute-done.1) | copy-start | bytes 786436
  35.0 13.4 %collective-permute-start.2 = (f32[16,4096]{1,0:T(8,128)S(1)}, f32[16,4096]{1,0:T(8,128)S(1)}, u32[]{:S(2)}, u32[]{:S(2)}) collective-permute-start(f32[16,4096]{1,0:T(8,128)S(1)} %collective-permute-done.1), channel_id=1, source_target_pairs={{0,2},{1,15},{2,4},{3,1},{4,6},{5,3},{6,8},{7,5},{8,10},{9,7},{10,... | collective-permute-start | bytes 786440 | tf_op jit(solution)/shard_map/ppermute | solution.py:260
  41.4 37.6 %collective-permute-start.8 = (f32[48,4096]{1,0:T(8,128)S(1)}, f32[48,4096]{1,0:T(8,128)}, u32[]{:S(2)}, u32[]{:S(2)}) collective-permute-start(f32[48,4096]{1,0:T(8,128)S(1)} %pad_maximum_fusion.refs_0_), channel_id=1, source_target_pairs={{0,1},{1,0},{2,3},{3,2},{4,5},{5,4},{6,7},{7,6},{8,9},{9,8},{10,11... | collective-permute-start | bytes 2359304 | tf_op jit(solution)/shard_map/ppermute | solution.py:264
  43.9 9.9 %copy-start.11 = (f32[16,4096]{1,0:T(8,128)}, f32[16,4096]{1,0:T(8,128)S(1)}, u32[]{:S(2)}) copy-start(f32[16,4096]{1,0:T(8,128)S(1)} %collective-permute-done.5) | copy-start | bytes 786436
  43.9 17.7 %collective-permute-start.6 = (f32[16,4096]{1,0:T(8,128)S(1)}, f32[16,4096]{1,0:T(8,128)S(1)}, u32[]{:S(2)}, u32[]{:S(2)}) collective-permute-start(f32[16,4096]{1,0:T(8,128)S(1)} %collective-permute-done.5), channel_id=1, source_target_pairs={{0,14},{1,3},{2,0},{3,5},{4,2},{5,7},{6,4},{7,9},{8,6},{9,11},{10,... | collective-permute-start | bytes 786440 | tf_op jit(solution)/shard_map/ppermute | solution.py:260
  48.4 13.3 %copy-start.12 = (f32[16,4096]{1,0:T(8,128)}, f32[16,4096]{1,0:T(8,128)S(1)}, u32[]{:S(2)}) copy-start(f32[16,4096]{1,0:T(8,128)S(1)} %collective-permute-done.2) | copy-start | bytes 786436
  48.4 15.5 %collective-permute-start.3 = (f32[16,4096]{1,0:T(8,128)S(1)}, f32[16,4096]{1,0:T(8,128)}, u32[]{:S(2)}, u32[]{:S(2)}) collective-permute-start(f32[16,4096]{1,0:T(8,128)S(1)} %collective-permute-done.2), channel_id=1, source_target_pairs={{0,2},{1,15},{2,4},{3,1},{4,6},{5,3},{6,8},{7,5},{8,10},{9,7},{10,... | collective-permute-start | bytes 786440 | tf_op jit(solution)/shard_map/ppermute | solution.py:260
  61.7 0.7 copy-start.13
  64.7 21.8 %collective-permute-start.7 = (f32[128,4096]{1,0:T(8,128)}, f32[128,4096]{1,0:T(8,128)S(1)}, u32[]{:S(2)}, u32[]{:S(2)}) collective-permute-start(f32[128,4096]{1,0:T(8,128)} %bitcast.5), channel_id=1, source_target_pairs={{0,1},{1,0},{2,3},{3,2},{4,5},{5,4},{6,7},{7,6},{8,9},{9,8},{10,11... | collective-permute-start | bytes 6291464 | tf_op jit(solution)/shard_map/ppermute | solution.py:264
  70.6 8.4 %collective-permute-start.9 = (f32[32,4096]{1,0:T(8,128)S(1)}, f32[32,4096]{1,0:T(8,128)S(1)}, u32[]{:S(2)}, u32[]{:S(2)}) collective-permute-start(f32[32,4096]{1,0:T(8,128)S(1)} %constant_dynamic-update-slice_fusion.refs_1_), channel_id=1, source_target_pairs={{0,1},{1,0},{2,3},{3,2},{4,5},{5,4},{6,7},{7,6},{8,9},{9,8},{10,11... | collective-permute-start | bytes 1572872 | tf_op jit(solution)/shard_map/ppermute | solution.py:264
  74.4 6.1 %collective-permute-start.10 = (f32[32,4096]{1,0:T(8,128)S(1)}, f32[32,4096]{1,0:T(8,128)S(1)}, u32[]{:S(2)}, u32[]{:S(2)}) collective-permute-start(f32[32,4096]{1,0:T(8,128)S(1)} %constant_dynamic-update-slice_fusion.2.refs_2_), channel_id=1, source_target_pairs={{0,1},{1,0},{2,3},{3,2},{4,5},{5,4},{6,7},{7,6},{8,9},{9,8},{10,11... | collective-permute-start | bytes 1572872 | tf_op jit(solution)/shard_map/ppermute | solution.py:264
  76.9 3.6 %collective-permute-start.11 = (f32[16,4096]{1,0:T(8,128)}, f32[16,4096]{1,0:T(8,128)S(1)}, u32[]{:S(2)}, u32[]{:S(2)}) collective-permute-start(f32[16,4096]{1,0:T(8,128)} %collective-permute-done.3.refs_3_), channel_id=1, source_target_pairs={{0,1},{1,0},{2,3},{3,2},{4,5},{5,4},{6,7},{7,6},{8,9},{9,8},{10,11... | collective-permute-start | bytes 786440 | tf_op jit(solution)/shard_map/ppermute | solution.py:264
  79.0 7.5 %copy-start.9 = (f32[1,128,4096]{2,1,0:T(8,128)S(1)}, f32[1,128,4096]{2,1,0:T(8,128)}, u32[]{:S(2)}) copy-start(f32[1,128,4096]{2,1,0:T(8,128)} %all-gather.3.cloned.1.call-done) | copy-start | bytes 6291460
  86.5 5.9 %copy-start.1 = (bf16[256,4096]{1,0:T(8,128)(2,1)}, bf16[256,4096]{1,0:T(8,128)(2,1)S(1)}, u32[]{:S(2)}) copy-start(bf16[256,4096]{1,0:T(8,128)(2,1)S(1)} %get-tuple-element.18.whi) | copy-start | bytes 6291460
  86.5 5.9 %copy-start.3 = (bf16[256,4096]{1,0:T(8,128)(2,1)}, bf16[256,4096]{1,0:T(8,128)(2,1)S(1)}, u32[]{:S(2)}) copy-start(bf16[256,4096]{1,0:T(8,128)(2,1)S(1)} %get-tuple-element.19.wlo) | copy-start | bytes 6291460
  92.4 1.3 copy-start.5
  93.7 1.4 copy-start.7
  124.2 35.3 %copy-start.2 = (bf16[256,4096]{1,0:T(8,128)(2,1)S(1)}, bf16[256,4096]{1,0:T(8,128)(2,1)}, u32[]{:S(2)}) copy-start(bf16[256,4096]{1,0:T(8,128)(2,1)} %copy-done.1) | copy-start | bytes 6291460
  146.8 7.4 %collective-permute-start.12 = (f32[32,24,128]{2,1,0:T(8,128)S(1)}, f32[32,24,128]{2,1,0:T(8,128)S(1)}, u32[]{:S(2)}, u32[]{:S(2)}) collective-permute-start(f32[32,24,128]{2,1,0:T(8,128)S(1)} %slice.15), channel_id=1, source_target_pairs={{0,1},{1,0},{2,3},{3,2},{4,5},{5,4},{6,7},{7,6},{8,9},{9,8},{10,11... | collective-permute-start | bytes 1179656 | tf_op jit(solution)/shard_map/ppermute | solution.py:264
  159.6 1.6 copy-start.4
  161.2 1.6 copy-start.6
  162.8 1.6 copy-start.8
Sparse Core Ops, SparseCore 0:
  9.4 55.2 all-gather.2

commit v4 on v2

--- a/solution.py
+++ b/solution.py
@@ -13,6 +13,8 @@
 NV = 512
 STEP = 1024
 VMEM = 24 * 1024 * 1024
+MOST_VMEM = 56 * 1024 * 1024
+ARRIVAL = ((0, 1), (-1, -2), (2, 3), (-3, -4))
 GRAM_BLOCKS = (
     ((0, 2), (0, 3), (1, 2), (1, 3)),
     ((0, 0), (0, 1), (1, 1), (2, 2), (2, 3), (3, 3)),
@@ -37,27 +39,41 @@
     return jnp.dot(left, right, precision=lax.Precision.HIGHEST, preferred_element_type=F32)
 
 
-def assemble(place, pieces, vhi, vlo):
+def assemble(me, pieces, vhi, vlo):
+    chip, core = me // 2, me % 2
+    turn = 1 - 2 * ((chip + core) % 2)
     for index, piece in enumerate(pieces):
-        for block in range(2):
-            high, low = split(piece[block * 16 : block * 16 + 16, :])
-            at = pl.ds(pl.multiple_of(place[index] + block * 256, 16), 16)
+        swapped, arrival, block = index // 8, index % 8 // 2, index % 2
+        for half in range(2):
+            step = ARRIVAL[arrival][half] * (1 - 2 * swapped)
+            source = (chip + turn * step + CHIPS) % CHIPS
+            column = block * 256 + source * 32 + (1 - core if swapped else core) * 16
+            high, low = split(piece[half * 16 : half * 16 + 16, :])
+            at = pl.ds(pl.multiple_of(column, 16), 16)
             vhi[at, :] = high
             vlo[at, :] = low
 
 
-def products_kernel(place, *refs):
+def strip(rows):
+    return pl.BlockSpec((rows, STEP), lambda k: (0, k))
+
+
+def whole(*shape):
+    return pl.BlockSpec(shape, lambda k: (0,) * len(shape))
+
+
+def products_kernel(me, *refs):
     pieces = refs[:16]
-    c_ref, out, proj, gram, vhi, vlo = refs[16:]
+    c_ref, vhi, vlo, out, proj, gram = refs[16:]
     step = pl.program_id(0)
-    first_core = place[16] == 0
+    first_core = me[0] % 2 == 0
 
     @pl.when(step == 0)
     def _():
         proj[...] = jnp.zeros_like(proj)
         gram[...] = jnp.zeros_like(gram)
 
-    assemble(place, pieces, vhi, vlo)
+    assemble(me[0], pieces, vhi, vlo)
     chi, clo = split(c_ref[...])
     both = nn(vhi[...], jnp.concatenate([chi, clo], axis=1))
     proj[...] += both[:, :COLS] + both[:, COLS:] + nn(vlo[...], chi)
@@ -96,24 +112,23 @@
             out[:, 16:, :] = jnp.concatenate(parts, axis=0).reshape(32, 24, COLS)
 
 
-def products(place, pieces, current):
+def products(me, pieces, current):
     return pl.pallas_call(
         products_kernel,
         grid=(ROWS // STEP,),
         in_specs=[pl.BlockSpec(memory_space=pltpu.SMEM)]
-        + [pl.BlockSpec((32, STEP), lambda k: (0, k))] * 16
+        + [strip(32)] * 16
         + [pl.BlockSpec((STEP, COLS), lambda k: (k, 0))],
-        out_specs=pl.BlockSpec((32, 40, COLS), lambda k: (0, 0, 0)),
-        out_shape=jax.ShapeDtypeStruct((32, 40, COLS), F32),
-        scratch_shapes=[
-            pltpu.VMEM((NV, COLS), F32),
-            pltpu.VMEM((512, 512), F32),
-            pltpu.VMEM((NV, STEP), BF16),
-            pltpu.VMEM((NV, STEP), BF16),
+        out_specs=[strip(NV), strip(NV), whole(32, 40, COLS)],
+        out_shape=[
+            pltpu.HBM((NV, ROWS), BF16),
+            pltpu.HBM((NV, ROWS), BF16),
+            jax.ShapeDtypeStruct((32, 40, COLS), F32),
         ],
+        scratch_shapes=[pltpu.VMEM((NV, COLS), F32), pltpu.VMEM((512, 512), F32)],
         compiler_params=pltpu.CompilerParams(vmem_limit_bytes=VMEM),
         name="products",
-    )(place, *pieces, current)
+    )(me, *pieces, current)
 
 
 def invert_unit(nilpot):
@@ -132,8 +147,8 @@
     return inverse
 
 
-def solve_kernel(place, mine, other, xt):
-    zero = place[16] == 0
+def solve_kernel(me, mine, other, xt):
+    zero = me[0] % 2 == 0
     gram = {}
     for which in range(2):
         flat = jnp.where(zero == (which == 0), mine[:, 16:, :], other[...]).reshape(768, 128)
@@ -156,46 +171,41 @@
     xt[COLS:, :] = low
 
 
-def solve(place, mine, other):
+def solve(me, mine, other):
     return pl.pallas_call(
         solve_kernel,
         in_specs=[pl.BlockSpec(memory_space=pltpu.SMEM)] + [pl.BlockSpec(memory_space=pltpu.VMEM)] * 2,
         out_specs=pl.BlockSpec(memory_space=pltpu.VMEM),
-        out_shape=jax.ShapeDtypeStruct((2 * COLS, NV), BF16),
+        out_shape=pltpu.HBM((2 * COLS, NV), BF16),
         compiler_params=pltpu.CompilerParams(vmem_limit_bytes=VMEM),
         name="solve",
-    )(place, mine, other)
-
-
-def update_kernel(place, *refs):
-    pieces = refs[:16]
-    c_ref, xt, out, vhi, vlo = refs[16:]
-    assemble(place, pieces, vhi, vlo)
+    )(me, mine, other)
+
+
+def update_kernel(c_ref, vhi, vlo, xt, out):
     both = nn(xt[...], vhi[...])
     change = both[:COLS] + both[COLS:] + nn(xt[:COLS, :], vlo[...])
     out[...] = c_ref[...] - change.T
 
 
-def update(place, pieces, current, xt):
+def update(current, vhi, vlo, xt):
     return pl.pallas_call(
         update_kernel,
         grid=(ROWS // STEP,),
-        in_specs=[pl.BlockSpec(memory_space=pltpu.SMEM)]
-        + [pl.BlockSpec((32, STEP), lambda k: (0, k))] * 16
-        + [pl.BlockSpec((STEP, COLS), lambda k: (k, 0)), pl.BlockSpec((2 * COLS, NV), lambda k: (0, 0))],
+        in_specs=[pl.BlockSpec((STEP, COLS), lambda k: (k, 0)), strip(NV), strip(NV), whole(2 * COLS, NV)],
         out_specs=pl.BlockSpec((STEP, COLS), lambda k: (k, 0)),
         out_shape=jax.ShapeDtypeStruct((ROWS, COLS), F32),
-        scratch_shapes=[pltpu.VMEM((NV, STEP), BF16), pltpu.VMEM((NV, STEP), BF16)],
-        compiler_params=pltpu.CompilerParams(vmem_limit_bytes=VMEM),
+        compiler_params=pltpu.CompilerParams(vmem_limit_bytes=MOST_VMEM),
         name="update",
-    )(place, *pieces, current, xt)
-
-
-def shift(value, way):
+    )(current, vhi, vlo, xt)
+
+
+def exchange(value, side):
     perm = []
     for chip in range(CHIPS):
         for core in range(2):
-            target = (chip + way * (1 - 2 * core)) % CHIPS
+            turn = 1 if (chip + core) % 2 == 0 else -1
+            target = (chip + side * turn) % CHIPS
             perm.append((chip * 2 + core, target * 2 + core))
     return lax.ppermute(value, "col", perm)
 
@@ -205,27 +215,21 @@
 
 
 def shards(eigvecs, householder):
-    me = lax.axis_index("col")
-    chip, core = me // 2, me % 2
-    steps = jnp.array((0, -1, 1, -2, 2, -3, 3, -4), jnp.int32) * (1 - 2 * core)
-    here = ((chip + steps + 8) % CHIPS) * 32 + core * 16
-    there = ((chip - steps + 8) % CHIPS) * 32 + (1 - core) * 16
-    place = jnp.concatenate([here, there, core.reshape(1)])
-
-    own = householder.transpose(0, 2, 1).reshape(32, ROWS)
-    pieces = [own]
-    ahead = behind = own
-    for _ in range(3):
-        ahead, behind = shift(ahead, 1), shift(behind, -1)
-        pieces += [ahead, behind]
-    pieces.append(shift(ahead, 1))
+    me = lax.axis_index("col").reshape(1)
+    own = householder.transpose(0, 2, 1)
+    chains = [own[0], own[1]]
+    chains = [jnp.concatenate([piece, exchange(piece, 1)], axis=0) for piece in chains]
+    pieces = list(chains)
+    for side in (-1, 1, -1):
+        chains = [exchange(piece, side) for piece in chains]
+        pieces += chains
     pieces += [swap_cores(piece) for piece in pieces]
 
-    partial = products(place, pieces, eigvecs)
+    vhi, vlo, partial = products(me, pieces, eigvecs)
     summed = lax.all_to_all(partial, "row", 0, 0, tiled=True).sum(axis=0)
     mine = lax.all_to_all(jnp.broadcast_to(summed[None], (32, 40, COLS)), "row", 0, 0, tiled=True)
     other = swap_cores(mine[:, 16:, :])
-    return update(place, pieces, eigvecs, solve(place, mine, other))
+    return update(eigvecs, vhi, vlo, solve(me, mine, other))
 
 
 def solution(mesh):

time: 158 us -> 156 us (0.987)
  Pallas kernels: 21.2 us -> 23.6 us
  local copies, waits for them, and re-layouts: 6.4 us -> 8.63 us
  waiting for transfers between devices: 14.7 us -> 12.5 us
  other arithmetic: 1.9 us -> 0.12 us
    ppermute x7 -> x8, waiting for transfers between devices: 11.9 us -> 9.3 us  [exchange(): return lax.ppermute(value, 'col', perm)]
    pallas_call x1, Pallas kernels: 9.09 us -> 10.8 us  [products(): pl.pallas_call(products_kernel, grid=(ROWS // STEP,), in_specs=[pl.BlockS...]
    ppermute x7 -> x8, starting transfers between devices: 33.3 us -> 31.9 us  [exchange(): return lax.ppermute(value, 'col', perm)]
    unnamed x20 -> x18, local copies, waits for them, and re-layouts: 6.33 us -> 7.34 us
  transfers between devices with their start and end apart: 16 -> 17, of which waited for: 4 -> 6; matrix products, arithmetic and copies ran while one was open for 0% -> 0% of each run, Pallas kernels for 0% -> 0%
where the time goes in v4:
time: 156 us; the launch traced here: 155 us
  starting transfers between devices  59.3 us (38%)
  blocking collectives  50.9 us (33%)
  Pallas kernels  23.6 us (15%)
  waiting for transfers between devices  12.5 us (8%)
  local copies, waits for them, and re-layouts  8.63 us (6%)
    ppermute x8, starting transfers between devices, exchange(): return lax.ppermute(value, 'col', perm)  31.9 us
    all_to_all x1, blocking collectives, shards(): summed = lax.all_to_all(partial, 'row', 0, 0, tiled=True).sum(axis=0)  27.4 us
    ppermute x9, starting transfers between devices, swap_cores(): return lax.ppermute(value, 'col', [(i, i ^ 1) for i in range(2 * CHIPS)])  27.3 us
    all_to_all x1, blocking collectives, shards(): lax.all_to_all(jnp.broadcast_to(summed[None], (32, 40, COLS)), 'row', 0,...  23.4 us
    pallas_call x1, Pallas kernels, products(): pl.pallas_call(products_kernel, grid=(ROWS // STEP,), in_specs=[pl.BlockS...  10.8 us
    ppermute x8, waiting for transfers between devices, exchange(): return lax.ppermute(value, 'col', perm)  9.3 us
    unnamed x18, local copies, waits for them, and re-layouts  7.34 us
    pallas_call x1, Pallas kernels, update(): pl.pallas_call(update_kernel, grid=(ROWS // STEP,), in_specs=[pl.BlockSpe...  7.23 us
  transfers between devices with their start and end apart: 17, of which 6 were waited for; matrix products, arithmetic and copies ran while one was open for 0% of the time, Pallas kernels for 0%

profile of v4, /device:TPU:1, one launch (start us, length us, event | category | flops | bytes accessed | tf_op | source)
XLA Modules:
  0.0 155.3 jit_solution(17241911752796374383)
XLA Ops:
  0.0 0.0 copy-start
  0.0 1.2 slice_bitcast_fusion
  1.2 11.5 %collective-permute-start = (f32[16,4096]{1,0:T(8,128)S(1)}, f32[16,4096]{1,0:T(8,128)S(1)}, u32[]{:S(2)}, u32[]{:S(2)}) collective-permute-start(f32[16,4096]{1,0:T(8,128)S(1)} %get-tuple-element.12), channel_id=1, source_target_pairs={{0,2},{1,15},{2,0},{3,5},{4,6},{5,3},{6,4},{7,9},{8,10},{9,7},{10,... | collective-permute-start | bytes 786440 | tf_op jit(solution)/shard_map/ppermute | solution.py:210
  12.7 1.9 %collective-permute-start.1 = (f32[16,4096]{1,0:T(8,128)S(1)}, f32[16,4096]{1,0:T(8,128)S(1)}, u32[]{:S(2)}, u32[]{:S(2)}) collective-permute-start(f32[16,4096]{1,0:T(8,128)S(1)} %get-tuple-element.11), channel_id=1, source_target_pairs={{0,2},{1,15},{2,0},{3,5},{4,6},{5,3},{6,4},{7,9},{8,10},{9,7},{10,... | collective-permute-start | bytes 786440 | tf_op jit(solution)/shard_map/ppermute | solution.py:210
  14.7 1.8 %collective-permute-done = f32[16,4096]{1,0:T(8,128)S(1)} collective-permute-done((f32[16,4096]{1,0:T(8,128)S(1)}, f32[16,4096]{1,0:T(8,128)S(1)}, u32[]{:S(2)}, u32[]{:S(2)}) %collective-permute-start) | collective-permute-done | bytes 262176 | tf_op jit(solution)/shard_map/ppermute | solution.py:210
  16.5 1.9 %collective-permute-start.2 = (f32[32,4096]{1,0:T(8,128)S(1)}, f32[32,4096]{1,0:T(8,128)S(1)}, u32[]{:S(2)}, u32[]{:S(2)}) collective-permute-start(f32[32,4096]{1,0:T(8,128)S(1)} %pad_maximum_fusion.refs_0_), channel_id=1, source_target_pairs={{0,14},{1,3},{2,4},{3,1},{4,2},{5,7},{6,8},{7,5},{8,6},{9,11},{10,... | collective-permute-start | bytes 1572872 | tf_op jit(solution)/shard_map/ppermute | solution.py:210
  18.4 2.6 %collective-permute-done.1 = f32[16,4096]{1,0:T(8,128)S(1)} collective-permute-done((f32[16,4096]{1,0:T(8,128)S(1)}, f32[16,4096]{1,0:T(8,128)S(1)}, u32[]{:S(2)}, u32[]{:S(2)}) %collective-permute-start.1) | collective-permute-done | bytes 262176 | tf_op jit(solution)/shard_map/ppermute | solution.py:210
  21.1 1.9 %collective-permute-start.3 = (f32[32,4096]{1,0:T(8,128)S(1)}, f32[32,4096]{1,0:T(8,128)}, u32[]{:S(2)}, u32[]{:S(2)}) collective-permute-start(f32[32,4096]{1,0:T(8,128)S(1)} %pad_maximum_fusion.1.refs_1_), channel_id=1, source_target_pairs={{0,14},{1,3},{2,4},{3,1},{4,2},{5,7},{6,8},{7,5},{8,6},{9,11},{10,... | collective-permute-start | bytes 1572872 | tf_op jit(solution)/shard_map/ppermute | solution.py:210
  23.0 3.7 %collective-permute-done.2.refs_2_ = f32[32,4096]{1,0:T(8,128)S(1)} collective-permute-done((f32[32,4096]{1,0:T(8,128)S(1)}, f32[32,4096]{1,0:T(8,128)S(1)}, u32[]{:S(2)}, u32[]{:S(2)}) %collective-permute-start.2) | collective-permute-done | bytes 524320 | tf_op jit(solution)/shard_map/ppermute | solution.py:210
  26.7 4.6 %collective-permute-start.4 = (f32[32,4096]{1,0:T(8,128)S(1)}, f32[32,4096]{1,0:T(8,128)}, u32[]{:S(2)}, u32[]{:S(2)}) collective-permute-start(f32[32,4096]{1,0:T(8,128)S(1)} %collective-permute-done.2.refs_2_), channel_id=1, source_target_pairs={{0,2},{1,15},{2,0},{3,5},{4,6},{5,3},{6,4},{7,9},{8,10},{9,7},{10,... | collective-permute-start | bytes 1572872 | tf_op jit(solution)/shard_map/ppermute | solution.py:210
  31.3 1.2 collective-permute-done.3.refs_3_
  32.5 4.6 %collective-permute-start.5 = (f32[32,4096]{1,0:T(8,128)}, f32[32,4096]{1,0:T(8,128)}, u32[]{:S(2)}, u32[]{:S(2)}) collective-permute-start(f32[32,4096]{1,0:T(8,128)} %collective-permute-done.3.refs_3_), channel_id=1, source_target_pairs={{0,2},{1,15},{2,0},{3,5},{4,6},{5,3},{6,4},{7,9},{8,10},{9,7},{10,... | collective-permute-start | bytes 1572872 | tf_op jit(solution)/shard_map/ppermute | solution.py:210
  37.0 3.4 %collective-permute-start.8 = (f32[32,4096]{1,0:T(8,128)S(1)}, f32[32,4096]{1,0:T(8,128)S(1)}, u32[]{:S(2)}, u32[]{:S(2)}) collective-permute-start(f32[32,4096]{1,0:T(8,128)S(1)} %pad_maximum_fusion.refs_0_), channel_id=1, source_target_pairs={{0,1},{1,0},{2,3},{3,2},{4,5},{5,4},{6,7},{7,6},{8,9},{9,8},{10,11... | collective-permute-start | bytes 1572872 | tf_op jit(solution)/shard_map/ppermute | solution.py:214
  40.4 1.9 %collective-permute-start.9 = (f32[32,4096]{1,0:T(8,128)S(1)}, f32[32,4096]{1,0:T(8,128)S(1)}, u32[]{:S(2)}, u32[]{:S(2)}) collective-permute-start(f32[32,4096]{1,0:T(8,128)S(1)} %pad_maximum_fusion.1.refs_1_), channel_id=1, source_target_pairs={{0,1},{1,0},{2,3},{3,2},{4,5},{5,4},{6,7},{7,6},{8,9},{9,8},{10,11... | collective-permute-start | bytes 1572872 | tf_op jit(solution)/shard_map/ppermute | solution.py:214
  42.4 2.4 %collective-permute-start.10 = (f32[32,4096]{1,0:T(8,128)S(1)}, f32[32,4096]{1,0:T(8,128)S(1)}, u32[]{:S(2)}, u32[]{:S(2)}) collective-permute-start(f32[32,4096]{1,0:T(8,128)S(1)} %collective-permute-done.2.refs_2_), channel_id=1, source_target_pairs={{0,1},{1,0},{2,3},{3,2},{4,5},{5,4},{6,7},{7,6},{8,9},{9,8},{10,11... | collective-permute-start | bytes 1572872 | tf_op jit(solution)/shard_map/ppermute | solution.py:214
  44.8 0.0 copy-start.1
  44.8 0.8 copy-done.1
  45.6 0.0 collective-permute-done.4.refs_4_
  45.6 3.6 %collective-permute-start.6 = (f32[32,4096]{1,0:T(8,128)}, f32[32,4096]{1,0:T(8,128)}, u32[]{:S(2)}, u32[]{:S(2)}) collective-permute-start(f32[32,4096]{1,0:T(8,128)} %collective-permute-done.4.refs_4_), channel_id=1, source_target_pairs={{0,14},{1,3},{2,4},{3,1},{4,2},{5,7},{6,8},{7,5},{8,6},{9,11},{10,... | collective-permute-start | bytes 1572872 | tf_op jit(solution)/shard_map/ppermute | solution.py:210
  49.2 0.0 collective-permute-done.5.refs_5_
  49.2 1.9 %collective-permute-start.7 = (f32[32,4096]{1,0:T(8,128)}, f32[32,4096]{1,0:T(8,128)}, u32[]{:S(2)}, u32[]{:S(2)}) collective-permute-start(f32[32,4096]{1,0:T(8,128)} %collective-permute-done.5.refs_5_), channel_id=1, source_target_pairs={{0,14},{1,3},{2,4},{3,1},{4,2},{5,7},{6,8},{7,5},{8,6},{9,11},{10,... | collective-permute-start | bytes 1572872 | tf_op jit(solution)/shard_map/ppermute | solution.py:210
  51.2 0.0 collective-permute-done.8.refs_8_
  51.2 0.0 copy-start.3
  51.2 0.8 copy-done.3
  52.0 4.1 %collective-permute-start.11 = (f32[32,4096]{1,0:T(8,128)}, f32[32,4096]{1,0:T(8,128)}, u32[]{:S(2)}, u32[]{:S(2)}) collective-permute-start(f32[32,4096]{1,0:T(8,128)} %collective-permute-done.3.refs_3_), channel_id=1, source_target_pairs={{0,1},{1,0},{2,3},{3,2},{4,5},{5,4},{6,7},{7,6},{8,9},{9,8},{10,11... | collective-permute-start | bytes 1572872 | tf_op jit(solution)/shard_map/ppermute | solution.py:214
  56.1 0.0 collective-permute-done.9.refs_9_
  56.1 0.0 copy-start.5
  56.1 0.8 copy-done.5
  56.9 1.9 %collective-permute-start.12 = (f32[32,4096]{1,0:T(8,128)}, f32[32,4096]{1,0:T(8,128)}, u32[]{:S(2)}, u32[]{:S(2)}) collective-permute-start(f32[32,4096]{1,0:T(8,128)} %collective-permute-done.4.refs_4_), channel_id=1, source_target_pairs={{0,1},{1,0},{2,3},{3,2},{4,5},{5,4},{6,7},{7,6},{8,9},{9,8},{10,11... | collective-permute-start | bytes 1572872 | tf_op jit(solution)/shard_map/ppermute | solution.py:214
  58.8 0.0 collective-permute-done.10.refs_10_
  58.9 0.0 copy-start.7
  58.9 0.8 copy-done.7
  59.7 2.4 %collective-permute-start.13 = (f32[32,4096]{1,0:T(8,128)}, f32[32,4096]{1,0:T(8,128)}, u32[]{:S(2)}, u32[]{:S(2)}) collective-permute-start(f32[32,4096]{1,0:T(8,128)} %collective-permute-done.5.refs_5_), channel_id=1, source_target_pairs={{0,1},{1,0},{2,3},{3,2},{4,5},{5,4},{6,7},{7,6},{8,9},{9,8},{10,11... | collective-permute-start | bytes 1572872 | tf_op jit(solution)/shard_map/ppermute | solution.py:214
  62.1 0.0 collective-permute-done.6.refs_6_
  62.1 1.9 %collective-permute-start.14 = (f32[32,4096]{1,0:T(8,128)}, f32[32,4096]{1,0:T(8,128)}, u32[]{:S(2)}, u32[]{:S(2)}) collective-permute-start(f32[32,4096]{1,0:T(8,128)} %collective-permute-done.6.refs_6_), channel_id=1, source_target_pairs={{0,1},{1,0},{2,3},{3,2},{4,5},{5,4},{6,7},{7,6},{8,9},{9,8},{10,11... | collective-permute-start | bytes 1572872 | tf_op jit(solution)/shard_map/ppermute | solution.py:214
  64.0 0.0 collective-permute-done.7.refs_7_
  64.0 2.4 %collective-permute-start.15 = (f32[32,4096]{1,0:T(8,128)}, f32[32,4096]{1,0:T(8,128)}, u32[]{:S(2)}, u32[]{:S(2)}) collective-permute-start(f32[32,4096]{1,0:T(8,128)} %collective-permute-done.7.refs_7_), channel_id=1, source_target_pairs={{0,1},{1,0},{2,3},{3,2},{4,5},{5,4},{6,7},{7,6},{8,9},{9,8},{10,11... | collective-permute-start | bytes 1572872 | tf_op jit(solution)/shard_map/ppermute | solution.py:214
  66.4 0.0 collective-permute-done.11.refs_11_
  66.4 0.0 collective-permute-done.12.refs_12_
  66.5 0.0 collective-permute-done.13.refs_13_
  66.5 0.0 collective-permute-done.14.refs_14_
  66.5 1.8 %collective-permute-done.15.refs_15_ = f32[32,4096]{1,0:T(8,128)} collective-permute-done((f32[32,4096]{1,0:T(8,128)}, f32[32,4096]{1,0:T(8,128)}, u32[]{:S(2)}, u32[]{:S(2)}) %collective-permute-start.15) | collective-permute-done | bytes 524320 | tf_op jit(solution)/shard_map/ppermute | solution.py:214
  68.3 0.0 copy-done
  68.3 0.0 copy-start.2
  68.3 1.0 copy-done.2
  69.3 0.0 copy-start.4
  69.3 1.0 copy-done.4
  70.4 0.0 copy-start.6
  70.4 1.0 copy-done.6
  71.4 0.0 copy-start.8
  71.4 1.0 copy-done.8
  72.5 10.8 %products.1 = (bf16[512,4096]{1,0:T(8,128)(2,1)}, bf16[512,4096]{1,0:T(8,128)(2,1)}, f32[32,40,128]{2,1,0:T(8,128)S(1)}) custom-call(s32[1]{0:T(128)} %bitcast.me, f32[32,4096]{1,0:T(8,128)S(1)} %pad_maximum_fusion.refs_0_, f32[32,4096]{1,0:T(8,128)S(1)} %pad_maximum_fusion.1.refs_1_, f32[32,4096]{1,0:T(8,128)S(1)} %copy-done.2, ...), custom_call_target="tpu_custom_call" | custom-call | tf_op jit(solution)/shard_map/products/pallas_call | solution.py:116
  83.3 27.4 %all_to_all.10 = f32[32,40,128]{2,1,0:T(8,128)S(1)} all-to-all(f32[32,40,128]{2,1,0:T(8,128)S(1)} %get-tuple-element.10), channel_id=1, replica_groups=mesh['row'=32,'col'=16] {'row'}, dimensions={0} | all-to-all | bytes 1310720 | tf_op jit(solution)/shard_map/all_to_all | solution.py:229
  110.7 0.1 reduce_sum.9
  110.8 23.4 %all_to_all.11.mine = f32[32,40,128]{2,1,0:T(8,128)S(1)} all-to-all(f32[32,40,128]{2,1,0:T(8,128)S(1)} %broadcast_in_dim.2), channel_id=1, replica_groups=mesh['row'=32,'col'=16] {'row'}, dimensions={0} | all-to-all | bytes 1310720 | tf_op jit(solution)/shard_map/all_to_all | solution.py:230
  134.3 6.9 %collective-permute-start.16 = (f32[32,24,128]{2,1,0:T(8,128)S(1)}, f32[32,24,128]{2,1,0:T(8,128)S(1)}, u32[]{:S(2)}, u32[]{:S(2)}) collective-permute-start(f32[32,24,128]{2,1,0:T(8,128)S(1)} %slice.14), channel_id=1, source_target_pairs={{0,1},{1,0},{2,3},{3,2},{4,5},{5,4},{6,7},{7,6},{8,9},{9,8},{10,11... | collective-permute-start | bytes 1179656 | tf_op jit(solution)/shard_map/ppermute | solution.py:214
  141.2 1.3 collective-permute-done.16.other
  142.5 5.6 %solve.1.xt = bf16[256,512]{1,0:T(8,128)(2,1)} custom-call(s32[1]{0:T(128)} %bitcast.me, f32[32,40,128]{2,1,0:T(8,128)S(1)} %all_to_all.11.mine, f32[32,24,128]{2,1,0:T(8,128)S(1)} %collective-permute-done.16.other), custom_call_target="tpu_custom_call" | custom-call | tf_op jit(solution)/shard_map/solve/pallas_call | solution.py:175
  148.0 7.2 %update.1 = f32[4096,128]{1,0:T(8,128)} custom-call(f32[4096,128]{1,0:T(8,128)} %c_ref.1, bf16[512,4096]{1,0:T(8,128)(2,1)} %get-tuple-element.8.vhi, bf16[512,4096]{1,0:T(8,128)(2,1)} %get-tuple-element.9.vlo, bf16[256,512]{1,0:T(8,128)(2,1)} %solve.1.xt), custom_call_target="tpu_custom_call" | custom-call | tf_op jit(solution)/shard_map/update/pallas_call | solution.py:192
  (4 shorter events, 0.1 us)
Async XLA Ops:
  0.0 68.3 %copy-start = (f32[4096,128]{1,0:T(8,128)S(1)}, f32[4096,128]{1,0:T(8,128)}, u32[]{:S(2)}) copy-start(f32[4096,128]{1,0:T(8,128)} %c_ref.1) | copy-start | bytes 6291460
  1.2 15.3 %collective-permute-start = (f32[16,4096]{1,0:T(8,128)S(1)}, f32[16,4096]{1,0:T(8,128)S(1)}, u32[]{:S(2)}, u32[]{:S(2)}) collective-permute-start(f32[16,4096]{1,0:T(8,128)S(1)} %get-tuple-element.12), channel_id=1, source_target_pairs={{0,2},{1,15},{2,0},{3,5},{4,6},{5,3},{6,4},{7,9},{8,10},{9,7},{10,... | collective-permute-start | bytes 786440 | tf_op jit(solution)/shard_map/ppermute | solution.py:210
  12.7 8.3 %collective-permute-start.1 = (f32[16,4096]{1,0:T(8,128)S(1)}, f32[16,4096]{1,0:T(8,128)S(1)}, u32[]{:S(2)}, u32[]{:S(2)}) collective-permute-start(f32[16,4096]{1,0:T(8,128)S(1)} %get-tuple-element.11), channel_id=1, source_target_pairs={{0,2},{1,15},{2,0},{3,5},{4,6},{5,3},{6,4},{7,9},{8,10},{9,7},{10,... | collective-permute-start | bytes 786440 | tf_op jit(solution)/shard_map/ppermute | solution.py:210
  16.5 10.2 %collective-permute-start.2 = (f32[32,4096]{1,0:T(8,128)S(1)}, f32[32,4096]{1,0:T(8,128)S(1)}, u32[]{:S(2)}, u32[]{:S(2)}) collective-permute-start(f32[32,4096]{1,0:T(8,128)S(1)} %pad_maximum_fusion.refs_0_), channel_id=1, source_target_pairs={{0,14},{1,3},{2,4},{3,1},{4,2},{5,7},{6,8},{7,5},{8,6},{9,11},{10,... | collective-permute-start | bytes 1572872 | tf_op jit(solution)/shard_map/ppermute | solution.py:210
  21.1 11.4 %collective-permute-start.3 = (f32[32,4096]{1,0:T(8,128)S(1)}, f32[32,4096]{1,0:T(8,128)}, u32[]{:S(2)}, u32[]{:S(2)}) collective-permute-start(f32[32,4096]{1,0:T(8,128)S(1)} %pad_maximum_fusion.1.refs_1_), channel_id=1, source_target_pairs={{0,14},{1,3},{2,4},{3,1},{4,2},{5,7},{6,8},{7,5},{8,6},{9,11},{10,... | collective-permute-start | bytes 1572872 | tf_op jit(solution)/shard_map/ppermute | solution.py:210
  26.7 18.8 %collective-permute-start.4 = (f32[32,4096]{1,0:T(8,128)S(1)}, f32[32,4096]{1,0:T(8,128)}, u32[]{:S(2)}, u32[]{:S(2)}) collective-permute-start(f32[32,4096]{1,0:T(8,128)S(1)} %collective-permute-done.2.refs_2_), channel_id=1, source_target_pairs={{0,2},{1,15},{2,0},{3,5},{4,6},{5,3},{6,4},{7,9},{8,10},{9,7},{10,... | collective-permute-start | bytes 1572872 | tf_op jit(solution)/shard_map/ppermute | solution.py:210
  32.5 16.8 %collective-permute-start.5 = (f32[32,4096]{1,0:T(8,128)}, f32[32,4096]{1,0:T(8,128)}, u32[]{:S(2)}, u32[]{:S(2)}) collective-permute-start(f32[32,4096]{1,0:T(8,128)} %collective-permute-done.3.refs_3_), channel_id=1, source_target_pairs={{0,2},{1,15},{2,0},{3,5},{4,6},{5,3},{6,4},{7,9},{8,10},{9,7},{10,... | collective-permute-start | bytes 1572872 | tf_op jit(solution)/shard_map/ppermute | solution.py:210
  37.0 14.1 %collective-permute-start.8 = (f32[32,4096]{1,0:T(8,128)S(1)}, f32[32,4096]{1,0:T(8,128)S(1)}, u32[]{:S(2)}, u32[]{:S(2)}) collective-permute-start(f32[32,4096]{1,0:T(8,128)S(1)} %pad_maximum_fusion.refs_0_), channel_id=1, source_target_pairs={{0,1},{1,0},{2,3},{3,2},{4,5},{5,4},{6,7},{7,6},{8,9},{9,8},{10,11... | collective-permute-start | bytes 1572872 | tf_op jit(solution)/shard_map/ppermute | solution.py:214
  40.4 15.7 %collective-permute-start.9 = (f32[32,4096]{1,0:T(8,128)S(1)}, f32[32,4096]{1,0:T(8,128)S(1)}, u32[]{:S(2)}, u32[]{:S(2)}) collective-permute-start(f32[32,4096]{1,0:T(8,128)S(1)} %pad_maximum_fusion.1.refs_1_), channel_id=1, source_target_pairs={{0,1},{1,0},{2,3},{3,2},{4,5},{5,4},{6,7},{7,6},{8,9},{9,8},{10,11... | collective-permute-start | bytes 1572872 | tf_op jit(solution)/shard_map/ppermute | solution.py:214
  42.4 16.5 %collective-permute-start.10 = (f32[32,4096]{1,0:T(8,128)S(1)}, f32[32,4096]{1,0:T(8,128)S(1)}, u32[]{:S(2)}, u32[]{:S(2)}) collective-permute-start(f32[32,4096]{1,0:T(8,128)S(1)} %collective-permute-done.2.refs_2_), channel_id=1, source_target_pairs={{0,1},{1,0},{2,3},{3,2},{4,5},{5,4},{6,7},{7,6},{8,9},{9,8},{10,11... | collective-permute-start | bytes 1572872 | tf_op jit(solution)/shard_map/ppermute | solution.py:214
  44.8 0.8 copy-start.1
  45.6 16.5 %collective-permute-start.6 = (f32[32,4096]{1,0:T(8,128)}, f32[32,4096]{1,0:T(8,128)}, u32[]{:S(2)}, u32[]{:S(2)}) collective-permute-start(f32[32,4096]{1,0:T(8,128)} %collective-permute-done.4.refs_4_), channel_id=1, source_target_pairs={{0,14},{1,3},{2,4},{3,1},{4,2},{5,7},{6,8},{7,5},{8,6},{9,11},{10,... | collective-permute-start | bytes 1572872 | tf_op jit(solution)/shard_map/ppermute | solution.py:210
  49.2 14.8 %collective-permute-start.7 = (f32[32,4096]{1,0:T(8,128)}, f32[32,4096]{1,0:T(8,128)}, u32[]{:S(2)}, u32[]{:S(2)}) collective-permute-start(f32[32,4096]{1,0:T(8,128)} %collective-permute-done.5.refs_5_), channel_id=1, source_target_pairs={{0,14},{1,3},{2,4},{3,1},{4,2},{5,7},{6,8},{7,5},{8,6},{9,11},{10,... | collective-permute-start | bytes 1572872 | tf_op jit(solution)/shard_map/ppermute | solution.py:210
  51.2 0.8 copy-start.3
  52.0 14.5 %collective-permute-start.11 = (f32[32,4096]{1,0:T(8,128)}, f32[32,4096]{1,0:T(8,128)}, u32[]{:S(2)}, u32[]{:S(2)}) collective-permute-start(f32[32,4096]{1,0:T(8,128)} %collective-permute-done.3.refs_3_), channel_id=1, source_target_pairs={{0,1},{1,0},{2,3},{3,2},{4,5},{5,4},{6,7},{7,6},{8,9},{9,8},{10,11... | collective-permute-start | bytes 1572872 | tf_op jit(solution)/shard_map/ppermute | solution.py:214
  56.1 0.8 copy-start.5
  56.9 9.5 %collective-permute-start.12 = (f32[32,4096]{1,0:T(8,128)}, f32[32,4096]{1,0:T(8,128)}, u32[]{:S(2)}, u32[]{:S(2)}) collective-permute-start(f32[32,4096]{1,0:T(8,128)} %collective-permute-done.4.refs_4_), channel_id=1, source_target_pairs={{0,1},{1,0},{2,3},{3,2},{4,5},{5,4},{6,7},{7,6},{8,9},{9,8},{10,11... | collective-permute-start | bytes 1572872 | tf_op jit(solution)/shard_map/ppermute | solution.py:214
  58.9 0.8 copy-start.7
  59.7 6.8 %collective-permute-start.13 = (f32[32,4096]{1,0:T(8,128)}, f32[32,4096]{1,0:T(8,128)}, u32[]{:S(2)}, u32[]{:S(2)}) collective-permute-start(f32[32,4096]{1,0:T(8,128)} %collective-permute-done.5.refs_5_), channel_id=1, source_target_pairs={{0,1},{1,0},{2,3},{3,2},{4,5},{5,4},{6,7},{7,6},{8,9},{9,8},{10,11... | collective-permute-start | bytes 1572872 | tf_op jit(solution)/shard_map/ppermute | solution.py:214
  62.1 4.4 %collective-permute-start.14 = (f32[32,4096]{1,0:T(8,128)}, f32[32,4096]{1,0:T(8,128)}, u32[]{:S(2)}, u32[]{:S(2)}) collective-permute-start(f32[32,4096]{1,0:T(8,128)} %collective-permute-done.6.refs_6_), channel_id=1, source_target_pairs={{0,1},{1,0},{2,3},{3,2},{4,5},{5,4},{6,7},{7,6},{8,9},{9,8},{10,11... | collective-permute-start | bytes 1572872 | tf_op jit(solution)/shard_map/ppermute | solution.py:214
  64.0 4.3 %collective-permute-start.15 = (f32[32,4096]{1,0:T(8,128)}, f32[32,4096]{1,0:T(8,128)}, u32[]{:S(2)}, u32[]{:S(2)}) collective-permute-start(f32[32,4096]{1,0:T(8,128)} %collective-permute-done.7.refs_7_), channel_id=1, source_target_pairs={{0,1},{1,0},{2,3},{3,2},{4,5},{5,4},{6,7},{7,6},{8,9},{9,8},{10,11... | collective-permute-start | bytes 1572872 | tf_op jit(solution)/shard_map/ppermute | solution.py:214
  68.3 1.0 copy-start.2
  69.3 1.0 copy-start.4
  70.4 1.0 copy-start.6
  71.4 1.0 copy-start.8
  134.3 8.2 %collective-permute-start.16 = (f32[32,24,128]{2,1,0:T(8,128)S(1)}, f32[32,24,128]{2,1,0:T(8,128)S(1)}, u32[]{:S(2)}, u32[]{:S(2)}) collective-permute-start(f32[32,24,128]{2,1,0:T(8,128)S(1)} %slice.14), channel_id=1, source_target_pairs={{0,1},{1,0},{2,3},{3,2},{4,5},{5,4},{6,7},{7,6},{8,9},{9,8},{10,11... | collective-permute-start | bytes 1179656 | tf_op jit(solution)/shard_map/ppermute | solution.py:214

commit v5 on v4

v5 whole, which is shorter than its diff:
```python
import jax
import jax.numpy as jnp
from jax import lax
from jax.experimental import pallas as pl
from jax.experimental.pallas import tpu as pltpu
from jax.sharding import PartitionSpec as P

F32 = jnp.float32
BF16 = jnp.bfloat16
CHIPS = 8
ROWS = 4096
COLS = 128
NV = 512
PARTS = tuple(pl.ds(first, 1024) for first in range(0, ROWS, 1024))
VMEM = 32 * 1024 * 1024
ARRIVAL = ((0, 1), (-1, -2), (2, 3), (-3, -4))
GRAM_BLOCKS = (
    ((0, 2), (0, 3), (1, 2), (1, 3)),
    ((0, 0), (0, 1), (1, 1), (2, 2), (2, 3), (3, 3)),
)


def split(value):
    high = value.astype(BF16)
    low = (value - high.astype(F32)).astype(BF16)
    return high, low


def nt(left, right):
    return lax.dot_general(left, right, (((1,), (1,)), ((), ())), preferred_element_type=F32)


def nn(left, right):
    return lax.dot_general(left, right, (((1,), (0,)), ((), ())), preferred_element_type=F32)


def hidot(left, right):
    return jnp.dot(left, right, precision=lax.Precision.HIGHEST, preferred_element_type=F32)


def assemble(me, index, piece, vhi, vlo):
    chip, core = me // 2, me % 2
    turn = 1 - 2 * ((chip + core) % 2)
    swapped, arrival, block = index // 8, index % 8 // 2, index % 2
    for half in range(2):
        step = ARRIVAL[arrival][half] * (1 - 2 * swapped)
        source = (chip + turn * step + CHIPS) % CHIPS
        column = block * 256 + source * 32 + (1 - core if swapped else core) * 16
        high, low = split(piece[half * 16 : half * 16 + 16, :])
        at = pl.ds(pl.multiple_of(column, 16), 16)
        vhi[at, :] = high
        vlo[at, :] = low


def products_kernel(me, *refs):
    pieces = refs[:16]
    c_hbm, vhi_hbm, vlo_hbm, out, raw, c_ref, vhi, vlo, come, gone = refs[16:]
    first_core = me[0] % 2 == 0
    incoming = [pltpu.make_async_copy(piece, raw.at[n], come.at[n]) for n, piece in enumerate(pieces)]
    for index, at in enumerate(PARTS):
        incoming.append(pltpu.make_async_copy(c_hbm.at[at], c_ref.at[at], come.at[16 + index]))
    for copy in incoming:
        copy.start()
    for n in sorted(range(16), key=lambda n: -(n % 8)):
        incoming[n].wait()
        assemble(me[0], n, raw.at[n], vhi, vlo)
    outgoing = []
    for index, at in enumerate(PARTS):
        for which, (here, there) in enumerate(((vhi, vhi_hbm), (vlo, vlo_hbm))):
            outgoing.append(pltpu.make_async_copy(here.at[:, at], there.at[:, at], gone.at[index, which]))
            outgoing[-1].start()
    for copy in incoming[16:]:
        copy.wait()
    chi, clo = split(c_ref[...])
    both = nn(vhi[...], jnp.concatenate([chi, clo], axis=1))
    proj = both[:, :COLS] + both[:, COLS:] + nn(vlo[...], chi)
    out[:, :16, :] = proj.reshape(32, 16, COLS)

    @pl.when(first_core)
    def _():
        cross = nt(vhi[:256, :], vhi[256:, :]) + nt(vhi[:256, :], vlo[256:, :]) + nt(vlo[:256, :], vhi[256:, :])
        parts = [cross[:128, :128], cross[:128, 128:], cross[128:, :128], cross[128:, 128:]]
        parts.append(jnp.zeros((256, 128), F32))
        out[:, 16:, :] = jnp.concatenate(parts, axis=0).reshape(32, 24, COLS)

    @pl.when(jnp.logical_not(first_core))
    def _():
        parts = []
        for at in (0, 256):
            high = vhi[at : at + 256, :]
            mixed = nt(high, vlo[at : at + 256, :])
            square = nt(high, high) + mixed + mixed.T
            parts += [square[:128, :128], square[:128, 128:], square[128:, 128:]]
        out[:, 16:, :] = jnp.concatenate(parts, axis=0).reshape(32, 24, COLS)

    for copy in outgoing:
        copy.wait()


def products(me, pieces, current):
    return pl.pallas_call(
        products_kernel,
        in_specs=[pl.BlockSpec(memory_space=pltpu.SMEM)] + [pl.BlockSpec(memory_space=pl.ANY)] * 17,
        out_specs=[pl.BlockSpec(memory_space=pl.ANY)] * 2 + [pl.BlockSpec(memory_space=pltpu.VMEM)],
        out_shape=[
            pltpu.HBM((NV, ROWS), BF16),
            pltpu.HBM((NV, ROWS), BF16),
            jax.ShapeDtypeStruct((32, 40, COLS), F32),
        ],
        scratch_shapes=[
            pltpu.VMEM((16, 32, ROWS), F32),
            pltpu.VMEM((ROWS, COLS), F32),
            pltpu.VMEM((NV, ROWS), BF16),
            pltpu.VMEM((NV, ROWS), BF16),
            pltpu.SemaphoreType.DMA((16 + len(PARTS),)),
            pltpu.SemaphoreType.DMA((len(PARTS), 2)),
        ],
        compiler_params=pltpu.CompilerParams(vmem_limit_bytes=VMEM),
        name="products",
    )(me, *pieces, current)


def invert_unit(nilpot):
    row = lax.broadcasted_iota(jnp.int32, (128, 128), 0)
    col = lax.broadcasted_iota(jnp.int32, (128, 128), 1)
    eye = (row == col).astype(F32)
    near = [jnp.where(row // 4 == col // 4, n, 0.0) for n in nilpot]
    square = [hidot(n, n) for n in near]
    inverse = [hidot(eye - n, eye + s) for n, s in zip(near, square)]
    size = 4
    while size < 128:
        pair = (row // (2 * size) == col // (2 * size)) & (row // size != col // size)
        right = [hidot(jnp.where(pair, n, 0.0), r) for n, r in zip(nilpot, inverse)]
        inverse = [r - hidot(r, t) for r, t in zip(inverse, right)]
        size *= 2
    return inverse


def coefficients(me, mine, other):
    zero = me[0] % 2 == 0
    gram = {}
    for which in range(2):
        flat = jnp.where(zero == (which == 0), mine[:, 16:, :], other[...]).reshape(768, 128)
        for index, at in enumerate(GRAM_BLOCKS[which]):
            gram[at] = flat[index * 128 : index * 128 + 128]
    project = mine[:, :16, :].reshape(NV, COLS)
    row = lax.broadcasted_iota(jnp.int32, (128, 128), 0)
    col = lax.broadcasted_iota(jnp.int32, (128, 128), 1)
    scale = [2.0 / jnp.sum(jnp.where(row == col, gram[i, i], 0.0), axis=1, keepdims=True) for i in range(4)]
    inverse = invert_unit([jnp.where(row < col, gram[i, i] * scale[i], 0.0) for i in range(4)])
    wide = []
    for i in (0, 2):
        corner = hidot(inverse[i], hidot(gram[i, i + 1] * scale[i], inverse[i + 1]))
        upper = jnp.concatenate([inverse[i], -corner], axis=1)
        lower = jnp.concatenate([jnp.zeros((128, 128), F32), inverse[i + 1]], axis=1)
        wide.append(jnp.concatenate([upper, lower], axis=0))
    scales = [jnp.concatenate(scale[i : i + 2], axis=0) for i in (0, 2)]
    cross = jnp.concatenate([jnp.concatenate([gram[i, 2], gram[i, 3]], axis=1) for i in (0, 1)], axis=0)
    later = hidot(wide[1], project[256:] * scales[1])
    coef = [hidot(wide[0], (project[:256] - hidot(cross, later)) * scales[0]), later]
    return split(jnp.concatenate(coef, axis=0).T)


def finish_kernel(me, mine, other, c_hbm, vhi_hbm, vlo_hbm, out, c_ref, vhi, vlo, done, come, gone):
    copies = []
    for index, at in enumerate(PARTS):
        pairs = ((vhi_hbm.at[:, at], vhi.at[:, at]), (vlo_hbm.at[:, at], vlo.at[:, at]), (c_hbm.at[at], c_ref.at[at]))
        copies.append([pltpu.make_async_copy(*pair, come.at[index, which]) for which, pair in enumerate(pairs)])
        for copy in copies[-1]:
            copy.start()
    xhi, xlo = coefficients(me, mine, other)
    both = jnp.concatenate([xhi, xlo], axis=0)
    writes = []
    for index in range(0, len(PARTS), 2):
        for copy in copies[index] + copies[index + 1]:
            copy.wait()
        rows = pl.ds(PARTS[index].start, PARTS[index].size * 2)
        first = nn(both, vhi[:, rows])
        change = first[:COLS] + first[COLS:] + nn(xhi, vlo[:, rows])
        for half, at in enumerate(PARTS[index : index + 2]):
            done[at, :] = c_ref[at, :] - change[:, half * at.size : (half + 1) * at.size].T
            writes.append(pltpu.make_async_copy(done.at[at], out.at[at], gone.at[index + half]))
            writes[-1].start()
    for write in writes:
        write.wait()


def finish(me, mine, other, current, vhi, vlo):
    return pl.pallas_call(
        finish_kernel,
        in_specs=[pl.BlockSpec(memory_space=pltpu.SMEM)]
        + [pl.BlockSpec(memory_space=pltpu.VMEM)] * 2
        + [pl.BlockSpec(memory_space=pl.ANY)] * 3,
        out_specs=pl.BlockSpec(memory_space=pl.ANY),
        out_shape=jax.ShapeDtypeStruct((ROWS, COLS), F32),
        scratch_shapes=[
            pltpu.VMEM((ROWS, COLS), F32),
            pltpu.VMEM((NV, ROWS), BF16),
            pltpu.VMEM((NV, ROWS), BF16),
            pltpu.VMEM((ROWS, COLS), F32),
            pltpu.SemaphoreType.DMA((len(PARTS), 3)),
            pltpu.SemaphoreType.DMA((len(PARTS),)),
        ],
        compiler_params=pltpu.CompilerParams(vmem_limit_bytes=VMEM),
        name="finish",
    )(me, mine, other, current, vhi, vlo)


def exchange(value, side):
    perm = []
    for chip in range(CHIPS):
        for core in range(2):
            turn = 1 if (chip + core) % 2 == 0 else -1
            target = (chip + side * turn) % CHIPS
            perm.append((chip * 2 + core, target * 2 + core))
    return lax.ppermute(value, "col", perm)


def in_hbm(value):
    return pltpu.with_memory_space_constraint(value, pltpu.HBM)


def swap_cores(value):
    return lax.ppermute(value, "col", [(i, i ^ 1) for i in range(2 * CHIPS)])


def shards(eigvecs, householder):
    me = lax.axis_index("col").reshape(1)
    own = householder.transpose(0, 2, 1)
    chains = [own[0], own[1]]
    chains = [jnp.concatenate([piece, exchange(piece, 1)], axis=0) for piece in chains]
    pieces = list(chains)
    for side in (-1, 1, -1):
        chains = [exchange(piece, side) for piece in chains]
        pieces += chains
    pieces += [swap_cores(piece) for piece in pieces]

    vhi, vlo, partial = products(me, [in_hbm(piece) if n % 8 < 4 else piece for n, piece in enumerate(pieces)], in_hbm(eigvecs))
    summed = lax.all_to_all(partial, "row", 0, 0, tiled=True).sum(axis=0)
    mine = lax.all_to_all(jnp.broadcast_to(summed[None], (32, 40, COLS)), "row", 0, 0, tiled=True)
    other = swap_cores(mine[:, 16:, :])
    return finish(me, mine, other, in_hbm(eigvecs), in_hbm(vhi), in_hbm(vlo))


def solution(mesh):
    in_specs = (P("row", "col"), P(None, "row", "col"))
    out_specs = P("row", "col")
    return jax.shard_map(shards, mesh=mesh, in_specs=in_specs, out_specs=out_specs, check_vma=False)
```

time: 156 us -> 146 us (0.936)
  local copies, waits for them, and re-layouts: 8.63 us -> 1.16 us
  Pallas kernels: 23.6 us -> 19.5 us
  starting transfers between devices: 59.3 us -> 61.1 us
    unnamed x18 -> x12, local copies, waits for them, and re-layouts: 7.34 us -> 0.03 us
    pallas_call x3 -> x2, Pallas kernels: 23.6 us -> 19.5 us  [the longest x1 10.6 us: finish(): pl.pallas_call(finish_kernel, in_specs=[pl.BlockSpec(memory_space=pltpu.S...]
    ppermute x9, starting transfers between devices: 27.3 us -> 29.1 us  [swap_cores(): return lax.ppermute(value, 'col', [(i, i ^ 1) for i in range(2 * CHIPS)])]
where the time goes in v5:
time: 146 us; the launch traced here: 145 us
  starting transfers between devices  61.1 us (42%)
  blocking collectives  50.9 us (35%)
  Pallas kernels  19.5 us (13%)
  waiting for transfers between devices  12 us (8%)
    ppermute x8, starting transfers between devices, exchange(): return lax.ppermute(value, 'col', perm)  31.9 us
    ppermute x9, starting transfers between devices, swap_cores(): return lax.ppermute(value, 'col', [(i, i ^ 1) for i in range(2 * CHIPS)])  29.1 us
    all_to_all x1, blocking collectives, shards(): summed = lax.all_to_all(partial, 'row', 0, 0, tiled=True).sum(axis=0)  28.5 us
    all_to_all x1, blocking collectives, shards(): lax.all_to_all(jnp.broadcast_to(summed[None], (32, 40, COLS)), 'row', 0,...  22.4 us
    pallas_call x1, Pallas kernels, finish(): pl.pallas_call(finish_kernel, in_specs=[pl.BlockSpec(memory_space=pltpu.S...  10.6 us
    ppermute x8, waiting for transfers between devices, exchange(): return lax.ppermute(value, 'col', perm)  9.29 us
    pallas_call x1, Pallas kernels, products(): pl.pallas_call(products_kernel, in_specs=[pl.BlockSpec(memory_space=pltpu...  8.87 us
  transfers between devices with their start and end apart: 17, of which 6 were waited for; matrix products, arithmetic and copies ran while one was open for 0% of the time, Pallas kernels for 0%

profile of v5, /device:TPU:1, one launch (start us, length us, event | category | flops | bytes accessed | tf_op | source)
XLA Modules:
  0.0 145.3 jit_solution(15935333129445085571)
XLA Ops:
  0.0 1.1 slice_bitcast_fusion
  1.1 11.5 %collective-permute-start = (f32[16,4096]{1,0:T(8,128)S(1)}, f32[16,4096]{1,0:T(8,128)S(1)}, u32[]{:S(2)}, u32[]{:S(2)}) collective-permute-start(f32[16,4096]{1,0:T(8,128)S(1)} %get-tuple-element.12), channel_id=1, source_target_pairs={{0,2},{1,15},{2,0},{3,5},{4,6},{5,3},{6,4},{7,9},{8,10},{9,7},{10,... | collective-permute-start | bytes 786440 | tf_op jit(solution)/shard_map/ppermute | solution.py:216
  12.6 1.9 %collective-permute-start.1 = (f32[16,4096]{1,0:T(8,128)S(1)}, f32[16,4096]{1,0:T(8,128)S(1)}, u32[]{:S(2)}, u32[]{:S(2)}) collective-permute-start(f32[16,4096]{1,0:T(8,128)S(1)} %get-tuple-element.11), channel_id=1, source_target_pairs={{0,2},{1,15},{2,0},{3,5},{4,6},{5,3},{6,4},{7,9},{8,10},{9,7},{10,... | collective-permute-start | bytes 786440 | tf_op jit(solution)/shard_map/ppermute | solution.py:216
  14.5 1.8 %collective-permute-done = f32[16,4096]{1,0:T(8,128)S(1)} collective-permute-done((f32[16,4096]{1,0:T(8,128)S(1)}, f32[16,4096]{1,0:T(8,128)S(1)}, u32[]{:S(2)}, u32[]{:S(2)}) %collective-permute-start) | collective-permute-done | bytes 262176 | tf_op jit(solution)/shard_map/ppermute | solution.py:216
  16.4 0.0 copy-start
  16.4 1.9 %collective-permute-start.2 = (f32[32,4096]{1,0:T(8,128)S(1)}, f32[32,4096]{1,0:T(8,128)S(1)}, u32[]{:S(2)}, u32[]{:S(2)}) collective-permute-start(f32[32,4096]{1,0:T(8,128)S(1)} %pad_maximum_fusion.refs_0_), channel_id=1, source_target_pairs={{0,14},{1,3},{2,4},{3,1},{4,2},{5,7},{6,8},{7,5},{8,6},{9,11},{10,... | collective-permute-start | bytes 1572872 | tf_op jit(solution)/shard_map/ppermute | solution.py:216
  18.3 2.6 %collective-permute-done.1 = f32[16,4096]{1,0:T(8,128)S(1)} collective-permute-done((f32[16,4096]{1,0:T(8,128)S(1)}, f32[16,4096]{1,0:T(8,128)S(1)}, u32[]{:S(2)}, u32[]{:S(2)}) %collective-permute-start.1) | collective-permute-done | bytes 262176 | tf_op jit(solution)/shard_map/ppermute | solution.py:216
  20.9 0.0 copy-start.1
  21.0 1.9 %collective-permute-start.3 = (f32[32,4096]{1,0:T(8,128)S(1)}, f32[32,4096]{1,0:T(8,128)}, u32[]{:S(2)}, u32[]{:S(2)}) collective-permute-start(f32[32,4096]{1,0:T(8,128)S(1)} %pad_maximum_fusion.1.refs_1_), channel_id=1, source_target_pairs={{0,14},{1,3},{2,4},{3,1},{4,2},{5,7},{6,8},{7,5},{8,6},{9,11},{10,... | collective-permute-start | bytes 1572872 | tf_op jit(solution)/shard_map/ppermute | solution.py:216
  22.9 3.7 %collective-permute-done.2.refs_2_ = f32[32,4096]{1,0:T(8,128)S(1)} collective-permute-done((f32[32,4096]{1,0:T(8,128)S(1)}, f32[32,4096]{1,0:T(8,128)S(1)}, u32[]{:S(2)}, u32[]{:S(2)}) %collective-permute-start.2) | collective-permute-done | bytes 524320 | tf_op jit(solution)/shard_map/ppermute | solution.py:216
  26.6 0.0 copy-start.2
  26.6 4.6 %collective-permute-start.4 = (f32[32,4096]{1,0:T(8,128)S(1)}, f32[32,4096]{1,0:T(8,128)S(1)}, u32[]{:S(2)}, u32[]{:S(2)}) collective-permute-start(f32[32,4096]{1,0:T(8,128)S(1)} %collective-permute-done.2.refs_2_), channel_id=1, source_target_pairs={{0,2},{1,15},{2,0},{3,5},{4,6},{5,3},{6,4},{7,9},{8,10},{9,7},{10,... | collective-permute-start | bytes 1572872 | tf_op jit(solution)/shard_map/ppermute | solution.py:216
  31.2 1.2 collective-permute-done.3.refs_3_
  32.3 4.6 %collective-permute-start.5 = (f32[32,4096]{1,0:T(8,128)}, f32[32,4096]{1,0:T(8,128)S(1)}, u32[]{:S(2)}, u32[]{:S(2)}) collective-permute-start(f32[32,4096]{1,0:T(8,128)} %collective-permute-done.3.refs_3_), channel_id=1, source_target_pairs={{0,2},{1,15},{2,0},{3,5},{4,6},{5,3},{6,4},{7,9},{8,10},{9,7},{10,... | collective-permute-start | bytes 1572872 | tf_op jit(solution)/shard_map/ppermute | solution.py:216
  36.9 3.4 %collective-permute-start.8 = (f32[32,4096]{1,0:T(8,128)S(1)}, f32[32,4096]{1,0:T(8,128)S(1)}, u32[]{:S(2)}, u32[]{:S(2)}) collective-permute-start(f32[32,4096]{1,0:T(8,128)S(1)} %pad_maximum_fusion.refs_0_), channel_id=1, source_target_pairs={{0,1},{1,0},{2,3},{3,2},{4,5},{5,4},{6,7},{7,6},{8,9},{9,8},{10,11... | collective-permute-start | bytes 1572872 | tf_op jit(solution)/shard_map/ppermute | solution.py:224
  40.3 1.9 %collective-permute-start.9 = (f32[32,4096]{1,0:T(8,128)S(1)}, f32[32,4096]{1,0:T(8,128)S(1)}, u32[]{:S(2)}, u32[]{:S(2)}) collective-permute-start(f32[32,4096]{1,0:T(8,128)S(1)} %pad_maximum_fusion.1.refs_1_), channel_id=1, source_target_pairs={{0,1},{1,0},{2,3},{3,2},{4,5},{5,4},{6,7},{7,6},{8,9},{9,8},{10,11... | collective-permute-start | bytes 1572872 | tf_op jit(solution)/shard_map/ppermute | solution.py:224
  42.2 2.4 %collective-permute-start.10 = (f32[32,4096]{1,0:T(8,128)S(1)}, f32[32,4096]{1,0:T(8,128)S(1)}, u32[]{:S(2)}, u32[]{:S(2)}) collective-permute-start(f32[32,4096]{1,0:T(8,128)S(1)} %collective-permute-done.2.refs_2_), channel_id=1, source_target_pairs={{0,1},{1,0},{2,3},{3,2},{4,5},{5,4},{6,7},{7,6},{8,9},{9,8},{10,11... | collective-permute-start | bytes 1572872 | tf_op jit(solution)/shard_map/ppermute | solution.py:224
  44.6 0.0 collective-permute-done.4.refs_4_
  44.7 3.6 %collective-permute-start.6 = (f32[32,4096]{1,0:T(8,128)S(1)}, f32[32,4096]{1,0:T(8,128)S(1)}, u32[]{:S(2)}, u32[]{:S(2)}) collective-permute-start(f32[32,4096]{1,0:T(8,128)S(1)} %collective-permute-done.4.refs_4_), channel_id=1, source_target_pairs={{0,14},{1,3},{2,4},{3,1},{4,2},{5,7},{6,8},{7,5},{8,6},{9,11},{10,... | collective-permute-start | bytes 1572872 | tf_op jit(solution)/shard_map/ppermute | solution.py:216
  48.3 0.0 collective-permute-done.5.refs_5_
  48.3 1.9 %collective-permute-start.7 = (f32[32,4096]{1,0:T(8,128)S(1)}, f32[32,4096]{1,0:T(8,128)S(1)}, u32[]{:S(2)}, u32[]{:S(2)}) collective-permute-start(f32[32,4096]{1,0:T(8,128)S(1)} %collective-permute-done.5.refs_5_), channel_id=1, source_target_pairs={{0,14},{1,3},{2,4},{3,1},{4,2},{5,7},{6,8},{7,5},{8,6},{9,11},{10,... | collective-permute-start | bytes 1572872 | tf_op jit(solution)/shard_map/ppermute | solution.py:216
  50.2 0.0 collective-permute-done.8.refs_8_
  50.3 0.0 copy-start.3
  50.3 4.8 %collective-permute-start.11 = (f32[32,4096]{1,0:T(8,128)}, f32[32,4096]{1,0:T(8,128)}, u32[]{:S(2)}, u32[]{:S(2)}) collective-permute-start(f32[32,4096]{1,0:T(8,128)} %collective-permute-done.3.refs_3_), channel_id=1, source_target_pairs={{0,1},{1,0},{2,3},{3,2},{4,5},{5,4},{6,7},{7,6},{8,9},{9,8},{10,11... | collective-permute-start | bytes 1572872 | tf_op jit(solution)/shard_map/ppermute | solution.py:224
  55.1 0.0 collective-permute-done.9.refs_9_
  55.1 0.0 copy-start.4
  55.1 1.9 %collective-permute-start.12 = (f32[32,4096]{1,0:T(8,128)S(1)}, f32[32,4096]{1,0:T(8,128)S(1)}, u32[]{:S(2)}, u32[]{:S(2)}) collective-permute-start(f32[32,4096]{1,0:T(8,128)S(1)} %collective-permute-done.4.refs_4_), channel_id=1, source_target_pairs={{0,1},{1,0},{2,3},{3,2},{4,5},{5,4},{6,7},{7,6},{8,9},{9,8},{10,11... | collective-permute-start | bytes 1572872 | tf_op jit(solution)/shard_map/ppermute | solution.py:224
  57.0 0.0 collective-permute-done.10.refs_10_
  57.0 0.0 copy-start.5
  57.1 2.4 %collective-permute-start.13 = (f32[32,4096]{1,0:T(8,128)S(1)}, f32[32,4096]{1,0:T(8,128)S(1)}, u32[]{:S(2)}, u32[]{:S(2)}) collective-permute-start(f32[32,4096]{1,0:T(8,128)S(1)} %collective-permute-done.5.refs_5_), channel_id=1, source_target_pairs={{0,1},{1,0},{2,3},{3,2},{4,5},{5,4},{6,7},{7,6},{8,9},{9,8},{10,11... | collective-permute-start | bytes 1572872 | tf_op jit(solution)/shard_map/ppermute | solution.py:224
  59.5 0.0 collective-permute-done.6.refs_6_
  59.5 1.9 %collective-permute-start.14 = (f32[32,4096]{1,0:T(8,128)S(1)}, f32[32,4096]{1,0:T(8,128)}, u32[]{:S(2)}, u32[]{:S(2)}) collective-permute-start(f32[32,4096]{1,0:T(8,128)S(1)} %collective-permute-done.6.refs_6_), channel_id=1, source_target_pairs={{0,1},{1,0},{2,3},{3,2},{4,5},{5,4},{6,7},{7,6},{8,9},{9,8},{10,11... | collective-permute-start | bytes 1572872 | tf_op jit(solution)/shard_map/ppermute | solution.py:224
  61.4 0.0 collective-permute-done.7.refs_7_
  61.4 0.0 copy-done
  61.4 3.3 %collective-permute-start.15 = (f32[32,4096]{1,0:T(8,128)S(1)}, f32[32,4096]{1,0:T(8,128)}, u32[]{:S(2)}, u32[]{:S(2)}) collective-permute-start(f32[32,4096]{1,0:T(8,128)S(1)} %collective-permute-done.7.refs_7_), channel_id=1, source_target_pairs={{0,1},{1,0},{2,3},{3,2},{4,5},{5,4},{6,7},{7,6},{8,9},{9,8},{10,11... | collective-permute-start | bytes 1572872 | tf_op jit(solution)/shard_map/ppermute | solution.py:224
  64.8 0.0 copy-done.1
  64.8 0.0 copy-done.2
  64.8 0.0 copy-done.3
  64.8 0.0 copy-done.4
  64.8 0.0 copy-done.5
  64.8 0.0 collective-permute-done.11.refs_11_
  64.8 0.0 collective-permute-done.12.refs_12_
  64.8 0.0 collective-permute-done.13.refs_13_
  64.8 0.0 collective-permute-done.14.refs_14_
  64.9 1.6 %collective-permute-done.15.refs_15_ = f32[32,4096]{1,0:T(8,128)} collective-permute-done((f32[32,4096]{1,0:T(8,128)S(1)}, f32[32,4096]{1,0:T(8,128)}, u32[]{:S(2)}, u32[]{:S(2)}) %collective-permute-start.15) | collective-permute-done | bytes 524320 | tf_op jit(solution)/shard_map/ppermute | solution.py:224
  66.4 8.9 %products.1 = (bf16[512,4096]{1,0:T(8,128)(2,1)}, bf16[512,4096]{1,0:T(8,128)(2,1)}, f32[32,40,128]{2,1,0:T(8,128)S(1)}) custom-call(s32[1]{0:T(128)} %bitcast.me, f32[32,4096]{1,0:T(8,128)} %copy-done, f32[32,4096]{1,0:T(8,128)} %copy-done.1, f32[32,4096]{1,0:T(8,128)} %copy-done.2, f32[32,4096]{1,0:T(8,128)} %collective-permute-done.3.refs_3_, ...), custom_call_target="tpu_custom_call" | custom-call | tf_op jit(solution)/shard_map/products/pallas_call | solution.py:101
  75.3 28.5 %all_to_all.10 = f32[32,40,128]{2,1,0:T(8,128)S(1)} all-to-all(f32[32,40,128]{2,1,0:T(8,128)S(1)} %get-tuple-element.8), channel_id=1, replica_groups=mesh['row'=32,'col'=16] {'row'}, dimensions={0} | all-to-all | bytes 1310720 | tf_op jit(solution)/shard_map/all_to_all | solution.py:239
  103.8 0.1 reduce_sum.9
  103.9 22.4 %all_to_all.11.mine = f32[32,40,128]{2,1,0:T(8,128)S(1)} all-to-all(f32[32,40,128]{2,1,0:T(8,128)S(1)} %broadcast_in_dim.2), channel_id=1, replica_groups=mesh['row'=32,'col'=16] {'row'}, dimensions={0} | all-to-all | bytes 1310720 | tf_op jit(solution)/shard_map/all_to_all | solution.py:240
  126.4 7.0 %collective-permute-start.16 = (f32[32,24,128]{2,1,0:T(8,128)S(1)}, f32[32,24,128]{2,1,0:T(8,128)S(1)}, u32[]{:S(2)}, u32[]{:S(2)}) collective-permute-start(f32[32,24,128]{2,1,0:T(8,128)S(1)} %slice.14), channel_id=1, source_target_pairs={{0,1},{1,0},{2,3},{3,2},{4,5},{5,4},{6,7},{7,6},{8,9},{9,8},{10,11... | collective-permute-start | bytes 1179656 | tf_op jit(solution)/shard_map/ppermute | solution.py:224
  133.4 1.1 collective-permute-done.16.other
  134.5 10.6 %finish.1 = f32[4096,128]{1,0:T(8,128)} custom-call(s32[1]{0:T(128)} %bitcast.me, f32[32,40,128]{2,1,0:T(8,128)S(1)} %all_to_all.11.mine, f32[32,24,128]{2,1,0:T(8,128)S(1)} %collective-permute-done.16.other, f32[4096,128]{1,0:T(8,128)} %c_hbm.1, bf16[512,4096]{1,0:T(8,128)(2,1)} %get-tuple-element.9.vhi_hbm, bf16[512,4096]{1,0:T(8,128)(2,1)} %get-tuple-element.10.vlo_hbm), custom_call_target="tpu_custom_call" | custom-call | tf_op jit(solution)/shard_map/finish/pallas_call | solution.py:189
  (4 shorter events, 0.1 us)
Async XLA Ops:
  1.1 15.3 %collective-permute-start = (f32[16,4096]{1,0:T(8,128)S(1)}, f32[16,4096]{1,0:T(8,128)S(1)}, u32[]{:S(2)}, u32[]{:S(2)}) collective-permute-start(f32[16,4096]{1,0:T(8,128)S(1)} %get-tuple-element.12), channel_id=1, source_target_pairs={{0,2},{1,15},{2,0},{3,5},{4,6},{5,3},{6,4},{7,9},{8,10},{9,7},{10,... | collective-permute-start | bytes 786440 | tf_op jit(solution)/shard_map/ppermute | solution.py:216
  12.6 8.3 %collective-permute-start.1 = (f32[16,4096]{1,0:T(8,128)S(1)}, f32[16,4096]{1,0:T(8,128)S(1)}, u32[]{:S(2)}, u32[]{:S(2)}) collective-permute-start(f32[16,4096]{1,0:T(8,128)S(1)} %get-tuple-element.11), channel_id=1, source_target_pairs={{0,2},{1,15},{2,0},{3,5},{4,6},{5,3},{6,4},{7,9},{8,10},{9,7},{10,... | collective-permute-start | bytes 786440 | tf_op jit(solution)/shard_map/ppermute | solution.py:216
  16.4 45.1 %copy-start = (f32[32,4096]{1,0:T(8,128)}, f32[32,4096]{1,0:T(8,128)S(1)}, u32[]{:S(2)}) copy-start(f32[32,4096]{1,0:T(8,128)S(1)} %pad_maximum_fusion.refs_0_) | copy-start | bytes 1572868
  16.4 10.2 %collective-permute-start.2 = (f32[32,4096]{1,0:T(8,128)S(1)}, f32[32,4096]{1,0:T(8,128)S(1)}, u32[]{:S(2)}, u32[]{:S(2)}) collective-permute-start(f32[32,4096]{1,0:T(8,128)S(1)} %pad_maximum_fusion.refs_0_), channel_id=1, source_target_pairs={{0,14},{1,3},{2,4},{3,1},{4,2},{5,7},{6,8},{7,5},{8,6},{9,11},{10,... | collective-permute-start | bytes 1572872 | tf_op jit(solution)/shard_map/ppermute | solution.py:216
  20.9 43.8 %copy-start.1 = (f32[32,4096]{1,0:T(8,128)}, f32[32,4096]{1,0:T(8,128)S(1)}, u32[]{:S(2)}) copy-start(f32[32,4096]{1,0:T(8,128)S(1)} %pad_maximum_fusion.1.refs_1_) | copy-start | bytes 1572868
  21.0 11.4 %collective-permute-start.3 = (f32[32,4096]{1,0:T(8,128)S(1)}, f32[32,4096]{1,0:T(8,128)}, u32[]{:S(2)}, u32[]{:S(2)}) collective-permute-start(f32[32,4096]{1,0:T(8,128)S(1)} %pad_maximum_fusion.1.refs_1_), channel_id=1, source_target_pairs={{0,14},{1,3},{2,4},{3,1},{4,2},{5,7},{6,8},{7,5},{8,6},{9,11},{10,... | collective-permute-start | bytes 1572872 | tf_op jit(solution)/shard_map/ppermute | solution.py:216
  26.6 38.2 %copy-start.2 = (f32[32,4096]{1,0:T(8,128)}, f32[32,4096]{1,0:T(8,128)S(1)}, u32[]{:S(2)}) copy-start(f32[32,4096]{1,0:T(8,128)S(1)} %collective-permute-done.2.refs_2_) | copy-start | bytes 1572868
  26.6 18.0 %collective-permute-start.4 = (f32[32,4096]{1,0:T(8,128)S(1)}, f32[32,4096]{1,0:T(8,128)S(1)}, u32[]{:S(2)}, u32[]{:S(2)}) collective-permute-start(f32[32,4096]{1,0:T(8,128)S(1)} %collective-permute-done.2.refs_2_), channel_id=1, source_target_pairs={{0,2},{1,15},{2,0},{3,5},{4,6},{5,3},{6,4},{7,9},{8,10},{9,7},{10,... | collective-permute-start | bytes 1572872 | tf_op jit(solution)/shard_map/ppermute | solution.py:216
  32.3 16.0 %collective-permute-start.5 = (f32[32,4096]{1,0:T(8,128)}, f32[32,4096]{1,0:T(8,128)S(1)}, u32[]{:S(2)}, u32[]{:S(2)}) collective-permute-start(f32[32,4096]{1,0:T(8,128)} %collective-permute-done.3.refs_3_), channel_id=1, source_target_pairs={{0,2},{1,15},{2,0},{3,5},{4,6},{5,3},{6,4},{7,9},{8,10},{9,7},{10,... | collective-permute-start | bytes 1572872 | tf_op jit(solution)/shard_map/ppermute | solution.py:216
  36.9 13.4 %collective-permute-start.8 = (f32[32,4096]{1,0:T(8,128)S(1)}, f32[32,4096]{1,0:T(8,128)S(1)}, u32[]{:S(2)}, u32[]{:S(2)}) collective-permute-start(f32[32,4096]{1,0:T(8,128)S(1)} %pad_maximum_fusion.refs_0_), channel_id=1, source_target_pairs={{0,1},{1,0},{2,3},{3,2},{4,5},{5,4},{6,7},{7,6},{8,9},{9,8},{10,11... | collective-permute-start | bytes 1572872 | tf_op jit(solution)/shard_map/ppermute | solution.py:224
  40.3 14.8 %collective-permute-start.9 = (f32[32,4096]{1,0:T(8,128)S(1)}, f32[32,4096]{1,0:T(8,128)S(1)}, u32[]{:S(2)}, u32[]{:S(2)}) collective-permute-start(f32[32,4096]{1,0:T(8,128)S(1)} %pad_maximum_fusion.1.refs_1_), channel_id=1, source_target_pairs={{0,1},{1,0},{2,3},{3,2},{4,5},{5,4},{6,7},{7,6},{8,9},{9,8},{10,11... | collective-permute-start | bytes 1572872 | tf_op jit(solution)/shard_map/ppermute | solution.py:224
  42.2 14.8 %collective-permute-start.10 = (f32[32,4096]{1,0:T(8,128)S(1)}, f32[32,4096]{1,0:T(8,128)S(1)}, u32[]{:S(2)}, u32[]{:S(2)}) collective-permute-start(f32[32,4096]{1,0:T(8,128)S(1)} %collective-permute-done.2.refs_2_), channel_id=1, source_target_pairs={{0,1},{1,0},{2,3},{3,2},{4,5},{5,4},{6,7},{7,6},{8,9},{9,8},{10,11... | collective-permute-start | bytes 1572872 | tf_op jit(solution)/shard_map/ppermute | solution.py:224
  44.7 14.8 %collective-permute-start.6 = (f32[32,4096]{1,0:T(8,128)S(1)}, f32[32,4096]{1,0:T(8,128)S(1)}, u32[]{:S(2)}, u32[]{:S(2)}) collective-permute-start(f32[32,4096]{1,0:T(8,128)S(1)} %collective-permute-done.4.refs_4_), channel_id=1, source_target_pairs={{0,14},{1,3},{2,4},{3,1},{4,2},{5,7},{6,8},{7,5},{8,6},{9,11},{10,... | collective-permute-start | bytes 1572872 | tf_op jit(solution)/shard_map/ppermute | solution.py:216
  48.3 13.1 %collective-permute-start.7 = (f32[32,4096]{1,0:T(8,128)S(1)}, f32[32,4096]{1,0:T(8,128)S(1)}, u32[]{:S(2)}, u32[]{:S(2)}) collective-permute-start(f32[32,4096]{1,0:T(8,128)S(1)} %collective-permute-done.5.refs_5_), channel_id=1, source_target_pairs={{0,14},{1,3},{2,4},{3,1},{4,2},{5,7},{6,8},{7,5},{8,6},{9,11},{10,... | collective-permute-start | bytes 1572872 | tf_op jit(solution)/shard_map/ppermute | solution.py:216
  50.3 14.5 %copy-start.3 = (f32[32,4096]{1,0:T(8,128)}, f32[32,4096]{1,0:T(8,128)S(1)}, u32[]{:S(2)}) copy-start(f32[32,4096]{1,0:T(8,128)S(1)} %collective-permute-done.8.refs_8_) | copy-start | bytes 1572868
  50.3 14.6 %collective-permute-start.11 = (f32[32,4096]{1,0:T(8,128)}, f32[32,4096]{1,0:T(8,128)}, u32[]{:S(2)}, u32[]{:S(2)}) collective-permute-start(f32[32,4096]{1,0:T(8,128)} %collective-permute-done.3.refs_3_), channel_id=1, source_target_pairs={{0,1},{1,0},{2,3},{3,2},{4,5},{5,4},{6,7},{7,6},{8,9},{9,8},{10,11... | collective-permute-start | bytes 1572872 | tf_op jit(solution)/shard_map/ppermute | solution.py:224
  55.1 9.7 %copy-start.4 = (f32[32,4096]{1,0:T(8,128)}, f32[32,4096]{1,0:T(8,128)S(1)}, u32[]{:S(2)}) copy-start(f32[32,4096]{1,0:T(8,128)S(1)} %collective-permute-done.9.refs_9_) | copy-start | bytes 1572868
  55.1 9.7 %collective-permute-start.12 = (f32[32,4096]{1,0:T(8,128)S(1)}, f32[32,4096]{1,0:T(8,128)S(1)}, u32[]{:S(2)}, u32[]{:S(2)}) collective-permute-start(f32[32,4096]{1,0:T(8,128)S(1)} %collective-permute-done.4.refs_4_), channel_id=1, source_target_pairs={{0,1},{1,0},{2,3},{3,2},{4,5},{5,4},{6,7},{7,6},{8,9},{9,8},{10,11... | collective-permute-start | bytes 1572872 | tf_op jit(solution)/shard_map/ppermute | solution.py:224
  57.0 7.8 %copy-start.5 = (f32[32,4096]{1,0:T(8,128)}, f32[32,4096]{1,0:T(8,128)S(1)}, u32[]{:S(2)}) copy-start(f32[32,4096]{1,0:T(8,128)S(1)} %collective-permute-done.10.refs_10_) | copy-start | bytes 1572868
  57.1 7.8 %collective-permute-start.13 = (f32[32,4096]{1,0:T(8,128)S(1)}, f32[32,4096]{1,0:T(8,128)S(1)}, u32[]{:S(2)}, u32[]{:S(2)}) collective-permute-start(f32[32,4096]{1,0:T(8,128)S(1)} %collective-permute-done.5.refs_5_), channel_id=1, source_target_pairs={{0,1},{1,0},{2,3},{3,2},{4,5},{5,4},{6,7},{7,6},{8,9},{9,8},{10,11... | collective-permute-start | bytes 1572872 | tf_op jit(solution)/shard_map/ppermute | solution.py:224
  59.5 5.4 %collective-permute-start.14 = (f32[32,4096]{1,0:T(8,128)S(1)}, f32[32,4096]{1,0:T(8,128)}, u32[]{:S(2)}, u32[]{:S(2)}) collective-permute-start(f32[32,4096]{1,0:T(8,128)S(1)} %collective-permute-done.6.refs_6_), channel_id=1, source_target_pairs={{0,1},{1,0},{2,3},{3,2},{4,5},{5,4},{6,7},{7,6},{8,9},{9,8},{10,11... | collective-permute-start | bytes 1572872 | tf_op jit(solution)/shard_map/ppermute | solution.py:224
  61.4 5.0 %collective-permute-start.15 = (f32[32,4096]{1,0:T(8,128)S(1)}, f32[32,4096]{1,0:T(8,128)}, u32[]{:S(2)}, u32[]{:S(2)}) collective-permute-start(f32[32,4096]{1,0:T(8,128)S(1)} %collective-permute-done.7.refs_7_), channel_id=1, source_target_pairs={{0,1},{1,0},{2,3},{3,2},{4,5},{5,4},{6,7},{7,6},{8,9},{9,8},{10,11... | collective-permute-start | bytes 1572872 | tf_op jit(solution)/shard_map/ppermute | solution.py:224
  126.4 8.2 %collective-permute-start.16 = (f32[32,24,128]{2,1,0:T(8,128)S(1)}, f32[32,24,128]{2,1,0:T(8,128)S(1)}, u32[]{:S(2)}, u32[]{:S(2)}) collective-permute-start(f32[32,24,128]{2,1,0:T(8,128)S(1)} %slice.14), channel_id=1, source_target_pairs={{0,1},{1,0},{2,3},{3,2},{4,5},{5,4},{6,7},{7,6},{8,9},{9,8},{10,11... | collective-permute-start | bytes 1179656 | tf_op jit(solution)/shard_map/ppermute | solution.py:224

commit v6 on v5

v6 whole, which is shorter than its diff:
```python
import jax
import jax.numpy as jnp
from jax import lax
from jax.experimental import pallas as pl
from jax.experimental.pallas import tpu as pltpu
from jax.sharding import PartitionSpec as P

F32 = jnp.float32
BF16 = jnp.bfloat16
CHIPS = 8
ROWS = 4096
COLS = 128
NV = 512
PARTS = tuple(pl.ds(first, 1024) for first in range(0, ROWS, 1024))
VMEM = 32 * 1024 * 1024
ARRIVAL = ((0, 1), (-1, -2), (2, 3), (-3, -4))


def split(value):
    high = value.astype(BF16)
    low = (value - high.astype(F32)).astype(BF16)
    return high, low


def nt(left, right):
    return lax.dot_general(left, right, (((1,), (1,)), ((), ())), preferred_element_type=F32)


def nn(left, right):
    return lax.dot_general(left, right, (((1,), (0,)), ((), ())), preferred_element_type=F32)


def hidot(left, right):
    return jnp.dot(left, right, precision=lax.Precision.HIGHEST, preferred_element_type=F32)


def assemble(me, index, piece, vhi, vlo):
    chip, core = me // 2, me % 2
    turn = 1 - 2 * ((chip + core) % 2)
    swapped, arrival, block = index // 8, index % 8 // 2, index % 2
    for half in range(2):
        step = ARRIVAL[arrival][half] * (1 - 2 * swapped)
        source = (chip + turn * step + CHIPS) % CHIPS
        column = block * 256 + source * 32 + (1 - core if swapped else core) * 16
        high, low = split(piece[half * 16 : half * 16 + 16, :])
        at = pl.ds(pl.multiple_of(column, 16), 16)
        vhi[at, :] = high
        vlo[at, :] = low


def products_kernel(me, *refs):
    pieces = refs[:16]
    c_hbm, vhi_hbm, vlo_hbm, out, raw, c_ref, vhi, vlo, sums, come, gone, sent = refs[16:]
    core = me[0] % 2
    incoming = [pltpu.make_async_copy(piece, raw.at[n], come.at[n]) for n, piece in enumerate(pieces)]
    for index, at in enumerate(PARTS):
        incoming.append(pltpu.make_async_copy(c_hbm.at[at], c_ref.at[at], come.at[16 + index]))
    for copy in incoming:
        copy.start()
    for n in sorted(range(16), key=lambda n: -(n % 8)):
        incoming[n].wait()
        assemble(me[0], n, raw.at[n], vhi, vlo)
    outgoing = []
    for index, at in enumerate(PARTS):
        for which, (here, there) in enumerate(((vhi, vhi_hbm), (vlo, vlo_hbm))):
            outgoing.append(pltpu.make_async_copy(here.at[:, at], there.at[:, at], gone.at[index, which]))
            outgoing[-1].start()
    for copy in incoming[16:]:
        copy.wait()
    chi, clo = split(c_ref[...])
    both = nn(vhi[...], jnp.concatenate([chi, clo], axis=1))
    proj = both[:, :COLS] + both[:, COLS:] + nn(vlo[...], chi)
    sums[:, :16, :] = proj.reshape(32, 16, COLS)
    outgoing.append(pltpu.make_async_copy(sums.at[:, :16, :], out.at[:, :16, :], sent.at[0]))
    outgoing[-1].start()

    own = pl.ds(pl.multiple_of(core * 256, 256), 256)
    strip = pl.ds(pl.multiple_of(core * 128, 128), 128)
    mixed = nt(vhi[own, :], vlo[own, :])
    square = nt(vhi[own, :], vhi[own, :]) + mixed + mixed.T
    stacked = nt(jnp.concatenate([vhi[strip, :], vlo[strip, :]], axis=0), vhi[256:, :])
    cross = stacked[:128] + stacked[128:] + nt(vhi[strip, :], vlo[256:, :])
    parts = [square[:128, :128], square[:128, 128:], square[128:, 128:], cross[:, :128], cross[:, 128:]]
    parts.append(jnp.zeros((128, 128), F32))
    sums[:, 16:, :] = jnp.concatenate(parts, axis=0).reshape(32, 24, COLS)
    outgoing.append(pltpu.make_async_copy(sums.at[:, 16:, :], out.at[:, 16:, :], sent.at[1]))
    outgoing[-1].start()
    for copy in outgoing:
        copy.wait()


def products(me, pieces, current):
    return pl.pallas_call(
        products_kernel,
        in_specs=[pl.BlockSpec(memory_space=pltpu.SMEM)] + [pl.BlockSpec(memory_space=pl.ANY)] * 17,
        out_specs=[pl.BlockSpec(memory_space=pl.ANY)] * 3,
        out_shape=[
            pltpu.HBM((NV, ROWS), BF16),
            pltpu.HBM((NV, ROWS), BF16),
            jax.ShapeDtypeStruct((32, 40, COLS), F32),
        ],
        scratch_shapes=[
            pltpu.VMEM((16, 32, ROWS), F32),
            pltpu.VMEM((ROWS, COLS), F32),
            pltpu.VMEM((NV, ROWS), BF16),
            pltpu.VMEM((NV, ROWS), BF16),
            pltpu.VMEM((32, 40, COLS), F32),
            pltpu.SemaphoreType.DMA((16 + len(PARTS),)),
            pltpu.SemaphoreType.DMA((len(PARTS), 2)),
            pltpu.SemaphoreType.DMA((2,)),
        ],
        compiler_params=pltpu.CompilerParams(vmem_limit_bytes=VMEM),
        name="products",
    )(me, *pieces, current)


def invert_unit(nilpot):
    row = lax.broadcasted_iota(jnp.int32, (128, 128), 0)
    col = lax.broadcasted_iota(jnp.int32, (128, 128), 1)
    eye = (row == col).astype(F32)
    near = [jnp.where(row // 4 == col // 4, n, 0.0) for n in nilpot]
    square = [hidot(n, n) for n in near]
    inverse = [hidot(eye - n, eye + s) for n, s in zip(near, square)]
    size = 4
    while size < 128:
        pair = (row // (2 * size) == col // (2 * size)) & (row // size != col // size)
        right = [hidot(jnp.where(pair, n, 0.0), r) for n, r in zip(nilpot, inverse)]
        inverse = [r - hidot(r, t) for r, t in zip(inverse, right)]
        size *= 2
    return inverse


def invert_kernel(mine, out, part, come):
    copy = pltpu.make_async_copy(mine.at[:, 16:, :], part, come)
    copy.start()
    copy.wait()
    flat = part[...].reshape(768, 128)
    gram = [flat[:128], flat[128:256], flat[256:384]]
    row = lax.broadcasted_iota(jnp.int32, (128, 128), 0)
    col = lax.broadcasted_iota(jnp.int32, (128, 128), 1)
    diagonal = [jnp.where(row == col, gram[i], 0.0) for i in (0, 2)]
    scale = [2.0 / jnp.sum(d, axis=1, keepdims=True) for d in diagonal]
    across = [2.0 / jnp.sum(d, axis=0, keepdims=True) for d in diagonal]
    upper, lower = invert_unit([jnp.where(row < col, gram[2 * i] * scale[i], 0.0) for i in range(2)])
    corner = hidot(upper, hidot(gram[1] * scale[0], lower))
    out[:128, :] = upper * across[0]
    out[128:256, :] = -corner * across[1]
    out[256:384, :] = lower * across[1]
    out[384:, :] = flat[384:640]


def invert(mine):
    return pl.pallas_call(
        invert_kernel,
        in_specs=[pl.BlockSpec(memory_space=pl.ANY)],
        out_specs=pl.BlockSpec(memory_space=pltpu.VMEM),
        out_shape=jax.ShapeDtypeStruct((640, 128), F32),
        scratch_shapes=[pltpu.VMEM((32, 24, COLS), F32), pltpu.SemaphoreType.DMA],
        compiler_params=pltpu.CompilerParams(vmem_limit_bytes=VMEM),
        name="invert",
    )(mine)


def coefficients(me, project, here, there):
    first_core = me[0] % 2 == 0
    project = project[...].reshape(NV, COLS)
    inverse, cross = [], []
    for block in range(2):
        data = jnp.where(first_core == (block == 0), here[...], there[...])
        upper = jnp.concatenate([data[:128], data[128:256]], axis=1)
        lower = jnp.concatenate([jnp.zeros((128, 128), F32), data[256:384]], axis=1)
        inverse.append(jnp.concatenate([upper, lower], axis=0))
        cross.append(jnp.concatenate([data[384:512], data[512:]], axis=1))
    later = hidot(inverse[1], project[256:])
    earlier = hidot(inverse[0], project[:256] - hidot(jnp.concatenate(cross, axis=0), later))
    return split(jnp.concatenate([earlier, later], axis=0).T)


def finish_kernel(me, mine, here, there, c_hbm, vhi_hbm, vlo_hbm, out, project, first, second, c_ref, vhi, vlo, done, small, come, gone):
    needed = ((mine.at[:, :16, :], project), (here, first), (there, second))
    needed = [pltpu.make_async_copy(*pair, small.at[which]) for which, pair in enumerate(needed)]
    for copy in needed:
        copy.start()
    copies = []
    for index, at in enumerate(PARTS):
        pairs = ((vhi_hbm.at[:, at], vhi.at[:, at]), (vlo_hbm.at[:, at], vlo.at[:, at]), (c_hbm.at[at], c_ref.at[at]))
        copies.append([pltpu.make_async_copy(*pair, come.at[index, which]) for which, pair in enumerate(pairs)])
        for copy in copies[-1]:
            copy.start()
    for copy in needed:
        copy.wait()
    xhi, xlo = coefficients(me, project, first, second)
    both = jnp.concatenate([xhi, xlo], axis=0)
    writes = []
    for index, at in enumerate(PARTS):
        for copy in copies[index]:
            copy.wait()
        wide = nn(both, vhi[:, at])
        change = wide[:COLS] + wide[COLS:] + nn(xhi, vlo[:, at])
        done[at, :] = c_ref[at, :] - change.T
        writes.append(pltpu.make_async_copy(done.at[at], out.at[at], gone.at[index]))
        writes[-1].start()
    for write in writes:
        write.wait()


def finish(me, mine, here, there, current, vhi, vlo):
    return pl.pallas_call(
        finish_kernel,
        in_specs=[pl.BlockSpec(memory_space=pltpu.SMEM)]
        + [pl.BlockSpec(memory_space=pl.ANY)] * 6,
        out_specs=pl.BlockSpec(memory_space=pl.ANY),
        out_shape=jax.ShapeDtypeStruct((ROWS, COLS), F32),
        scratch_shapes=[
            pltpu.VMEM((32, 16, COLS), F32),
            pltpu.VMEM((640, 128), F32),
            pltpu.VMEM((640, 128), F32),
            pltpu.VMEM((ROWS, COLS), F32),
            pltpu.VMEM((NV, ROWS), BF16),
            pltpu.VMEM((NV, ROWS), BF16),
            pltpu.VMEM((ROWS, COLS), F32),
            pltpu.SemaphoreType.DMA((3,)),
            pltpu.SemaphoreType.DMA((len(PARTS), 3)),
            pltpu.SemaphoreType.DMA((len(PARTS),)),
        ],
        compiler_params=pltpu.CompilerParams(vmem_limit_bytes=VMEM),
        name="finish",
    )(me, mine, here, there, current, vhi, vlo)


def exchange(value, side):
    perm = []
    for chip in range(CHIPS):
        for core in range(2):
            turn = 1 if (chip + core) % 2 == 0 else -1
            target = (chip + side * turn) % CHIPS
            perm.append((chip * 2 + core, target * 2 + core))
    return lax.ppermute(value, "col", perm)


def in_hbm(value):
    return pltpu.with_memory_space_constraint(value, pltpu.HBM)


def swap_cores(value):
    return lax.ppermute(value, "col", [(i, i ^ 1) for i in range(2 * CHIPS)])


def shards(eigvecs, householder):
    me = lax.axis_index("col").reshape(1)
    own = householder.transpose(0, 2, 1)
    chains = [own[0], own[1]]
    chains = [jnp.concatenate([piece, exchange(piece, 1)], axis=0) for piece in chains]
    pieces = list(chains)
    for side in (-1, 1, -1):
        chains = [exchange(piece, side) for piece in chains]
        pieces += chains
    pieces += [swap_cores(piece) for piece in pieces]

    vhi, vlo, partial = products(me, [in_hbm(piece) if n % 8 < 4 else piece for n, piece in enumerate(pieces)], in_hbm(eigvecs))
    summed = lax.all_to_all(partial, "row", 0, 0, tiled=True).sum(axis=0)
    mine = lax.all_to_all(jnp.broadcast_to(summed[None], (32, 40, COLS)), "row", 0, 0, tiled=True)
    here = invert(mine)
    return finish(me, mine, here, swap_cores(here), in_hbm(eigvecs), in_hbm(vhi), in_hbm(vlo))


def solution(mesh):
    in_specs = (P("row", "col"), P(None, "row", "col"))
    out_specs = P("row", "col")
    return jax.shard_map(shards, mesh=mesh, in_specs=in_specs, out_specs=out_specs, check_vma=False)
```

time: 146 us -> 147 us (level)
    pallas_call x1, Pallas kernels: 10.6 us -> 6.04 us  [finish(): pl.pallas_call(finish_kernel, in_specs=[pl.BlockSpec(memory_space=pltpu.S...]
    pallas_call x0 -> x1, Pallas kernels: none -> 3.38 us  [invert(): pl.pallas_call(invert_kernel, in_specs=[pl.BlockSpec(memory_space=pl.ANY)...]
    all_to_all x1, blocking collectives: 28.5 us -> 26.3 us  [shards(): summed = lax.all_to_all(partial, 'row', 0, 0, tiled=True).sum(axis=0)]
    pallas_call x1, Pallas kernels: 8.87 us -> 11 us  [products(): pl.pallas_call(products_kernel, in_specs=[pl.BlockSpec(memory_space=pltpu...]
    all_to_all x1, blocking collectives: 22.4 us -> 24.6 us  [shards(): lax.all_to_all(jnp.broadcast_to(summed[None], (32, 40, COLS)), 'row', 0,...]
where the time goes in v6:
time: 147 us; the launch traced here: 146 us
  starting transfers between devices  60.9 us (41%)
  blocking collectives  50.9 us (35%)
  Pallas kernels  20.4 us (14%)
  waiting for transfers between devices  12.1 us (8%)
    ppermute x8, starting transfers between devices, exchange(): return lax.ppermute(value, 'col', perm)  31.9 us
    ppermute x9, starting transfers between devices, swap_cores(): return lax.ppermute(value, 'col', [(i, i ^ 1) for i in range(2 * CHIPS)])  28.9 us
    all_to_all x1, blocking collectives, shards(): summed = lax.all_to_all(partial, 'row', 0, 0, tiled=True).sum(axis=0)  26.3 us
    all_to_all x1, blocking collectives, shards(): lax.all_to_all(jnp.broadcast_to(summed[None], (32, 40, COLS)), 'row', 0,...  24.6 us
    pallas_call x1, Pallas kernels, products(): pl.pallas_call(products_kernel, in_specs=[pl.BlockSpec(memory_space=pltpu...  11 us
    ppermute x8, waiting for transfers between devices, exchange(): return lax.ppermute(value, 'col', perm)  9.29 us
    pallas_call x1, Pallas kernels, finish(): pl.pallas_call(finish_kernel, in_specs=[pl.BlockSpec(memory_space=pltpu.S...  6.04 us
    pallas_call x1, Pallas kernels, invert(): pl.pallas_call(invert_kernel, in_specs=[pl.BlockSpec(memory_space=pl.ANY)...  3.38 us
  transfers between devices with their start and end apart: 17, of which 6 were waited for; matrix products, arithmetic and copies ran while one was open for 0% of the time, Pallas kernels for 0%

profile of v6, /device:TPU:1, one launch (start us, length us, event | category | flops | bytes accessed | tf_op | source)
XLA Modules:
  0.0 146.0 jit_solution(14232063196504678086)
XLA Ops:
  0.0 1.1 slice_bitcast_fusion
  1.1 11.5 %collective-permute-start = (f32[16,4096]{1,0:T(8,128)S(1)}, f32[16,4096]{1,0:T(8,128)S(1)}, u32[]{:S(2)}, u32[]{:S(2)}) collective-permute-start(f32[16,4096]{1,0:T(8,128)S(1)} %get-tuple-element.12), channel_id=1, source_target_pairs={{0,2},{1,15},{2,0},{3,5},{4,6},{5,3},{6,4},{7,9},{8,10},{9,7},{10,... | collective-permute-start | bytes 786440 | tf_op jit(solution)/shard_map/ppermute | solution.py:238
  12.6 1.9 %collective-permute-start.1 = (f32[16,4096]{1,0:T(8,128)S(1)}, f32[16,4096]{1,0:T(8,128)S(1)}, u32[]{:S(2)}, u32[]{:S(2)}) collective-permute-start(f32[16,4096]{1,0:T(8,128)S(1)} %get-tuple-element.11), channel_id=1, source_target_pairs={{0,2},{1,15},{2,0},{3,5},{4,6},{5,3},{6,4},{7,9},{8,10},{9,7},{10,... | collective-permute-start | bytes 786440 | tf_op jit(solution)/shard_map/ppermute | solution.py:238
  14.5 1.8 %collective-permute-done = f32[16,4096]{1,0:T(8,128)S(1)} collective-permute-done((f32[16,4096]{1,0:T(8,128)S(1)}, f32[16,4096]{1,0:T(8,128)S(1)}, u32[]{:S(2)}, u32[]{:S(2)}) %collective-permute-start) | collective-permute-done | bytes 262176 | tf_op jit(solution)/shard_map/ppermute | solution.py:238
  16.4 0.0 copy-start
  16.4 1.9 %collective-permute-start.2 = (f32[32,4096]{1,0:T(8,128)S(1)}, f32[32,4096]{1,0:T(8,128)S(1)}, u32[]{:S(2)}, u32[]{:S(2)}) collective-permute-start(f32[32,4096]{1,0:T(8,128)S(1)} %pad_maximum_fusion.refs_0_), channel_id=1, source_target_pairs={{0,14},{1,3},{2,4},{3,1},{4,2},{5,7},{6,8},{7,5},{8,6},{9,11},{10,... | collective-permute-start | bytes 1572872 | tf_op jit(solution)/shard_map/ppermute | solution.py:238
  18.3 2.6 %collective-permute-done.1 = f32[16,4096]{1,0:T(8,128)S(1)} collective-permute-done((f32[16,4096]{1,0:T(8,128)S(1)}, f32[16,4096]{1,0:T(8,128)S(1)}, u32[]{:S(2)}, u32[]{:S(2)}) %collective-permute-start.1) | collective-permute-done | bytes 262176 | tf_op jit(solution)/shard_map/ppermute | solution.py:238
  20.9 0.0 copy-start.1
  21.0 1.9 %collective-permute-start.3 = (f32[32,4096]{1,0:T(8,128)S(1)}, f32[32,4096]{1,0:T(8,128)}, u32[]{:S(2)}, u32[]{:S(2)}) collective-permute-start(f32[32,4096]{1,0:T(8,128)S(1)} %pad_maximum_fusion.1.refs_1_), channel_id=1, source_target_pairs={{0,14},{1,3},{2,4},{3,1},{4,2},{5,7},{6,8},{7,5},{8,6},{9,11},{10,... | collective-permute-start | bytes 1572872 | tf_op jit(solution)/shard_map/ppermute | solution.py:238
  22.9 3.7 %collective-permute-done.2.refs_2_ = f32[32,4096]{1,0:T(8,128)S(1)} collective-permute-done((f32[32,4096]{1,0:T(8,128)S(1)}, f32[32,4096]{1,0:T(8,128)S(1)}, u32[]{:S(2)}, u32[]{:S(2)}) %collective-permute-start.2) | collective-permute-done | bytes 524320 | tf_op jit(solution)/shard_map/ppermute | solution.py:238
  26.6 0.0 copy-start.2
  26.6 4.6 %collective-permute-start.4 = (f32[32,4096]{1,0:T(8,128)S(1)}, f32[32,4096]{1,0:T(8,128)S(1)}, u32[]{:S(2)}, u32[]{:S(2)}) collective-permute-start(f32[32,4096]{1,0:T(8,128)S(1)} %collective-permute-done.2.refs_2_), channel_id=1, source_target_pairs={{0,2},{1,15},{2,0},{3,5},{4,6},{5,3},{6,4},{7,9},{8,10},{9,7},{10,... | collective-permute-start | bytes 1572872 | tf_op jit(solution)/shard_map/ppermute | solution.py:238
  31.2 1.2 collective-permute-done.3.refs_3_
  32.3 4.6 %collective-permute-start.5 = (f32[32,4096]{1,0:T(8,128)}, f32[32,4096]{1,0:T(8,128)S(1)}, u32[]{:S(2)}, u32[]{:S(2)}) collective-permute-start(f32[32,4096]{1,0:T(8,128)} %collective-permute-done.3.refs_3_), channel_id=1, source_target_pairs={{0,2},{1,15},{2,0},{3,5},{4,6},{5,3},{6,4},{7,9},{8,10},{9,7},{10,... | collective-permute-start | bytes 1572872 | tf_op jit(solution)/shard_map/ppermute | solution.py:238
  36.9 3.4 %collective-permute-start.8 = (f32[32,4096]{1,0:T(8,128)S(1)}, f32[32,4096]{1,0:T(8,128)S(1)}, u32[]{:S(2)}, u32[]{:S(2)}) collective-permute-start(f32[32,4096]{1,0:T(8,128)S(1)} %pad_maximum_fusion.refs_0_), channel_id=1, source_target_pairs={{0,1},{1,0},{2,3},{3,2},{4,5},{5,4},{6,7},{7,6},{8,9},{9,8},{10,11... | collective-permute-start | bytes 1572872 | tf_op jit(solution)/shard_map/ppermute | solution.py:246
  40.3 1.9 %collective-permute-start.9 = (f32[32,4096]{1,0:T(8,128)S(1)}, f32[32,4096]{1,0:T(8,128)S(1)}, u32[]{:S(2)}, u32[]{:S(2)}) collective-permute-start(f32[32,4096]{1,0:T(8,128)S(1)} %pad_maximum_fusion.1.refs_1_), channel_id=1, source_target_pairs={{0,1},{1,0},{2,3},{3,2},{4,5},{5,4},{6,7},{7,6},{8,9},{9,8},{10,11... | collective-permute-start | bytes 1572872 | tf_op jit(solution)/shard_map/ppermute | solution.py:246
  42.2 2.4 %collective-permute-start.10 = (f32[32,4096]{1,0:T(8,128)S(1)}, f32[32,4096]{1,0:T(8,128)S(1)}, u32[]{:S(2)}, u32[]{:S(2)}) collective-permute-start(f32[32,4096]{1,0:T(8,128)S(1)} %collective-permute-done.2.refs_2_), channel_id=1, source_target_pairs={{0,1},{1,0},{2,3},{3,2},{4,5},{5,4},{6,7},{7,6},{8,9},{9,8},{10,11... | collective-permute-start | bytes 1572872 | tf_op jit(solution)/shard_map/ppermute | solution.py:246
  44.6 0.0 collective-permute-done.4.refs_4_
  44.7 3.6 %collective-permute-start.6 = (f32[32,4096]{1,0:T(8,128)S(1)}, f32[32,4096]{1,0:T(8,128)S(1)}, u32[]{:S(2)}, u32[]{:S(2)}) collective-permute-start(f32[32,4096]{1,0:T(8,128)S(1)} %collective-permute-done.4.refs_4_), channel_id=1, source_target_pairs={{0,14},{1,3},{2,4},{3,1},{4,2},{5,7},{6,8},{7,5},{8,6},{9,11},{10,... | collective-permute-start | bytes 1572872 | tf_op jit(solution)/shard_map/ppermute | solution.py:238
  48.3 0.0 collective-permute-done.5.refs_5_
  48.3 1.9 %collective-permute-start.7 = (f32[32,4096]{1,0:T(8,128)S(1)}, f32[32,4096]{1,0:T(8,128)S(1)}, u32[]{:S(2)}, u32[]{:S(2)}) collective-permute-start(f32[32,4096]{1,0:T(8,128)S(1)} %collective-permute-done.5.refs_5_), channel_id=1, source_target_pairs={{0,14},{1,3},{2,4},{3,1},{4,2},{5,7},{6,8},{7,5},{8,6},{9,11},{10,... | collective-permute-start | bytes 1572872 | tf_op jit(solution)/shard_map/ppermute | solution.py:238
  50.2 0.0 collective-permute-done.8.refs_8_
  50.3 0.0 copy-start.3
  50.3 4.8 %collective-permute-start.11 = (f32[32,4096]{1,0:T(8,128)}, f32[32,4096]{1,0:T(8,128)}, u32[]{:S(2)}, u32[]{:S(2)}) collective-permute-start(f32[32,4096]{1,0:T(8,128)} %collective-permute-done.3.refs_3_), channel_id=1, source_target_pairs={{0,1},{1,0},{2,3},{3,2},{4,5},{5,4},{6,7},{7,6},{8,9},{9,8},{10,11... | collective-permute-start | bytes 1572872 | tf_op jit(solution)/shard_map/ppermute | solution.py:246
  55.1 0.0 collective-permute-done.9.refs_9_
  55.1 0.0 copy-start.4
  55.1 1.9 %collective-permute-start.12 = (f32[32,4096]{1,0:T(8,128)S(1)}, f32[32,4096]{1,0:T(8,128)S(1)}, u32[]{:S(2)}, u32[]{:S(2)}) collective-permute-start(f32[32,4096]{1,0:T(8,128)S(1)} %collective-permute-done.4.refs_4_), channel_id=1, source_target_pairs={{0,1},{1,0},{2,3},{3,2},{4,5},{5,4},{6,7},{7,6},{8,9},{9,8},{10,11... | collective-permute-start | bytes 1572872 | tf_op jit(solution)/shard_map/ppermute | solution.py:246
  57.0 0.0 collective-permute-done.10.refs_10_
  57.0 0.0 copy-start.5
  57.1 2.4 %collective-permute-start.13 = (f32[32,4096]{1,0:T(8,128)S(1)}, f32[32,4096]{1,0:T(8,128)S(1)}, u32[]{:S(2)}, u32[]{:S(2)}) collective-permute-start(f32[32,4096]{1,0:T(8,128)S(1)} %collective-permute-done.5.refs_5_), channel_id=1, source_target_pairs={{0,1},{1,0},{2,3},{3,2},{4,5},{5,4},{6,7},{7,6},{8,9},{9,8},{10,11... | collective-permute-start | bytes 1572872 | tf_op jit(solution)/shard_map/ppermute | solution.py:246
  59.5 0.0 collective-permute-done.6.refs_6_
  59.5 1.9 %collective-permute-start.14 = (f32[32,4096]{1,0:T(8,128)S(1)}, f32[32,4096]{1,0:T(8,128)}, u32[]{:S(2)}, u32[]{:S(2)}) collective-permute-start(f32[32,4096]{1,0:T(8,128)S(1)} %collective-permute-done.6.refs_6_), channel_id=1, source_target_pairs={{0,1},{1,0},{2,3},{3,2},{4,5},{5,4},{6,7},{7,6},{8,9},{9,8},{10,11... | collective-permute-start | bytes 1572872 | tf_op jit(solution)/shard_map/ppermute | solution.py:246
  61.4 0.0 collective-permute-done.7.refs_7_
  61.4 0.0 copy-done
  61.4 3.3 %collective-permute-start.15 = (f32[32,4096]{1,0:T(8,128)S(1)}, f32[32,4096]{1,0:T(8,128)}, u32[]{:S(2)}, u32[]{:S(2)}) collective-permute-start(f32[32,4096]{1,0:T(8,128)S(1)} %collective-permute-done.7.refs_7_), channel_id=1, source_target_pairs={{0,1},{1,0},{2,3},{3,2},{4,5},{5,4},{6,7},{7,6},{8,9},{9,8},{10,11... | collective-permute-start | bytes 1572872 | tf_op jit(solution)/shard_map/ppermute | solution.py:246
  64.8 0.0 copy-done.1
  64.8 0.0 copy-done.2
  64.8 0.0 copy-done.3
  64.8 0.0 copy-done.4
  64.8 0.0 copy-done.5
  64.8 0.0 collective-permute-done.11.refs_11_
  64.8 0.0 collective-permute-done.12.refs_12_
  64.8 0.0 collective-permute-done.13.refs_13_
  64.8 0.0 collective-permute-done.14.refs_14_
  64.9 1.6 %collective-permute-done.15.refs_15_ = f32[32,4096]{1,0:T(8,128)} collective-permute-done((f32[32,4096]{1,0:T(8,128)S(1)}, f32[32,4096]{1,0:T(8,128)}, u32[]{:S(2)}, u32[]{:S(2)}) %collective-permute-start.15) | collective-permute-done | bytes 524320 | tf_op jit(solution)/shard_map/ppermute | solution.py:246
  66.4 11.0 %products.1 = (bf16[512,4096]{1,0:T(8,128)(2,1)}, bf16[512,4096]{1,0:T(8,128)(2,1)}, f32[32,40,128]{2,1,0:T(8,128)S(1)}) custom-call(s32[1]{0:T(128)} %bitcast.me, f32[32,4096]{1,0:T(8,128)} %copy-done, f32[32,4096]{1,0:T(8,128)} %copy-done.1, f32[32,4096]{1,0:T(8,128)} %copy-done.2, f32[32,4096]{1,0:T(8,128)} %collective-permute-done.3.refs_3_, ...), custom_call_target="tpu_custom_call" | custom-call | tf_op jit(solution)/shard_map/products/pallas_call | solution.py:93
  77.4 26.3 %all_to_all.10 = f32[32,40,128]{2,1,0:T(8,128)S(1)} all-to-all(f32[32,40,128]{2,1,0:T(8,128)S(1)} %get-tuple-element.8), channel_id=1, replica_groups=mesh['row'=32,'col'=16] {'row'}, dimensions={0} | all-to-all | bytes 1310720 | tf_op jit(solution)/shard_map/all_to_all | solution.py:261
  103.7 0.1 reduce_sum.9
  103.8 24.6 %all_to_all.11.mine = f32[32,40,128]{2,1,0:T(8,128)S(1)} all-to-all(f32[32,40,128]{2,1,0:T(8,128)S(1)} %broadcast_in_dim.2), channel_id=1, replica_groups=mesh['row'=32,'col'=16] {'row'}, dimensions={0} | all-to-all | bytes 1310720 | tf_op jit(solution)/shard_map/all_to_all | solution.py:262
  128.4 3.4 %invert.1.here = f32[640,128]{1,0:T(8,128)S(1)} custom-call(f32[32,40,128]{2,1,0:T(8,128)S(1)} %all_to_all.11.mine), custom_call_target="tpu_custom_call" | custom-call | tf_op jit(solution)/shard_map/invert/pallas_call | solution.py:153
  131.8 6.8 %collective-permute-start.16 = (f32[640,128]{1,0:T(8,128)S(1)}, f32[640,128]{1,0:T(8,128)S(1)}, u32[]{:S(2)}, u32[]{:S(2)}) collective-permute-start(f32[640,128]{1,0:T(8,128)S(1)} %invert.1.here), channel_id=1, source_target_pairs={{0,1},{1,0},{2,3},{3,2},{4,5},{5,4},{6,7},{7,6},{8,9},{9,8},{10,11... | collective-permute-start | bytes 983048 | tf_op jit(solution)/shard_map/ppermute | solution.py:246
  138.6 1.2 collective-permute-done.16.there
  139.8 6.0 %finish.1 = f32[4096,128]{1,0:T(8,128)} custom-call(s32[1]{0:T(128)} %bitcast.me, f32[32,40,128]{2,1,0:T(8,128)S(1)} %all_to_all.11.mine, f32[640,128]{1,0:T(8,128)S(1)} %invert.1.here, f32[640,128]{1,0:T(8,128)S(1)} %collective-permute-done.16.there, f32[4096,128]{1,0:T(8,128)} %c_hbm.1, bf16[512,4096]{1,0:T(8,128)(2,1)} %get-tuple-element.9.vhi_hbm, ...), custom_call_target="tpu_custom_call" | custom-call | tf_op jit(solution)/shard_map/finish/pallas_call | solution.py:208
  (3 shorter events, 0.1 us)
Async XLA Ops:
  1.1 15.3 %collective-permute-start = (f32[16,4096]{1,0:T(8,128)S(1)}, f32[16,4096]{1,0:T(8,128)S(1)}, u32[]{:S(2)}, u32[]{:S(2)}) collective-permute-start(f32[16,4096]{1,0:T(8,128)S(1)} %get-tuple-element.12), channel_id=1, source_target_pairs={{0,2},{1,15},{2,0},{3,5},{4,6},{5,3},{6,4},{7,9},{8,10},{9,7},{10,... | collective-permute-start | bytes 786440 | tf_op jit(solution)/shard_map/ppermute | solution.py:238
  12.6 8.3 %collective-permute-start.1 = (f32[16,4096]{1,0:T(8,128)S(1)}, f32[16,4096]{1,0:T(8,128)S(1)}, u32[]{:S(2)}, u32[]{:S(2)}) collective-permute-start(f32[16,4096]{1,0:T(8,128)S(1)} %get-tuple-element.11), channel_id=1, source_target_pairs={{0,2},{1,15},{2,0},{3,5},{4,6},{5,3},{6,4},{7,9},{8,10},{9,7},{10,... | collective-permute-start | bytes 786440 | tf_op jit(solution)/shard_map/ppermute | solution.py:238
  16.4 45.1 %copy-start = (f32[32,4096]{1,0:T(8,128)}, f32[32,4096]{1,0:T(8,128)S(1)}, u32[]{:S(2)}) copy-start(f32[32,4096]{1,0:T(8,128)S(1)} %pad_maximum_fusion.refs_0_) | copy-start | bytes 1572868
  16.4 10.2 %collective-permute-start.2 = (f32[32,4096]{1,0:T(8,128)S(1)}, f32[32,4096]{1,0:T(8,128)S(1)}, u32[]{:S(2)}, u32[]{:S(2)}) collective-permute-start(f32[32,4096]{1,0:T(8,128)S(1)} %pad_maximum_fusion.refs_0_), channel_id=1, source_target_pairs={{0,14},{1,3},{2,4},{3,1},{4,2},{5,7},{6,8},{7,5},{8,6},{9,11},{10,... | collective-permute-start | bytes 1572872 | tf_op jit(solution)/shard_map/ppermute | solution.py:238
  20.9 43.8 %copy-start.1 = (f32[32,4096]{1,0:T(8,128)}, f32[32,4096]{1,0:T(8,128)S(1)}, u32[]{:S(2)}) copy-start(f32[32,4096]{1,0:T(8,128)S(1)} %pad_maximum_fusion.1.refs_1_) | copy-start | bytes 1572868
  21.0 11.4 %collective-permute-start.3 = (f32[32,4096]{1,0:T(8,128)S(1)}, f32[32,4096]{1,0:T(8,128)}, u32[]{:S(2)}, u32[]{:S(2)}) collective-permute-start(f32[32,4096]{1,0:T(8,128)S(1)} %pad_maximum_fusion.1.refs_1_), channel_id=1, source_target_pairs={{0,14},{1,3},{2,4},{3,1},{4,2},{5,7},{6,8},{7,5},{8,6},{9,11},{10,... | collective-permute-start | bytes 1572872 | tf_op jit(solution)/shard_map/ppermute | solution.py:238
  26.6 38.2 %copy-start.2 = (f32[32,4096]{1,0:T(8,128)}, f32[32,4096]{1,0:T(8,128)S(1)}, u32[]{:S(2)}) copy-start(f32[32,4096]{1,0:T(8,128)S(1)} %collective-permute-done.2.refs_2_) | copy-start | bytes 1572868
  26.6 18.0 %collective-permute-start.4 = (f32[32,4096]{1,0:T(8,128)S(1)}, f32[32,4096]{1,0:T(8,128)S(1)}, u32[]{:S(2)}, u32[]{:S(2)}) collective-permute-start(f32[32,4096]{1,0:T(8,128)S(1)} %collective-permute-done.2.refs_2_), channel_id=1, source_target_pairs={{0,2},{1,15},{2,0},{3,5},{4,6},{5,3},{6,4},{7,9},{8,10},{9,7},{10,... | collective-permute-start | bytes 1572872 | tf_op jit(solution)/shard_map/ppermute | solution.py:238
  32.3 16.0 %collective-permute-start.5 = (f32[32,4096]{1,0:T(8,128)}, f32[32,4096]{1,0:T(8,128)S(1)}, u32[]{:S(2)}, u32[]{:S(2)}) collective-permute-start(f32[32,4096]{1,0:T(8,128)} %collective-permute-done.3.refs_3_), channel_id=1, source_target_pairs={{0,2},{1,15},{2,0},{3,5},{4,6},{5,3},{6,4},{7,9},{8,10},{9,7},{10,... | collective-permute-start | bytes 1572872 | tf_op jit(solution)/shard_map/ppermute | solution.py:238
  36.9 13.4 %collective-permute-start.8 = (f32[32,4096]{1,0:T(8,128)S(1)}, f32[32,4096]{1,0:T(8,128)S(1)}, u32[]{:S(2)}, u32[]{:S(2)}) collective-permute-start(f32[32,4096]{1,0:T(8,128)S(1)} %pad_maximum_fusion.refs_0_), channel_id=1, source_target_pairs={{0,1},{1,0},{2,3},{3,2},{4,5},{5,4},{6,7},{7,6},{8,9},{9,8},{10,11... | collective-permute-start | bytes 1572872 | tf_op jit(solution)/shard_map/ppermute | solution.py:246
  40.3 14.8 %collective-permute-start.9 = (f32[32,4096]{1,0:T(8,128)S(1)}, f32[32,4096]{1,0:T(8,128)S(1)}, u32[]{:S(2)}, u32[]{:S(2)}) collective-permute-start(f32[32,4096]{1,0:T(8,128)S(1)} %pad_maximum_fusion.1.refs_1_), channel_id=1, source_target_pairs={{0,1},{1,0},{2,3},{3,2},{4,5},{5,4},{6,7},{7,6},{8,9},{9,8},{10,11... | collective-permute-start | bytes 1572872 | tf_op jit(solution)/shard_map/ppermute | solution.py:246
  42.2 14.8 %collective-permute-start.10 = (f32[32,4096]{1,0:T(8,128)S(1)}, f32[32,4096]{1,0:T(8,128)S(1)}, u32[]{:S(2)}, u32[]{:S(2)}) collective-permute-start(f32[32,4096]{1,0:T(8,128)S(1)} %collective-permute-done.2.refs_2_), channel_id=1, source_target_pairs={{0,1},{1,0},{2,3},{3,2},{4,5},{5,4},{6,7},{7,6},{8,9},{9,8},{10,11... | collective-permute-start | bytes 1572872 | tf_op jit(solution)/shard_map/ppermute | solution.py:246
  44.7 14.8 %collective-permute-start.6 = (f32[32,4096]{1,0:T(8,128)S(1)}, f32[32,4096]{1,0:T(8,128)S(1)}, u32[]{:S(2)}, u32[]{:S(2)}) collective-permute-start(f32[32,4096]{1,0:T(8,128)S(1)} %collective-permute-done.4.refs_4_), channel_id=1, source_target_pairs={{0,14},{1,3},{2,4},{3,1},{4,2},{5,7},{6,8},{7,5},{8,6},{9,11},{10,... | collective-permute-start | bytes 1572872 | tf_op jit(solution)/shard_map/ppermute | solution.py:238
  48.3 13.1 %collective-permute-start.7 = (f32[32,4096]{1,0:T(8,128)S(1)}, f32[32,4096]{1,0:T(8,128)S(1)}, u32[]{:S(2)}, u32[]{:S(2)}) collective-permute-start(f32[32,4096]{1,0:T(8,128)S(1)} %collective-permute-done.5.refs_5_), channel_id=1, source_target_pairs={{0,14},{1,3},{2,4},{3,1},{4,2},{5,7},{6,8},{7,5},{8,6},{9,11},{10,... | collective-permute-start | bytes 1572872 | tf_op jit(solution)/shard_map/ppermute | solution.py:238
  50.3 14.5 %copy-start.3 = (f32[32,4096]{1,0:T(8,128)}, f32[32,4096]{1,0:T(8,128)S(1)}, u32[]{:S(2)}) copy-start(f32[32,4096]{1,0:T(8,128)S(1)} %collective-permute-done.8.refs_8_) | copy-start | bytes 1572868
  50.3 14.6 %collective-permute-start.11 = (f32[32,4096]{1,0:T(8,128)}, f32[32,4096]{1,0:T(8,128)}, u32[]{:S(2)}, u32[]{:S(2)}) collective-permute-start(f32[32,4096]{1,0:T(8,128)} %collective-permute-done.3.refs_3_), channel_id=1, source_target_pairs={{0,1},{1,0},{2,3},{3,2},{4,5},{5,4},{6,7},{7,6},{8,9},{9,8},{10,11... | collective-permute-start | bytes 1572872 | tf_op jit(solution)/shard_map/ppermute | solution.py:246
  55.1 9.7 %copy-start.4 = (f32[32,4096]{1,0:T(8,128)}, f32[32,4096]{1,0:T(8,128)S(1)}, u32[]{:S(2)}) copy-start(f32[32,4096]{1,0:T(8,128)S(1)} %collective-permute-done.9.refs_9_) | copy-start | bytes 1572868
  55.1 9.7 %collective-permute-start.12 = (f32[32,4096]{1,0:T(8,128)S(1)}, f32[32,4096]{1,0:T(8,128)S(1)}, u32[]{:S(2)}, u32[]{:S(2)}) collective-permute-start(f32[32,4096]{1,0:T(8,128)S(1)} %collective-permute-done.4.refs_4_), channel_id=1, source_target_pairs={{0,1},{1,0},{2,3},{3,2},{4,5},{5,4},{6,7},{7,6},{8,9},{9,8},{10,11... | collective-permute-start | bytes 1572872 | tf_op jit(solution)/shard_map/ppermute | solution.py:246
  57.0 7.8 %copy-start.5 = (f32[32,4096]{1,0:T(8,128)}, f32[32,4096]{1,0:T(8,128)S(1)}, u32[]{:S(2)}) copy-start(f32[32,4096]{1,0:T(8,128)S(1)} %collective-permute-done.10.refs_10_) | copy-start | bytes 1572868
  57.1 7.8 %collective-permute-start.13 = (f32[32,4096]{1,0:T(8,128)S(1)}, f32[32,4096]{1,0:T(8,128)S(1)}, u32[]{:S(2)}, u32[]{:S(2)}) collective-permute-start(f32[32,4096]{1,0:T(8,128)S(1)} %collective-permute-done.5.refs_5_), channel_id=1, source_target_pairs={{0,1},{1,0},{2,3},{3,2},{4,5},{5,4},{6,7},{7,6},{8,9},{9,8},{10,11... | collective-permute-start | bytes 1572872 | tf_op jit(solution)/shard_map/ppermute | solution.py:246
  59.5 5.4 %collective-permute-start.14 = (f32[32,4096]{1,0:T(8,128)S(1)}, f32[32,4096]{1,0:T(8,128)}, u32[]{:S(2)}, u32[]{:S(2)}) collective-permute-start(f32[32,4096]{1,0:T(8,128)S(1)} %collective-permute-done.6.refs_6_), channel_id=1, source_target_pairs={{0,1},{1,0},{2,3},{3,2},{4,5},{5,4},{6,7},{7,6},{8,9},{9,8},{10,11... | collective-permute-start | bytes 1572872 | tf_op jit(solution)/shard_map/ppermute | solution.py:246
  61.4 5.0 %collective-permute-start.15 = (f32[32,4096]{1,0:T(8,128)S(1)}, f32[32,4096]{1,0:T(8,128)}, u32[]{:S(2)}, u32[]{:S(2)}) collective-permute-start(f32[32,4096]{1,0:T(8,128)S(1)} %collective-permute-done.7.refs_7_), channel_id=1, source_target_pairs={{0,1},{1,0},{2,3},{3,2},{4,5},{5,4},{6,7},{7,6},{8,9},{9,8},{10,11... | collective-permute-start | bytes 1572872 | tf_op jit(solution)/shard_map/ppermute | solution.py:246
  131.8 8.1 %collective-permute-start.16 = (f32[640,128]{1,0:T(8,128)S(1)}, f32[640,128]{1,0:T(8,128)S(1)}, u32[]{:S(2)}, u32[]{:S(2)}) collective-permute-start(f32[640,128]{1,0:T(8,128)S(1)} %invert.1.here), channel_id=1, source_target_pairs={{0,1},{1,0},{2,3},{3,2},{4,5},{5,4},{6,7},{7,6},{8,9},{9,8},{10,11... | collective-permute-start | bytes 983048 | tf_op jit(solution)/shard_map/ppermute | solution.py:246

commit v7 on v6

--- a/solution.py
+++ b/solution.py
@@ -50,7 +50,7 @@
 
 def products_kernel(me, *refs):
     pieces = refs[:16]
-    c_hbm, vhi_hbm, vlo_hbm, out, raw, c_ref, vhi, vlo, sums, come, gone, sent = refs[16:]
+    c_hbm, vhi_hbm, vlo_hbm, out, raw, c_ref, vhi, vlo, come, gone = refs[16:]
     core = me[0] % 2
     incoming = [pltpu.make_async_copy(piece, raw.at[n], come.at[n]) for n, piece in enumerate(pieces)]
     for index, at in enumerate(PARTS):
@@ -70,9 +70,7 @@
     chi, clo = split(c_ref[...])
     both = nn(vhi[...], jnp.concatenate([chi, clo], axis=1))
     proj = both[:, :COLS] + both[:, COLS:] + nn(vlo[...], chi)
-    sums[:, :16, :] = proj.reshape(32, 16, COLS)
-    outgoing.append(pltpu.make_async_copy(sums.at[:, :16, :], out.at[:, :16, :], sent.at[0]))
-    outgoing[-1].start()
+    out[:, :16, :] = proj.reshape(32, 16, COLS)
 
     own = pl.ds(pl.multiple_of(core * 256, 256), 256)
     strip = pl.ds(pl.multiple_of(core * 128, 128), 128)
@@ -82,9 +80,8 @@
     cross = stacked[:128] + stacked[128:] + nt(vhi[strip, :], vlo[256:, :])
     parts = [square[:128, :128], square[:128, 128:], square[128:, 128:], cross[:, :128], cross[:, 128:]]
     parts.append(jnp.zeros((128, 128), F32))
-    sums[:, 16:, :] = jnp.concatenate(parts, axis=0).reshape(32, 24, COLS)
-    outgoing.append(pltpu.make_async_copy(sums.at[:, 16:, :], out.at[:, 16:, :], sent.at[1]))
-    outgoing[-1].start()
+    out[:, 16:, :] = jnp.concatenate(parts, axis=0).reshape(32, 24, COLS)
+
     for copy in outgoing:
         copy.wait()
 
@@ -93,7 +90,7 @@
     return pl.pallas_call(
         products_kernel,
         in_specs=[pl.BlockSpec(memory_space=pltpu.SMEM)] + [pl.BlockSpec(memory_space=pl.ANY)] * 17,
-        out_specs=[pl.BlockSpec(memory_space=pl.ANY)] * 3,
+        out_specs=[pl.BlockSpec(memory_space=pl.ANY)] * 2 + [pl.BlockSpec(memory_space=pltpu.VMEM)],
         out_shape=[
             pltpu.HBM((NV, ROWS), BF16),
             pltpu.HBM((NV, ROWS), BF16),
@@ -104,10 +101,8 @@
             pltpu.VMEM((ROWS, COLS), F32),
             pltpu.VMEM((NV, ROWS), BF16),
             pltpu.VMEM((NV, ROWS), BF16),
-            pltpu.VMEM((32, 40, COLS), F32),
             pltpu.SemaphoreType.DMA((16 + len(PARTS),)),
             pltpu.SemaphoreType.DMA((len(PARTS), 2)),
-            pltpu.SemaphoreType.DMA((2,)),
         ],
         compiler_params=pltpu.CompilerParams(vmem_limit_bytes=VMEM),
         name="products",

time: 147 us -> 144 us (0.980)
  Pallas kernels: 20.4 us -> 18 us
    pallas_call x1, Pallas kernels: 11 us -> 8.54 us  [products(): pl.pallas_call(products_kernel, in_specs=[pl.BlockSpec(memory_space=pltpu...]
where the time goes in v7:
time: 144 us
  starting transfers between devices  61.1 us (42%)
  blocking collectives  50.9 us (35%)
  Pallas kernels  18 us (12%)
  waiting for transfers between devices  11.9 us (8%)
    ppermute x8, starting transfers between devices, exchange(): return lax.ppermute(value, 'col', perm)  31.9 us
    ppermute x9, starting transfers between devices, swap_cores(): return lax.ppermute(value, 'col', [(i, i ^ 1) for i in range(2 * CHIPS)])  29.1 us
    all_to_all x1, blocking collectives, shards(): summed = lax.all_to_all(partial, 'row', 0, 0, tiled=True).sum(axis=0)  26.3 us
    all_to_all x1, blocking collectives, shards(): lax.all_to_all(jnp.broadcast_to(summed[None], (32, 40, COLS)), 'row', 0,...  24.6 us
    ppermute x8, waiting for transfers between devices, exchange(): return lax.ppermute(value, 'col', perm)  9.29 us
    pallas_call x1, Pallas kernels, products(): pl.pallas_call(products_kernel, in_specs=[pl.BlockSpec(memory_space=pltpu...  8.54 us
    pallas_call x1, Pallas kernels, finish(): pl.pallas_call(finish_kernel, in_specs=[pl.BlockSpec(memory_space=pltpu.S...  6.04 us
    pallas_call x1, Pallas kernels, invert(): pl.pallas_call(invert_kernel, in_specs=[pl.BlockSpec(memory_space=pl.ANY)...  3.38 us
  transfers between devices with their start and end apart: 17, of which 6 were waited for; matrix products, arithmetic and copies ran while one was open for 0% of the time, Pallas kernels for 0%

profile of v7, /device:TPU:1, one launch (start us, length us, event | category | flops | bytes accessed | tf_op | source)
XLA Modules:
  0.0 143.6 jit_solution(16682698992123587643)
XLA Ops:
  0.0 1.1 slice_bitcast_fusion
  1.1 11.5 %collective-permute-start = (f32[16,4096]{1,0:T(8,128)S(1)}, f32[16,4096]{1,0:T(8,128)S(1)}, u32[]{:S(2)}, u32[]{:S(2)}) collective-permute-start(f32[16,4096]{1,0:T(8,128)S(1)} %get-tuple-element.12), channel_id=1, source_target_pairs={{0,2},{1,15},{2,0},{3,5},{4,6},{5,3},{6,4},{7,9},{8,10},{9,7},{10,... | collective-permute-start | bytes 786440 | tf_op jit(solution)/shard_map/ppermute | solution.py:233
  12.6 1.9 %collective-permute-start.1 = (f32[16,4096]{1,0:T(8,128)S(1)}, f32[16,4096]{1,0:T(8,128)S(1)}, u32[]{:S(2)}, u32[]{:S(2)}) collective-permute-start(f32[16,4096]{1,0:T(8,128)S(1)} %get-tuple-element.11), channel_id=1, source_target_pairs={{0,2},{1,15},{2,0},{3,5},{4,6},{5,3},{6,4},{7,9},{8,10},{9,7},{10,... | collective-permute-start | bytes 786440 | tf_op jit(solution)/shard_map/ppermute | solution.py:233
  14.5 1.8 %collective-permute-done = f32[16,4096]{1,0:T(8,128)S(1)} collective-permute-done((f32[16,4096]{1,0:T(8,128)S(1)}, f32[16,4096]{1,0:T(8,128)S(1)}, u32[]{:S(2)}, u32[]{:S(2)}) %collective-permute-start) | collective-permute-done | bytes 262176 | tf_op jit(solution)/shard_map/ppermute | solution.py:233
  16.4 0.0 copy-start
  16.4 1.9 %collective-permute-start.2 = (f32[32,4096]{1,0:T(8,128)S(1)}, f32[32,4096]{1,0:T(8,128)S(1)}, u32[]{:S(2)}, u32[]{:S(2)}) collective-permute-start(f32[32,4096]{1,0:T(8,128)S(1)} %pad_maximum_fusion.refs_0_), channel_id=1, source_target_pairs={{0,14},{1,3},{2,4},{3,1},{4,2},{5,7},{6,8},{7,5},{8,6},{9,11},{10,... | collective-permute-start | bytes 1572872 | tf_op jit(solution)/shard_map/ppermute | solution.py:233
  18.3 2.6 %collective-permute-done.1 = f32[16,4096]{1,0:T(8,128)S(1)} collective-permute-done((f32[16,4096]{1,0:T(8,128)S(1)}, f32[16,4096]{1,0:T(8,128)S(1)}, u32[]{:S(2)}, u32[]{:S(2)}) %collective-permute-start.1) | collective-permute-done | bytes 262176 | tf_op jit(solution)/shard_map/ppermute | solution.py:233
  20.9 0.0 copy-start.1
  21.0 1.9 %collective-permute-start.3 = (f32[32,4096]{1,0:T(8,128)S(1)}, f32[32,4096]{1,0:T(8,128)}, u32[]{:S(2)}, u32[]{:S(2)}) collective-permute-start(f32[32,4096]{1,0:T(8,128)S(1)} %pad_maximum_fusion.1.refs_1_), channel_id=1, source_target_pairs={{0,14},{1,3},{2,4},{3,1},{4,2},{5,7},{6,8},{7,5},{8,6},{9,11},{10,... | collective-permute-start | bytes 1572872 | tf_op jit(solution)/shard_map/ppermute | solution.py:233
  22.9 3.7 %collective-permute-done.2.refs_2_ = f32[32,4096]{1,0:T(8,128)S(1)} collective-permute-done((f32[32,4096]{1,0:T(8,128)S(1)}, f32[32,4096]{1,0:T(8,128)S(1)}, u32[]{:S(2)}, u32[]{:S(2)}) %collective-permute-start.2) | collective-permute-done | bytes 524320 | tf_op jit(solution)/shard_map/ppermute | solution.py:233
  26.6 0.0 copy-start.2
  26.6 4.6 %collective-permute-start.4 = (f32[32,4096]{1,0:T(8,128)S(1)}, f32[32,4096]{1,0:T(8,128)S(1)}, u32[]{:S(2)}, u32[]{:S(2)}) collective-permute-start(f32[32,4096]{1,0:T(8,128)S(1)} %collective-permute-done.2.refs_2_), channel_id=1, source_target_pairs={{0,2},{1,15},{2,0},{3,5},{4,6},{5,3},{6,4},{7,9},{8,10},{9,7},{10,... | collective-permute-start | bytes 1572872 | tf_op jit(solution)/shard_map/ppermute | solution.py:233
  31.2 1.2 collective-permute-done.3.refs_3_
  32.3 4.6 %collective-permute-start.5 = (f32[32,4096]{1,0:T(8,128)}, f32[32,4096]{1,0:T(8,128)S(1)}, u32[]{:S(2)}, u32[]{:S(2)}) collective-permute-start(f32[32,4096]{1,0:T(8,128)} %collective-permute-done.3.refs_3_), channel_id=1, source_target_pairs={{0,2},{1,15},{2,0},{3,5},{4,6},{5,3},{6,4},{7,9},{8,10},{9,7},{10,... | collective-permute-start | bytes 1572872 | tf_op jit(solution)/shard_map/ppermute | solution.py:233
  36.9 3.4 %collective-permute-start.8 = (f32[32,4096]{1,0:T(8,128)S(1)}, f32[32,4096]{1,0:T(8,128)S(1)}, u32[]{:S(2)}, u32[]{:S(2)}) collective-permute-start(f32[32,4096]{1,0:T(8,128)S(1)} %pad_maximum_fusion.refs_0_), channel_id=1, source_target_pairs={{0,1},{1,0},{2,3},{3,2},{4,5},{5,4},{6,7},{7,6},{8,9},{9,8},{10,11... | collective-permute-start | bytes 1572872 | tf_op jit(solution)/shard_map/ppermute | solution.py:241
  40.3 1.9 %collective-permute-start.9 = (f32[32,4096]{1,0:T(8,128)S(1)}, f32[32,4096]{1,0:T(8,128)S(1)}, u32[]{:S(2)}, u32[]{:S(2)}) collective-permute-start(f32[32,4096]{1,0:T(8,128)S(1)} %pad_maximum_fusion.1.refs_1_), channel_id=1, source_target_pairs={{0,1},{1,0},{2,3},{3,2},{4,5},{5,4},{6,7},{7,6},{8,9},{9,8},{10,11... | collective-permute-start | bytes 1572872 | tf_op jit(solution)/shard_map/ppermute | solution.py:241
  42.2 2.4 %collective-permute-start.10 = (f32[32,4096]{1,0:T(8,128)S(1)}, f32[32,4096]{1,0:T(8,128)S(1)}, u32[]{:S(2)}, u32[]{:S(2)}) collective-permute-start(f32[32,4096]{1,0:T(8,128)S(1)} %collective-permute-done.2.refs_2_), channel_id=1, source_target_pairs={{0,1},{1,0},{2,3},{3,2},{4,5},{5,4},{6,7},{7,6},{8,9},{9,8},{10,11... | collective-permute-start | bytes 1572872 | tf_op jit(solution)/shard_map/ppermute | solution.py:241
  44.6 0.0 collective-permute-done.4.refs_4_
  44.7 3.6 %collective-permute-start.6 = (f32[32,4096]{1,0:T(8,128)S(1)}, f32[32,4096]{1,0:T(8,128)S(1)}, u32[]{:S(2)}, u32[]{:S(2)}) collective-permute-start(f32[32,4096]{1,0:T(8,128)S(1)} %collective-permute-done.4.refs_4_), channel_id=1, source_target_pairs={{0,14},{1,3},{2,4},{3,1},{4,2},{5,7},{6,8},{7,5},{8,6},{9,11},{10,... | collective-permute-start | bytes 1572872 | tf_op jit(solution)/shard_map/ppermute | solution.py:233
  48.3 0.0 collective-permute-done.5.refs_5_
  48.3 1.9 %collective-permute-start.7 = (f32[32,4096]{1,0:T(8,128)S(1)}, f32[32,4096]{1,0:T(8,128)S(1)}, u32[]{:S(2)}, u32[]{:S(2)}) collective-permute-start(f32[32,4096]{1,0:T(8,128)S(1)} %collective-permute-done.5.refs_5_), channel_id=1, source_target_pairs={{0,14},{1,3},{2,4},{3,1},{4,2},{5,7},{6,8},{7,5},{8,6},{9,11},{10,... | collective-permute-start | bytes 1572872 | tf_op jit(solution)/shard_map/ppermute | solution.py:233
  50.2 0.0 collective-permute-done.8.refs_8_
  50.3 0.0 copy-start.3
  50.3 4.8 %collective-permute-start.11 = (f32[32,4096]{1,0:T(8,128)}, f32[32,4096]{1,0:T(8,128)}, u32[]{:S(2)}, u32[]{:S(2)}) collective-permute-start(f32[32,4096]{1,0:T(8,128)} %collective-permute-done.3.refs_3_), channel_id=1, source_target_pairs={{0,1},{1,0},{2,3},{3,2},{4,5},{5,4},{6,7},{7,6},{8,9},{9,8},{10,11... | collective-permute-start | bytes 1572872 | tf_op jit(solution)/shard_map/ppermute | solution.py:241
  55.1 0.0 collective-permute-done.9.refs_9_
  55.1 0.0 copy-start.4
  55.1 1.9 %collective-permute-start.12 = (f32[32,4096]{1,0:T(8,128)S(1)}, f32[32,4096]{1,0:T(8,128)S(1)}, u32[]{:S(2)}, u32[]{:S(2)}) collective-permute-start(f32[32,4096]{1,0:T(8,128)S(1)} %collective-permute-done.4.refs_4_), channel_id=1, source_target_pairs={{0,1},{1,0},{2,3},{3,2},{4,5},{5,4},{6,7},{7,6},{8,9},{9,8},{10,11... | collective-permute-start | bytes 1572872 | tf_op jit(solution)/shard_map/ppermute | solution.py:241
  57.0 0.0 collective-permute-done.10.refs_10_
  57.0 0.0 copy-start.5
  57.1 2.4 %collective-permute-start.13 = (f32[32,4096]{1,0:T(8,128)S(1)}, f32[32,4096]{1,0:T(8,128)S(1)}, u32[]{:S(2)}, u32[]{:S(2)}) collective-permute-start(f32[32,4096]{1,0:T(8,128)S(1)} %collective-permute-done.5.refs_5_), channel_id=1, source_target_pairs={{0,1},{1,0},{2,3},{3,2},{4,5},{5,4},{6,7},{7,6},{8,9},{9,8},{10,11... | collective-permute-start | bytes 1572872 | tf_op jit(solution)/shard_map/ppermute | solution.py:241
  59.5 0.0 collective-permute-done.6.refs_6_
  59.5 1.9 %collective-permute-start.14 = (f32[32,4096]{1,0:T(8,128)S(1)}, f32[32,4096]{1,0:T(8,128)}, u32[]{:S(2)}, u32[]{:S(2)}) collective-permute-start(f32[32,4096]{1,0:T(8,128)S(1)} %collective-permute-done.6.refs_6_), channel_id=1, source_target_pairs={{0,1},{1,0},{2,3},{3,2},{4,5},{5,4},{6,7},{7,6},{8,9},{9,8},{10,11... | collective-permute-start | bytes 1572872 | tf_op jit(solution)/shard_map/ppermute | solution.py:241
  61.4 0.0 collective-permute-done.7.refs_7_
  61.4 0.0 copy-done
  61.4 3.3 %collective-permute-start.15 = (f32[32,4096]{1,0:T(8,128)S(1)}, f32[32,4096]{1,0:T(8,128)}, u32[]{:S(2)}, u32[]{:S(2)}) collective-permute-start(f32[32,4096]{1,0:T(8,128)S(1)} %collective-permute-done.7.refs_7_), channel_id=1, source_target_pairs={{0,1},{1,0},{2,3},{3,2},{4,5},{5,4},{6,7},{7,6},{8,9},{9,8},{10,11... | collective-permute-start | bytes 1572872 | tf_op jit(solution)/shard_map/ppermute | solution.py:241
  64.8 0.0 copy-done.1
  64.8 0.0 copy-done.2
  64.8 0.0 copy-done.3
  64.8 0.0 copy-done.4
  64.8 0.0 copy-done.5
  64.8 0.0 collective-permute-done.11.refs_11_
  64.8 0.0 collective-permute-done.12.refs_12_
  64.8 0.0 collective-permute-done.13.refs_13_
  64.8 0.0 collective-permute-done.14.refs_14_
  64.9 1.6 %collective-permute-done.15.refs_15_ = f32[32,4096]{1,0:T(8,128)} collective-permute-done((f32[32,4096]{1,0:T(8,128)S(1)}, f32[32,4096]{1,0:T(8,128)}, u32[]{:S(2)}, u32[]{:S(2)}) %collective-permute-start.15) | collective-permute-done | bytes 524320 | tf_op jit(solution)/shard_map/ppermute | solution.py:241
  66.4 8.5 %products.1 = (bf16[512,4096]{1,0:T(8,128)(2,1)}, bf16[512,4096]{1,0:T(8,128)(2,1)}, f32[32,40,128]{2,1,0:T(8,128)S(1)}) custom-call(s32[1]{0:T(128)} %bitcast.me, f32[32,4096]{1,0:T(8,128)} %copy-done, f32[32,4096]{1,0:T(8,128)} %copy-done.1, f32[32,4096]{1,0:T(8,128)} %copy-done.2, f32[32,4096]{1,0:T(8,128)} %collective-permute-done.3.refs_3_, ...), custom_call_target="tpu_custom_call" | custom-call | tf_op jit(solution)/shard_map/products/pallas_call | solution.py:90
  75.0 26.3 %all_to_all.10 = f32[32,40,128]{2,1,0:T(8,128)S(1)} all-to-all(f32[32,40,128]{2,1,0:T(8,128)S(1)} %get-tuple-element.8), channel_id=1, replica_groups=mesh['row'=32,'col'=16] {'row'}, dimensions={0} | all-to-all | bytes 1310720 | tf_op jit(solution)/shard_map/all_to_all | solution.py:256
  101.3 0.1 reduce_sum.9
  101.4 24.6 %all_to_all.11.mine = f32[32,40,128]{2,1,0:T(8,128)S(1)} all-to-all(f32[32,40,128]{2,1,0:T(8,128)S(1)} %broadcast_in_dim.2), channel_id=1, replica_groups=mesh['row'=32,'col'=16] {'row'}, dimensions={0} | all-to-all | bytes 1310720 | tf_op jit(solution)/shard_map/all_to_all | solution.py:257
  125.9 3.4 %invert.1.here = f32[640,128]{1,0:T(8,128)S(1)} custom-call(f32[32,40,128]{2,1,0:T(8,128)S(1)} %all_to_all.11.mine), custom_call_target="tpu_custom_call" | custom-call | tf_op jit(solution)/shard_map/invert/pallas_call | solution.py:148
  129.3 7.0 %collective-permute-start.16 = (f32[640,128]{1,0:T(8,128)S(1)}, f32[640,128]{1,0:T(8,128)S(1)}, u32[]{:S(2)}, u32[]{:S(2)}) collective-permute-start(f32[640,128]{1,0:T(8,128)S(1)} %invert.1.here), channel_id=1, source_target_pairs={{0,1},{1,0},{2,3},{3,2},{4,5},{5,4},{6,7},{7,6},{8,9},{9,8},{10,11... | collective-permute-start | bytes 983048 | tf_op jit(solution)/shard_map/ppermute | solution.py:241
  136.3 1.1 collective-permute-done.16.there
  137.4 6.0 %finish.1 = f32[4096,128]{1,0:T(8,128)} custom-call(s32[1]{0:T(128)} %bitcast.me, f32[32,40,128]{2,1,0:T(8,128)S(1)} %all_to_all.11.mine, f32[640,128]{1,0:T(8,128)S(1)} %invert.1.here, f32[640,128]{1,0:T(8,128)S(1)} %collective-permute-done.16.there, f32[4096,128]{1,0:T(8,128)} %c_hbm.1, bf16[512,4096]{1,0:T(8,128)(2,1)} %get-tuple-element.9.vhi_hbm, ...), custom_call_target="tpu_custom_call" | custom-call | tf_op jit(solution)/shard_map/finish/pallas_call | solution.py:203
  (3 shorter events, 0.1 us)
Async XLA Ops:
  1.1 15.3 %collective-permute-start = (f32[16,4096]{1,0:T(8,128)S(1)}, f32[16,4096]{1,0:T(8,128)S(1)}, u32[]{:S(2)}, u32[]{:S(2)}) collective-permute-start(f32[16,4096]{1,0:T(8,128)S(1)} %get-tuple-element.12), channel_id=1, source_target_pairs={{0,2},{1,15},{2,0},{3,5},{4,6},{5,3},{6,4},{7,9},{8,10},{9,7},{10,... | collective-permute-start | bytes 786440 | tf_op jit(solution)/shard_map/ppermute | solution.py:233
  12.6 8.3 %collective-permute-start.1 = (f32[16,4096]{1,0:T(8,128)S(1)}, f32[16,4096]{1,0:T(8,128)S(1)}, u32[]{:S(2)}, u32[]{:S(2)}) collective-permute-start(f32[16,4096]{1,0:T(8,128)S(1)} %get-tuple-element.11), channel_id=1, source_target_pairs={{0,2},{1,15},{2,0},{3,5},{4,6},{5,3},{6,4},{7,9},{8,10},{9,7},{10,... | collective-permute-start | bytes 786440 | tf_op jit(solution)/shard_map/ppermute | solution.py:233
  16.4 45.1 %copy-start = (f32[32,4096]{1,0:T(8,128)}, f32[32,4096]{1,0:T(8,128)S(1)}, u32[]{:S(2)}) copy-start(f32[32,4096]{1,0:T(8,128)S(1)} %pad_maximum_fusion.refs_0_) | copy-start | bytes 1572868
  16.4 10.2 %collective-permute-start.2 = (f32[32,4096]{1,0:T(8,128)S(1)}, f32[32,4096]{1,0:T(8,128)S(1)}, u32[]{:S(2)}, u32[]{:S(2)}) collective-permute-start(f32[32,4096]{1,0:T(8,128)S(1)} %pad_maximum_fusion.refs_0_), channel_id=1, source_target_pairs={{0,14},{1,3},{2,4},{3,1},{4,2},{5,7},{6,8},{7,5},{8,6},{9,11},{10,... | collective-permute-start | bytes 1572872 | tf_op jit(solution)/shard_map/ppermute | solution.py:233
  20.9 43.8 %copy-start.1 = (f32[32,4096]{1,0:T(8,128)}, f32[32,4096]{1,0:T(8,128)S(1)}, u32[]{:S(2)}) copy-start(f32[32,4096]{1,0:T(8,128)S(1)} %pad_maximum_fusion.1.refs_1_) | copy-start | bytes 1572868
  21.0 11.4 %collective-permute-start.3 = (f32[32,4096]{1,0:T(8,128)S(1)}, f32[32,4096]{1,0:T(8,128)}, u32[]{:S(2)}, u32[]{:S(2)}) collective-permute-start(f32[32,4096]{1,0:T(8,128)S(1)} %pad_maximum_fusion.1.refs_1_), channel_id=1, source_target_pairs={{0,14},{1,3},{2,4},{3,1},{4,2},{5,7},{6,8},{7,5},{8,6},{9,11},{10,... | collective-permute-start | bytes 1572872 | tf_op jit(solution)/shard_map/ppermute | solution.py:233
  26.6 38.2 %copy-start.2 = (f32[32,4096]{1,0:T(8,128)}, f32[32,4096]{1,0:T(8,128)S(1)}, u32[]{:S(2)}) copy-start(f32[32,4096]{1,0:T(8,128)S(1)} %collective-permute-done.2.refs_2_) | copy-start | bytes 1572868
  26.6 18.0 %collective-permute-start.4 = (f32[32,4096]{1,0:T(8,128)S(1)}, f32[32,4096]{1,0:T(8,128)S(1)}, u32[]{:S(2)}, u32[]{:S(2)}) collective-permute-start(f32[32,4096]{1,0:T(8,128)S(1)} %collective-permute-done.2.refs_2_), channel_id=1, source_target_pairs={{0,2},{1,15},{2,0},{3,5},{4,6},{5,3},{6,4},{7,9},{8,10},{9,7},{10,... | collective-permute-start | bytes 1572872 | tf_op jit(solution)/shard_map/ppermute | solution.py:233
  32.3 16.0 %collective-permute-start.5 = (f32[32,4096]{1,0:T(8,128)}, f32[32,4096]{1,0:T(8,128)S(1)}, u32[]{:S(2)}, u32[]{:S(2)}) collective-permute-start(f32[32,4096]{1,0:T(8,128)} %collective-permute-done.3.refs_3_), channel_id=1, source_target_pairs={{0,2},{1,15},{2,0},{3,5},{4,6},{5,3},{6,4},{7,9},{8,10},{9,7},{10,... | collective-permute-start | bytes 1572872 | tf_op jit(solution)/shard_map/ppermute | solution.py:233
  36.9 13.4 %collective-permute-start.8 = (f32[32,4096]{1,0:T(8,128)S(1)}, f32[32,4096]{1,0:T(8,128)S(1)}, u32[]{:S(2)}, u32[]{:S(2)}) collective-permute-start(f32[32,4096]{1,0:T(8,128)S(1)} %pad_maximum_fusion.refs_0_), channel_id=1, source_target_pairs={{0,1},{1,0},{2,3},{3,2},{4,5},{5,4},{6,7},{7,6},{8,9},{9,8},{10,11... | collective-permute-start | bytes 1572872 | tf_op jit(solution)/shard_map/ppermute | solution.py:241
  40.3 14.8 %collective-permute-start.9 = (f32[32,4096]{1,0:T(8,128)S(1)}, f32[32,4096]{1,0:T(8,128)S(1)}, u32[]{:S(2)}, u32[]{:S(2)}) collective-permute-start(f32[32,4096]{1,0:T(8,128)S(1)} %pad_maximum_fusion.1.refs_1_), channel_id=1, source_target_pairs={{0,1},{1,0},{2,3},{3,2},{4,5},{5,4},{6,7},{7,6},{8,9},{9,8},{10,11... | collective-permute-start | bytes 1572872 | tf_op jit(solution)/shard_map/ppermute | solution.py:241
  42.2 14.8 %collective-permute-start.10 = (f32[32,4096]{1,0:T(8,128)S(1)}, f32[32,4096]{1,0:T(8,128)S(1)}, u32[]{:S(2)}, u32[]{:S(2)}) collective-permute-start(f32[32,4096]{1,0:T(8,128)S(1)} %collective-permute-done.2.refs_2_), channel_id=1, source_target_pairs={{0,1},{1,0},{2,3},{3,2},{4,5},{5,4},{6,7},{7,6},{8,9},{9,8},{10,11... | collective-permute-start | bytes 1572872 | tf_op jit(solution)/shard_map/ppermute | solution.py:241
  44.7 14.8 %collective-permute-start.6 = (f32[32,4096]{1,0:T(8,128)S(1)}, f32[32,4096]{1,0:T(8,128)S(1)}, u32[]{:S(2)}, u32[]{:S(2)}) collective-permute-start(f32[32,4096]{1,0:T(8,128)S(1)} %collective-permute-done.4.refs_4_), channel_id=1, source_target_pairs={{0,14},{1,3},{2,4},{3,1},{4,2},{5,7},{6,8},{7,5},{8,6},{9,11},{10,... | collective-permute-start | bytes 1572872 | tf_op jit(solution)/shard_map/ppermute | solution.py:233
  48.3 13.1 %collective-permute-start.7 = (f32[32,4096]{1,0:T(8,128)S(1)}, f32[32,4096]{1,0:T(8,128)S(1)}, u32[]{:S(2)}, u32[]{:S(2)}) collective-permute-start(f32[32,4096]{1,0:T(8,128)S(1)} %collective-permute-done.5.refs_5_), channel_id=1, source_target_pairs={{0,14},{1,3},{2,4},{3,1},{4,2},{5,7},{6,8},{7,5},{8,6},{9,11},{10,... | collective-permute-start | bytes 1572872 | tf_op jit(solution)/shard_map/ppermute | solution.py:233
  50.3 14.5 %copy-start.3 = (f32[32,4096]{1,0:T(8,128)}, f32[32,4096]{1,0:T(8,128)S(1)}, u32[]{:S(2)}) copy-start(f32[32,4096]{1,0:T(8,128)S(1)} %collective-permute-done.8.refs_8_) | copy-start | bytes 1572868
  50.3 14.6 %collective-permute-start.11 = (f32[32,4096]{1,0:T(8,128)}, f32[32,4096]{1,0:T(8,128)}, u32[]{:S(2)}, u32[]{:S(2)}) collective-permute-start(f32[32,4096]{1,0:T(8,128)} %collective-permute-done.3.refs_3_), channel_id=1, source_target_pairs={{0,1},{1,0},{2,3},{3,2},{4,5},{5,4},{6,7},{7,6},{8,9},{9,8},{10,11... | collective-permute-start | bytes 1572872 | tf_op jit(solution)/shard_map/ppermute | solution.py:241
  55.1 9.7 %copy-start.4 = (f32[32,4096]{1,0:T(8,128)}, f32[32,4096]{1,0:T(8,128)S(1)}, u32[]{:S(2)}) copy-start(f32[32,4096]{1,0:T(8,128)S(1)} %collective-permute-done.9.refs_9_) | copy-start | bytes 1572868
  55.1 9.7 %collective-permute-start.12 = (f32[32,4096]{1,0:T(8,128)S(1)}, f32[32,4096]{1,0:T(8,128)S(1)}, u32[]{:S(2)}, u32[]{:S(2)}) collective-permute-start(f32[32,4096]{1,0:T(8,128)S(1)} %collective-permute-done.4.refs_4_), channel_id=1, source_target_pairs={{0,1},{1,0},{2,3},{3,2},{4,5},{5,4},{6,7},{7,6},{8,9},{9,8},{10,11... | collective-permute-start | bytes 1572872 | tf_op jit(solution)/shard_map/ppermute | solution.py:241
  57.0 7.8 %copy-start.5 = (f32[32,4096]{1,0:T(8,128)}, f32[32,4096]{1,0:T(8,128)S(1)}, u32[]{:S(2)}) copy-start(f32[32,4096]{1,0:T(8,128)S(1)} %collective-permute-done.10.refs_10_) | copy-start | bytes 1572868
  57.1 7.8 %collective-permute-start.13 = (f32[32,4096]{1,0:T(8,128)S(1)}, f32[32,4096]{1,0:T(8,128)S(1)}, u32[]{:S(2)}, u32[]{:S(2)}) collective-permute-start(f32[32,4096]{1,0:T(8,128)S(1)} %collective-permute-done.5.refs_5_), channel_id=1, source_target_pairs={{0,1},{1,0},{2,3},{3,2},{4,5},{5,4},{6,7},{7,6},{8,9},{9,8},{10,11... | collective-permute-start | bytes 1572872 | tf_op jit(solution)/shard_map/ppermute | solution.py:241
  59.5 5.4 %collective-permute-start.14 = (f32[32,4096]{1,0:T(8,128)S(1)}, f32[32,4096]{1,0:T(8,128)}, u32[]{:S(2)}, u32[]{:S(2)}) collective-permute-start(f32[32,4096]{1,0:T(8,128)S(1)} %collective-permute-done.6.refs_6_), channel_id=1, source_target_pairs={{0,1},{1,0},{2,3},{3,2},{4,5},{5,4},{6,7},{7,6},{8,9},{9,8},{10,11... | collective-permute-start | bytes 1572872 | tf_op jit(solution)/shard_map/ppermute | solution.py:241
  61.4 5.0 %collective-permute-start.15 = (f32[32,4096]{1,0:T(8,128)S(1)}, f32[32,4096]{1,0:T(8,128)}, u32[]{:S(2)}, u32[]{:S(2)}) collective-permute-start(f32[32,4096]{1,0:T(8,128)S(1)} %collective-permute-done.7.refs_7_), channel_id=1, source_target_pairs={{0,1},{1,0},{2,3},{3,2},{4,5},{5,4},{6,7},{7,6},{8,9},{9,8},{10,11... | collective-permute-start | bytes 1572872 | tf_op jit(solution)/shard_map/ppermute | solution.py:241
  129.3 8.1 %collective-permute-start.16 = (f32[640,128]{1,0:T(8,128)S(1)}, f32[640,128]{1,0:T(8,128)S(1)}, u32[]{:S(2)}, u32[]{:S(2)}) collective-permute-start(f32[640,128]{1,0:T(8,128)S(1)} %invert.1.here), channel_id=1, source_target_pairs={{0,1},{1,0},{2,3},{3,2},{4,5},{5,4},{6,7},{7,6},{8,9},{9,8},{10,11... | collective-permute-start | bytes 983048 | tf_op jit(solution)/shard_map/ppermute | solution.py:241

commit v8 on v7

--- a/solution.py
+++ b/solution.py
@@ -256,7 +256,7 @@
     summed = lax.all_to_all(partial, "row", 0, 0, tiled=True).sum(axis=0)
     mine = lax.all_to_all(jnp.broadcast_to(summed[None], (32, 40, COLS)), "row", 0, 0, tiled=True)
     here = invert(mine)
-    return finish(me, mine, here, swap_cores(here), in_hbm(eigvecs), in_hbm(vhi), in_hbm(vlo))
+    return finish(me, mine, here, swap_cores(here), eigvecs, in_hbm(vhi), in_hbm(vlo))
 
 
 def solution(mesh):

time: 144 us -> 144 us (level)
  no operation moved by 1% of the time
where the time goes in v8:
time: 144 us
  starting transfers between devices  61.1 us (42%)
  blocking collectives  51 us (35%)
  Pallas kernels  17.9 us (12%)
  waiting for transfers between devices  11.9 us (8%)
    ppermute x8, starting transfers between devices, exchange(): return lax.ppermute(value, 'col', perm)  31.9 us
    ppermute x9, starting transfers between devices, swap_cores(): return lax.ppermute(value, 'col', [(i, i ^ 1) for i in range(2 * CHIPS)])  29.1 us
    all_to_all x1, blocking collectives, shards(): summed = lax.all_to_all(partial, 'row', 0, 0, tiled=True).sum(axis=0)  26.5 us
    all_to_all x1, blocking collectives, shards(): lax.all_to_all(jnp.broadcast_to(summed[None], (32, 40, COLS)), 'row', 0,...  24.6 us
    ppermute x8, waiting for transfers between devices, exchange(): return lax.ppermute(value, 'col', perm)  9.29 us
    pallas_call x1, Pallas kernels, products(): pl.pallas_call(products_kernel, in_specs=[pl.BlockSpec(memory_space=pltpu...  8.54 us
    pallas_call x1, Pallas kernels, finish(): pl.pallas_call(finish_kernel, in_specs=[pl.BlockSpec(memory_space=pltpu.S...  5.96 us
    pallas_call x1, Pallas kernels, invert(): pl.pallas_call(invert_kernel, in_specs=[pl.BlockSpec(memory_space=pl.ANY)...  3.38 us
  transfers between devices with their start and end apart: 17, of which 6 were waited for; matrix products, arithmetic and copies ran while one was open for 0% of the time, Pallas kernels for 0%

profile of v8, /device:TPU:1, one launch (start us, length us, event | category | flops | bytes accessed | tf_op | source)
XLA Modules:
  0.0 143.6 jit_solution(2083433400947152537)
XLA Ops:
  0.0 1.1 slice_bitcast_fusion
  1.1 11.5 %collective-permute-start = (f32[16,4096]{1,0:T(8,128)S(1)}, f32[16,4096]{1,0:T(8,128)S(1)}, u32[]{:S(2)}, u32[]{:S(2)}) collective-permute-start(f32[16,4096]{1,0:T(8,128)S(1)} %get-tuple-element.12), channel_id=1, source_target_pairs={{0,2},{1,15},{2,0},{3,5},{4,6},{5,3},{6,4},{7,9},{8,10},{9,7},{10,... | collective-permute-start | bytes 786440 | tf_op jit(solution)/shard_map/ppermute | solution.py:233
  12.6 1.9 %collective-permute-start.1 = (f32[16,4096]{1,0:T(8,128)S(1)}, f32[16,4096]{1,0:T(8,128)S(1)}, u32[]{:S(2)}, u32[]{:S(2)}) collective-permute-start(f32[16,4096]{1,0:T(8,128)S(1)} %get-tuple-element.11), channel_id=1, source_target_pairs={{0,2},{1,15},{2,0},{3,5},{4,6},{5,3},{6,4},{7,9},{8,10},{9,7},{10,... | collective-permute-start | bytes 786440 | tf_op jit(solution)/shard_map/ppermute | solution.py:233
  14.5 1.8 %collective-permute-done = f32[16,4096]{1,0:T(8,128)S(1)} collective-permute-done((f32[16,4096]{1,0:T(8,128)S(1)}, f32[16,4096]{1,0:T(8,128)S(1)}, u32[]{:S(2)}, u32[]{:S(2)}) %collective-permute-start) | collective-permute-done | bytes 262176 | tf_op jit(solution)/shard_map/ppermute | solution.py:233
  16.4 0.0 copy-start.1
  16.4 1.9 %collective-permute-start.2 = (f32[32,4096]{1,0:T(8,128)S(1)}, f32[32,4096]{1,0:T(8,128)S(1)}, u32[]{:S(2)}, u32[]{:S(2)}) collective-permute-start(f32[32,4096]{1,0:T(8,128)S(1)} %pad_maximum_fusion.refs_0_), channel_id=1, source_target_pairs={{0,14},{1,3},{2,4},{3,1},{4,2},{5,7},{6,8},{7,5},{8,6},{9,11},{10,... | collective-permute-start | bytes 1572872 | tf_op jit(solution)/shard_map/ppermute | solution.py:233
  18.3 2.6 %collective-permute-done.1 = f32[16,4096]{1,0:T(8,128)S(1)} collective-permute-done((f32[16,4096]{1,0:T(8,128)S(1)}, f32[16,4096]{1,0:T(8,128)S(1)}, u32[]{:S(2)}, u32[]{:S(2)}) %collective-permute-start.1) | collective-permute-done | bytes 262176 | tf_op jit(solution)/shard_map/ppermute | solution.py:233
  20.9 0.0 copy-start.2
  21.0 1.9 %collective-permute-start.3 = (f32[32,4096]{1,0:T(8,128)S(1)}, f32[32,4096]{1,0:T(8,128)}, u32[]{:S(2)}, u32[]{:S(2)}) collective-permute-start(f32[32,4096]{1,0:T(8,128)S(1)} %pad_maximum_fusion.1.refs_1_), channel_id=1, source_target_pairs={{0,14},{1,3},{2,4},{3,1},{4,2},{5,7},{6,8},{7,5},{8,6},{9,11},{10,... | collective-permute-start | bytes 1572872 | tf_op jit(solution)/shard_map/ppermute | solution.py:233
  22.9 3.7 %collective-permute-done.2.refs_2_ = f32[32,4096]{1,0:T(8,128)S(1)} collective-permute-done((f32[32,4096]{1,0:T(8,128)S(1)}, f32[32,4096]{1,0:T(8,128)S(1)}, u32[]{:S(2)}, u32[]{:S(2)}) %collective-permute-start.2) | collective-permute-done | bytes 524320 | tf_op jit(solution)/shard_map/ppermute | solution.py:233
  26.6 0.0 copy-start.3
  26.6 4.6 %collective-permute-start.4 = (f32[32,4096]{1,0:T(8,128)S(1)}, f32[32,4096]{1,0:T(8,128)S(1)}, u32[]{:S(2)}, u32[]{:S(2)}) collective-permute-start(f32[32,4096]{1,0:T(8,128)S(1)} %collective-permute-done.2.refs_2_), channel_id=1, source_target_pairs={{0,2},{1,15},{2,0},{3,5},{4,6},{5,3},{6,4},{7,9},{8,10},{9,7},{10,... | collective-permute-start | bytes 1572872 | tf_op jit(solution)/shard_map/ppermute | solution.py:233
  31.2 1.2 collective-permute-done.3.refs_3_
  32.3 4.6 %collective-permute-start.5 = (f32[32,4096]{1,0:T(8,128)}, f32[32,4096]{1,0:T(8,128)S(1)}, u32[]{:S(2)}, u32[]{:S(2)}) collective-permute-start(f32[32,4096]{1,0:T(8,128)} %collective-permute-done.3.refs_3_), channel_id=1, source_target_pairs={{0,2},{1,15},{2,0},{3,5},{4,6},{5,3},{6,4},{7,9},{8,10},{9,7},{10,... | collective-permute-start | bytes 1572872 | tf_op jit(solution)/shard_map/ppermute | solution.py:233
  36.9 3.4 %collective-permute-start.8 = (f32[32,4096]{1,0:T(8,128)S(1)}, f32[32,4096]{1,0:T(8,128)S(1)}, u32[]{:S(2)}, u32[]{:S(2)}) collective-permute-start(f32[32,4096]{1,0:T(8,128)S(1)} %pad_maximum_fusion.refs_0_), channel_id=1, source_target_pairs={{0,1},{1,0},{2,3},{3,2},{4,5},{5,4},{6,7},{7,6},{8,9},{9,8},{10,11... | collective-permute-start | bytes 1572872 | tf_op jit(solution)/shard_map/ppermute | solution.py:241
  40.3 1.9 %collective-permute-start.9 = (f32[32,4096]{1,0:T(8,128)S(1)}, f32[32,4096]{1,0:T(8,128)S(1)}, u32[]{:S(2)}, u32[]{:S(2)}) collective-permute-start(f32[32,4096]{1,0:T(8,128)S(1)} %pad_maximum_fusion.1.refs_1_), channel_id=1, source_target_pairs={{0,1},{1,0},{2,3},{3,2},{4,5},{5,4},{6,7},{7,6},{8,9},{9,8},{10,11... | collective-permute-start | bytes 1572872 | tf_op jit(solution)/shard_map/ppermute | solution.py:241
  42.2 2.4 %collective-permute-start.10 = (f32[32,4096]{1,0:T(8,128)S(1)}, f32[32,4096]{1,0:T(8,128)S(1)}, u32[]{:S(2)}, u32[]{:S(2)}) collective-permute-start(f32[32,4096]{1,0:T(8,128)S(1)} %collective-permute-done.2.refs_2_), channel_id=1, source_target_pairs={{0,1},{1,0},{2,3},{3,2},{4,5},{5,4},{6,7},{7,6},{8,9},{9,8},{10,11... | collective-permute-start | bytes 1572872 | tf_op jit(solution)/shard_map/ppermute | solution.py:241
  44.6 0.0 collective-permute-done.4.refs_4_
  44.7 3.6 %collective-permute-start.6 = (f32[32,4096]{1,0:T(8,128)S(1)}, f32[32,4096]{1,0:T(8,128)S(1)}, u32[]{:S(2)}, u32[]{:S(2)}) collective-permute-start(f32[32,4096]{1,0:T(8,128)S(1)} %collective-permute-done.4.refs_4_), channel_id=1, source_target_pairs={{0,14},{1,3},{2,4},{3,1},{4,2},{5,7},{6,8},{7,5},{8,6},{9,11},{10,... | collective-permute-start | bytes 1572872 | tf_op jit(solution)/shard_map/ppermute | solution.py:233
  48.3 0.0 collective-permute-done.5.refs_5_
  48.3 1.9 %collective-permute-start.7 = (f32[32,4096]{1,0:T(8,128)S(1)}, f32[32,4096]{1,0:T(8,128)S(1)}, u32[]{:S(2)}, u32[]{:S(2)}) collective-permute-start(f32[32,4096]{1,0:T(8,128)S(1)} %collective-permute-done.5.refs_5_), channel_id=1, source_target_pairs={{0,14},{1,3},{2,4},{3,1},{4,2},{5,7},{6,8},{7,5},{8,6},{9,11},{10,... | collective-permute-start | bytes 1572872 | tf_op jit(solution)/shard_map/ppermute | solution.py:233
  50.2 0.0 collective-permute-done.8.refs_8_
  50.3 0.0 copy-start.4
  50.3 4.8 %collective-permute-start.11 = (f32[32,4096]{1,0:T(8,128)}, f32[32,4096]{1,0:T(8,128)}, u32[]{:S(2)}, u32[]{:S(2)}) collective-permute-start(f32[32,4096]{1,0:T(8,128)} %collective-permute-done.3.refs_3_), channel_id=1, source_target_pairs={{0,1},{1,0},{2,3},{3,2},{4,5},{5,4},{6,7},{7,6},{8,9},{9,8},{10,11... | collective-permute-start | bytes 1572872 | tf_op jit(solution)/shard_map/ppermute | solution.py:241
  55.1 0.0 collective-permute-done.9.refs_9_
  55.1 0.0 copy-start.5
  55.1 1.9 %collective-permute-start.12 = (f32[32,4096]{1,0:T(8,128)S(1)}, f32[32,4096]{1,0:T(8,128)S(1)}, u32[]{:S(2)}, u32[]{:S(2)}) collective-permute-start(f32[32,4096]{1,0:T(8,128)S(1)} %collective-permute-done.4.refs_4_), channel_id=1, source_target_pairs={{0,1},{1,0},{2,3},{3,2},{4,5},{5,4},{6,7},{7,6},{8,9},{9,8},{10,11... | collective-permute-start | bytes 1572872 | tf_op jit(solution)/shard_map/ppermute | solution.py:241
  57.0 0.0 collective-permute-done.10.refs_10_
  57.0 0.0 copy-start.6
  57.1 2.4 %collective-permute-start.13 = (f32[32,4096]{1,0:T(8,128)S(1)}, f32[32,4096]{1,0:T(8,128)S(1)}, u32[]{:S(2)}, u32[]{:S(2)}) collective-permute-start(f32[32,4096]{1,0:T(8,128)S(1)} %collective-permute-done.5.refs_5_), channel_id=1, source_target_pairs={{0,1},{1,0},{2,3},{3,2},{4,5},{5,4},{6,7},{7,6},{8,9},{9,8},{10,11... | collective-permute-start | bytes 1572872 | tf_op jit(solution)/shard_map/ppermute | solution.py:241
  59.5 0.0 collective-permute-done.6.refs_6_
  59.5 1.9 %collective-permute-start.14 = (f32[32,4096]{1,0:T(8,128)S(1)}, f32[32,4096]{1,0:T(8,128)}, u32[]{:S(2)}, u32[]{:S(2)}) collective-permute-start(f32[32,4096]{1,0:T(8,128)S(1)} %collective-permute-done.6.refs_6_), channel_id=1, source_target_pairs={{0,1},{1,0},{2,3},{3,2},{4,5},{5,4},{6,7},{7,6},{8,9},{9,8},{10,11... | collective-permute-start | bytes 1572872 | tf_op jit(solution)/shard_map/ppermute | solution.py:241
  61.4 0.0 collective-permute-done.7.refs_7_
  61.4 0.0 copy-done.1
  61.4 3.3 %collective-permute-start.15 = (f32[32,4096]{1,0:T(8,128)S(1)}, f32[32,4096]{1,0:T(8,128)}, u32[]{:S(2)}, u32[]{:S(2)}) collective-permute-start(f32[32,4096]{1,0:T(8,128)S(1)} %collective-permute-done.7.refs_7_), channel_id=1, source_target_pairs={{0,1},{1,0},{2,3},{3,2},{4,5},{5,4},{6,7},{7,6},{8,9},{9,8},{10,11... | collective-permute-start | bytes 1572872 | tf_op jit(solution)/shard_map/ppermute | solution.py:241
  64.8 0.0 copy-done.2
  64.8 0.0 copy-done.3
  64.8 0.0 copy-done.4
  64.8 0.0 copy-done.5
  64.8 0.0 copy-done.6
  64.8 0.0 collective-permute-done.11.refs_11_
  64.8 0.0 collective-permute-done.12.refs_12_
  64.8 0.0 collective-permute-done.13.refs_13_
  64.8 0.0 collective-permute-done.14.refs_14_
  64.9 1.6 %collective-permute-done.15.refs_15_ = f32[32,4096]{1,0:T(8,128)} collective-permute-done((f32[32,4096]{1,0:T(8,128)S(1)}, f32[32,4096]{1,0:T(8,128)}, u32[]{:S(2)}, u32[]{:S(2)}) %collective-permute-start.15) | collective-permute-done | bytes 524320 | tf_op jit(solution)/shard_map/ppermute | solution.py:241
  66.4 8.5 %products.1 = (bf16[512,4096]{1,0:T(8,128)(2,1)}, bf16[512,4096]{1,0:T(8,128)(2,1)}, f32[32,40,128]{2,1,0:T(8,128)S(1)}) custom-call(s32[1]{0:T(128)} %bitcast.me, f32[32,4096]{1,0:T(8,128)} %copy-done.1, f32[32,4096]{1,0:T(8,128)} %copy-done.2, f32[32,4096]{1,0:T(8,128)} %copy-done.3, f32[32,4096]{1,0:T(8,128)} %collective-permute-done.3.refs_3_, ...), custom_call_target="tpu_custom_call" | custom-call | tf_op jit(solution)/shard_map/products/pallas_call | solution.py:90
  75.0 0.0 copy-start
  75.0 26.5 %all_to_all.10 = f32[32,40,128]{2,1,0:T(8,128)S(1)} all-to-all(f32[32,40,128]{2,1,0:T(8,128)S(1)} %get-tuple-element.8), channel_id=1, replica_groups=mesh['row'=32,'col'=16] {'row'}, dimensions={0} | all-to-all | bytes 1310720 | tf_op jit(solution)/shard_map/all_to_all | solution.py:256
  101.4 0.1 reduce_sum.9
  101.5 24.6 %all_to_all.11.mine = f32[32,40,128]{2,1,0:T(8,128)S(1)} all-to-all(f32[32,40,128]{2,1,0:T(8,128)S(1)} %broadcast_in_dim.2), channel_id=1, replica_groups=mesh['row'=32,'col'=16] {'row'}, dimensions={0} | all-to-all | bytes 1310720 | tf_op jit(solution)/shard_map/all_to_all | solution.py:257
  126.1 3.4 %invert.1.here = f32[640,128]{1,0:T(8,128)S(1)} custom-call(f32[32,40,128]{2,1,0:T(8,128)S(1)} %all_to_all.11.mine), custom_call_target="tpu_custom_call" | custom-call | tf_op jit(solution)/shard_map/invert/pallas_call | solution.py:148
  129.5 7.0 %collective-permute-start.16 = (f32[640,128]{1,0:T(8,128)S(1)}, f32[640,128]{1,0:T(8,128)S(1)}, u32[]{:S(2)}, u32[]{:S(2)}) collective-permute-start(f32[640,128]{1,0:T(8,128)S(1)} %invert.1.here), channel_id=1, source_target_pairs={{0,1},{1,0},{2,3},{3,2},{4,5},{5,4},{6,7},{7,6},{8,9},{9,8},{10,11... | collective-permute-start | bytes 983048 | tf_op jit(solution)/shard_map/ppermute | solution.py:241
  136.5 1.1 collective-permute-done.16.there
  137.5 0.0 copy-done
  137.5 6.0 %finish.1 = f32[4096,128]{1,0:T(8,128)} custom-call(s32[1]{0:T(128)} %bitcast.me, f32[32,40,128]{2,1,0:T(8,128)S(1)} %all_to_all.11.mine, f32[640,128]{1,0:T(8,128)S(1)} %invert.1.here, f32[640,128]{1,0:T(8,128)S(1)} %collective-permute-done.16.there, f32[4096,128]{1,0:T(8,128)S(1)} %copy-done, bf16[512,4096]{1,0:T(8,128)(2,1)} %get-tuple-element.9.vhi_hbm, ...), custom_call_target="tpu_custom_call" | custom-call | tf_op jit(solution)/shard_map/finish/pallas_call | solution.py:203
  (3 shorter events, 0.1 us)
Async XLA Ops:
  1.1 15.3 %collective-permute-start = (f32[16,4096]{1,0:T(8,128)S(1)}, f32[16,4096]{1,0:T(8,128)S(1)}, u32[]{:S(2)}, u32[]{:S(2)}) collective-permute-start(f32[16,4096]{1,0:T(8,128)S(1)} %get-tuple-element.12), channel_id=1, source_target_pairs={{0,2},{1,15},{2,0},{3,5},{4,6},{5,3},{6,4},{7,9},{8,10},{9,7},{10,... | collective-permute-start | bytes 786440 | tf_op jit(solution)/shard_map/ppermute | solution.py:233
  12.6 8.3 %collective-permute-start.1 = (f32[16,4096]{1,0:T(8,128)S(1)}, f32[16,4096]{1,0:T(8,128)S(1)}, u32[]{:S(2)}, u32[]{:S(2)}) collective-permute-start(f32[16,4096]{1,0:T(8,128)S(1)} %get-tuple-element.11), channel_id=1, source_target_pairs={{0,2},{1,15},{2,0},{3,5},{4,6},{5,3},{6,4},{7,9},{8,10},{9,7},{10,... | collective-permute-start | bytes 786440 | tf_op jit(solution)/shard_map/ppermute | solution.py:233
  16.4 45.1 %copy-start.1 = (f32[32,4096]{1,0:T(8,128)}, f32[32,4096]{1,0:T(8,128)S(1)}, u32[]{:S(2)}) copy-start(f32[32,4096]{1,0:T(8,128)S(1)} %pad_maximum_fusion.refs_0_) | copy-start | bytes 1572868
  16.4 10.2 %collective-permute-start.2 = (f32[32,4096]{1,0:T(8,128)S(1)}, f32[32,4096]{1,0:T(8,128)S(1)}, u32[]{:S(2)}, u32[]{:S(2)}) collective-permute-start(f32[32,4096]{1,0:T(8,128)S(1)} %pad_maximum_fusion.refs_0_), channel_id=1, source_target_pairs={{0,14},{1,3},{2,4},{3,1},{4,2},{5,7},{6,8},{7,5},{8,6},{9,11},{10,... | collective-permute-start | bytes 1572872 | tf_op jit(solution)/shard_map/ppermute | solution.py:233
  20.9 43.8 %copy-start.2 = (f32[32,4096]{1,0:T(8,128)}, f32[32,4096]{1,0:T(8,128)S(1)}, u32[]{:S(2)}) copy-start(f32[32,4096]{1,0:T(8,128)S(1)} %pad_maximum_fusion.1.refs_1_) | copy-start | bytes 1572868
  21.0 11.4 %collective-permute-start.3 = (f32[32,4096]{1,0:T(8,128)S(1)}, f32[32,4096]{1,0:T(8,128)}, u32[]{:S(2)}, u32[]{:S(2)}) collective-permute-start(f32[32,4096]{1,0:T(8,128)S(1)} %pad_maximum_fusion.1.refs_1_), channel_id=1, source_target_pairs={{0,14},{1,3},{2,4},{3,1},{4,2},{5,7},{6,8},{7,5},{8,6},{9,11},{10,... | collective-permute-start | bytes 1572872 | tf_op jit(solution)/shard_map/ppermute | solution.py:233
  26.6 38.2 %copy-start.3 = (f32[32,4096]{1,0:T(8,128)}, f32[32,4096]{1,0:T(8,128)S(1)}, u32[]{:S(2)}) copy-start(f32[32,4096]{1,0:T(8,128)S(1)} %collective-permute-done.2.refs_2_) | copy-start | bytes 1572868
  26.6 18.0 %collective-permute-start.4 = (f32[32,4096]{1,0:T(8,128)S(1)}, f32[32,4096]{1,0:T(8,128)S(1)}, u32[]{:S(2)}, u32[]{:S(2)}) collective-permute-start(f32[32,4096]{1,0:T(8,128)S(1)} %collective-permute-done.2.refs_2_), channel_id=1, source_target_pairs={{0,2},{1,15},{2,0},{3,5},{4,6},{5,3},{6,4},{7,9},{8,10},{9,7},{10,... | collective-permute-start | bytes 1572872 | tf_op jit(solution)/shard_map/ppermute | solution.py:233
  32.3 16.0 %collective-permute-start.5 = (f32[32,4096]{1,0:T(8,128)}, f32[32,4096]{1,0:T(8,128)S(1)}, u32[]{:S(2)}, u32[]{:S(2)}) collective-permute-start(f32[32,4096]{1,0:T(8,128)} %collective-permute-done.3.refs_3_), channel_id=1, source_target_pairs={{0,2},{1,15},{2,0},{3,5},{4,6},{5,3},{6,4},{7,9},{8,10},{9,7},{10,... | collective-permute-start | bytes 1572872 | tf_op jit(solution)/shard_map/ppermute | solution.py:233
  36.9 13.4 %collective-permute-start.8 = (f32[32,4096]{1,0:T(8,128)S(1)}, f32[32,4096]{1,0:T(8,128)S(1)}, u32[]{:S(2)}, u32[]{:S(2)}) collective-permute-start(f32[32,4096]{1,0:T(8,128)S(1)} %pad_maximum_fusion.refs_0_), channel_id=1, source_target_pairs={{0,1},{1,0},{2,3},{3,2},{4,5},{5,4},{6,7},{7,6},{8,9},{9,8},{10,11... | collective-permute-start | bytes 1572872 | tf_op jit(solution)/shard_map/ppermute | solution.py:241
  40.3 14.8 %collective-permute-start.9 = (f32[32,4096]{1,0:T(8,128)S(1)}, f32[32,4096]{1,0:T(8,128)S(1)}, u32[]{:S(2)}, u32[]{:S(2)}) collective-permute-start(f32[32,4096]{1,0:T(8,128)S(1)} %pad_maximum_fusion.1.refs_1_), channel_id=1, source_target_pairs={{0,1},{1,0},{2,3},{3,2},{4,5},{5,4},{6,7},{7,6},{8,9},{9,8},{10,11... | collective-permute-start | bytes 1572872 | tf_op jit(solution)/shard_map/ppermute | solution.py:241
  42.2 14.8 %collective-permute-start.10 = (f32[32,4096]{1,0:T(8,128)S(1)}, f32[32,4096]{1,0:T(8,128)S(1)}, u32[]{:S(2)}, u32[]{:S(2)}) collective-permute-start(f32[32,4096]{1,0:T(8,128)S(1)} %collective-permute-done.2.refs_2_), channel_id=1, source_target_pairs={{0,1},{1,0},{2,3},{3,2},{4,5},{5,4},{6,7},{7,6},{8,9},{9,8},{10,11... | collective-permute-start | bytes 1572872 | tf_op jit(solution)/shard_map/ppermute | solution.py:241
  44.7 14.8 %collective-permute-start.6 = (f32[32,4096]{1,0:T(8,128)S(1)}, f32[32,4096]{1,0:T(8,128)S(1)}, u32[]{:S(2)}, u32[]{:S(2)}) collective-permute-start(f32[32,4096]{1,0:T(8,128)S(1)} %collective-permute-done.4.refs_4_), channel_id=1, source_target_pairs={{0,14},{1,3},{2,4},{3,1},{4,2},{5,7},{6,8},{7,5},{8,6},{9,11},{10,... | collective-permute-start | bytes 1572872 | tf_op jit(solution)/shard_map/ppermute | solution.py:233
  48.3 13.1 %collective-permute-start.7 = (f32[32,4096]{1,0:T(8,128)S(1)}, f32[32,4096]{1,0:T(8,128)S(1)}, u32[]{:S(2)}, u32[]{:S(2)}) collective-permute-start(f32[32,4096]{1,0:T(8,128)S(1)} %collective-permute-done.5.refs_5_), channel_id=1, source_target_pairs={{0,14},{1,3},{2,4},{3,1},{4,2},{5,7},{6,8},{7,5},{8,6},{9,11},{10,... | collective-permute-start | bytes 1572872 | tf_op jit(solution)/shard_map/ppermute | solution.py:233
  50.3 14.5 %copy-start.4 = (f32[32,4096]{1,0:T(8,128)}, f32[32,4096]{1,0:T(8,128)S(1)}, u32[]{:S(2)}) copy-start(f32[32,4096]{1,0:T(8,128)S(1)} %collective-permute-done.8.refs_8_) | copy-start | bytes 1572868
  50.3 14.6 %collective-permute-start.11 = (f32[32,4096]{1,0:T(8,128)}, f32[32,4096]{1,0:T(8,128)}, u32[]{:S(2)}, u32[]{:S(2)}) collective-permute-start(f32[32,4096]{1,0:T(8,128)} %collective-permute-done.3.refs_3_), channel_id=1, source_target_pairs={{0,1},{1,0},{2,3},{3,2},{4,5},{5,4},{6,7},{7,6},{8,9},{9,8},{10,11... | collective-permute-start | bytes 1572872 | tf_op jit(solution)/shard_map/ppermute | solution.py:241
  55.1 9.7 %copy-start.5 = (f32[32,4096]{1,0:T(8,128)}, f32[32,4096]{1,0:T(8,128)S(1)}, u32[]{:S(2)}) copy-start(f32[32,4096]{1,0:T(8,128)S(1)} %collective-permute-done.9.refs_9_) | copy-start | bytes 1572868
  55.1 9.7 %collective-permute-start.12 = (f32[32,4096]{1,0:T(8,128)S(1)}, f32[32,4096]{1,0:T(8,128)S(1)}, u32[]{:S(2)}, u32[]{:S(2)}) collective-permute-start(f32[32,4096]{1,0:T(8,128)S(1)} %collective-permute-done.4.refs_4_), channel_id=1, source_target_pairs={{0,1},{1,0},{2,3},{3,2},{4,5},{5,4},{6,7},{7,6},{8,9},{9,8},{10,11... | collective-permute-start | bytes 1572872 | tf_op jit(solution)/shard_map/ppermute | solution.py:241
  57.0 7.8 %copy-start.6 = (f32[32,4096]{1,0:T(8,128)}, f32[32,4096]{1,0:T(8,128)S(1)}, u32[]{:S(2)}) copy-start(f32[32,4096]{1,0:T(8,128)S(1)} %collective-permute-done.10.refs_10_) | copy-start | bytes 1572868
  57.1 7.8 %collective-permute-start.13 = (f32[32,4096]{1,0:T(8,128)S(1)}, f32[32,4096]{1,0:T(8,128)S(1)}, u32[]{:S(2)}, u32[]{:S(2)}) collective-permute-start(f32[32,4096]{1,0:T(8,128)S(1)} %collective-permute-done.5.refs_5_), channel_id=1, source_target_pairs={{0,1},{1,0},{2,3},{3,2},{4,5},{5,4},{6,7},{7,6},{8,9},{9,8},{10,11... | collective-permute-start | bytes 1572872 | tf_op jit(solution)/shard_map/ppermute | solution.py:241
  59.5 5.4 %collective-permute-start.14 = (f32[32,4096]{1,0:T(8,128)S(1)}, f32[32,4096]{1,0:T(8,128)}, u32[]{:S(2)}, u32[]{:S(2)}) collective-permute-start(f32[32,4096]{1,0:T(8,128)S(1)} %collective-permute-done.6.refs_6_), channel_id=1, source_target_pairs={{0,1},{1,0},{2,3},{3,2},{4,5},{5,4},{6,7},{7,6},{8,9},{9,8},{10,11... | collective-permute-start | bytes 1572872 | tf_op jit(solution)/shard_map/ppermute | solution.py:241
  61.4 5.0 %collective-permute-start.15 = (f32[32,4096]{1,0:T(8,128)S(1)}, f32[32,4096]{1,0:T(8,128)}, u32[]{:S(2)}, u32[]{:S(2)}) collective-permute-start(f32[32,4096]{1,0:T(8,128)S(1)} %collective-permute-done.7.refs_7_), channel_id=1, source_target_pairs={{0,1},{1,0},{2,3},{3,2},{4,5},{5,4},{6,7},{7,6},{8,9},{9,8},{10,11... | collective-permute-start | bytes 1572872 | tf_op jit(solution)/shard_map/ppermute | solution.py:241
  75.0 62.6 %copy-start = (f32[4096,128]{1,0:T(8,128)S(1)}, f32[4096,128]{1,0:T(8,128)}, u32[]{:S(2)}) copy-start(f32[4096,128]{1,0:T(8,128)} %c_hbm.1) | copy-start | bytes 6291460
  129.5 8.1 %collective-permute-start.16 = (f32[640,128]{1,0:T(8,128)S(1)}, f32[640,128]{1,0:T(8,128)S(1)}, u32[]{:S(2)}, u32[]{:S(2)}) collective-permute-start(f32[640,128]{1,0:T(8,128)S(1)} %invert.1.here), channel_id=1, source_target_pairs={{0,1},{1,0},{2,3},{3,2},{4,5},{5,4},{6,7},{7,6},{8,9},{9,8},{10,11... | collective-permute-start | bytes 983048 | tf_op jit(solution)/shard_map/ppermute | solution.py:241
